TPU v7x, 32 devices: a whole 2x2x4 slice. The times are simulated.
32 devices in a mesh: rep: 4 (over x, core), fsdp: 8 (over z, y).
Axes of the slice: x: 2, y: 2, z: 4, core: 2. Of those that a mesh axis runs over, the one named last changes fastest.
Arguments:
- inputs: bfloat16 [24576, 1024], P(('rep', 'fsdp')), may hold values from -6 to 6
- noise_times: float32 [192], P(('rep', 'fsdp')), may hold values from 1 to 300
- cotangent: bfloat16 [24576, 1024], P(('rep', 'fsdp')), may hold values from -6 to 6
- norm1_gain: bfloat16 [1024], P('fsdp'), may hold values from 0.5 to 1.5
- norm1_bias: bfloat16 [1024], P('fsdp'), may hold values from -4 to 4
- norm1_time: bfloat16 [256, 2048], P('fsdp'), may hold values from -0.1875 to 0.1875
- project_weight: bfloat16 [1024, 3072], P('fsdp'), may hold values from -0.1875 to 0.1875
- project_bias: bfloat16 [3072], P('fsdp'), may hold values from -4 to 4
- output_weight: bfloat16 [1024, 1024], P('fsdp'), may hold values from -0.75 to 0.75
- output_bias: bfloat16 [1024], P('fsdp'), may hold values from -4 to 4
- norm2_gain: bfloat16 [1024], P('fsdp'), may hold values from 0.5 to 1.5
- norm2_bias: bfloat16 [1024], P('fsdp'), may hold values from -4 to 4
- norm2_time: bfloat16 [256, 2048], P('fsdp'), may hold values from -0.1875 to 0.1875
- up_weight: bfloat16 [1024, 4096], P('fsdp'), may hold values from -0.1875 to 0.1875
- up_bias: bfloat16 [4096], P('fsdp'), may hold values from -4 to 4
- down_weight: bfloat16 [4096, 1024], P('fsdp'), may hold values from -0.09375 to 0.09375
- down_bias: bfloat16 [1024], P('fsdp'), may hold values from -4 to 4
Outputs:
- layer_out: bfloat16 [24576, 1024], P(('rep', 'fsdp'))
- input_grad: float32 [24576, 1024], P(('rep', 'fsdp'))
- grad_norm1_gain: float32 [1024], P('fsdp')
- grad_norm1_bias: float32 [1024], P('fsdp')
- grad_norm1_time: float32 [256, 2048], P('fsdp')
- grad_project_weight: float32 [1024, 3072], P('fsdp')
- grad_project_bias: float32 [3072], P('fsdp')
- grad_output_weight: float32 [1024, 1024], P('fsdp')
- grad_output_bias: float32 [1024], P('fsdp')
- grad_norm2_gain: float32 [1024], P('fsdp')
- grad_norm2_bias: float32 [1024], P('fsdp')
- grad_norm2_time: float32 [256, 2048], P('fsdp')
- grad_up_weight: float32 [1024, 4096], P('fsdp')
- grad_up_bias: float32 [4096], P('fsdp')
- grad_down_weight: float32 [4096, 1024], P('fsdp')
- grad_down_bias: float32 [1024], P('fsdp')
All inputs are finite; a program needn't handle non-finite values.
Results may differ from a plain program's by a relative error of at most 0.017.
Values may be sent and summed in bfloat16 or wider, within the bound.
A program may use at most 192 MiB of HBM per device.

v0:
```python
import math

import jax
import jax.numpy as jnp
from jax import lax
from jax.sharding import PartitionSpec as P

HEADS = 16
TE = 256


epsilon = 1e-05
highest = lax.Precision.HIGHEST
low_type = jnp.bfloat16
wide_type = jnp.float32


def features(noise_times, feat_width):
    half_width = feat_width // 2
    rates = jnp.exp(jnp.arange(half_width, dtype=jnp.float32) * (math.log(100.0) / half_width))
    phases = (jnp.log(noise_times) * 0.25)[:, None] * rates[None, :]
    return jnp.concatenate([jnp.sin(phases), jnp.cos(phases)], axis=1)


def rotary_tables(length, head_dim):
    half_width = head_dim // 2
    inverse = jnp.exp(jnp.arange(half_width, dtype=jnp.float32) * (-math.log(10000.0) / half_width))
    angles = jnp.arange(length, dtype=jnp.float32)[:, None] * inverse[None, :]
    return (jnp.cos(angles), jnp.sin(angles))


def rotate(values_in, cosine, sine_table):
    half_width = values_in.shape[-1] // 2
    first = values_in[..., :half_width]
    second = values_in[..., half_width:]
    cosine = cosine[None, :, None, :]
    sine_table = sine_table[None, :, None, :]
    return jnp.concatenate(
        [first * cosine - second * sine_table, second * cosine + first * sine_table], axis=-1
    )


def unrotate(grads_in, cosine, sine_table):
    half_width = grads_in.shape[-1] // 2
    first = grads_in[..., :half_width]
    second = grads_in[..., half_width:]
    cosine = cosine[None, :, None, :]
    sine_table = sine_table[None, :, None, :]
    return jnp.concatenate(
        [first * cosine + second * sine_table, second * cosine - first * sine_table], axis=-1
    )


def gelu_exact(values_in):
    return jax.nn.gelu(values_in, approximate=False)


def norm_forward(values_in, gain, bias, time_weight, time_feat, sequences):
    model_width = values_in.shape[1]
    modulation = jnp.dot(time_feat, time_weight, preferred_element_type=wide_type)
    scale = gain.astype(wide_type)[None, :] + modulation[:, :model_width]
    shift = bias.astype(wide_type)[None, :] + modulation[:, model_width:]
    blocks = values_in.reshape(sequences, -1, model_width)
    centred = blocks - jnp.mean(blocks, axis=-1, keepdims=True)
    inverse = lax.rsqrt(jnp.mean(centred * centred, axis=-1, keepdims=True) + epsilon)
    normed = centred * inverse
    result = (
        (normed * scale[:, None, :] + shift[:, None, :]).reshape(values_in.shape).astype(low_type)
    )
    return (result, (normed, inverse, scale))


def norm_backward(grads_in, kept_norm, time_feat):
    normed, inverse, scale = kept_norm
    shaped = grads_in.reshape(normed.shape)
    grad_scale = jnp.sum(shaped * normed, axis=1)
    grad_shift = jnp.sum(shaped, axis=1)
    grad_time = jnp.dot(
        time_feat.astype(wide_type).T,
        jnp.concatenate([grad_scale, grad_shift], axis=1),
        precision=highest,
    )
    grad_hat = shaped * scale[:, None, :]
    grad_values = inverse * (
        grad_hat
        - jnp.mean(grad_hat, axis=-1, keepdims=True)
        - normed * jnp.mean(grad_hat * normed, axis=-1, keepdims=True)
    )
    return (
        grad_values.reshape(grads_in.shape),
        jnp.sum(grad_scale, axis=0),
        jnp.sum(grad_shift, axis=0),
        grad_time,
    )


def attend_forward(
    normed1, project_weight, project_bias, output_weight, output_bias, cosine, sine_table, sequences
):
    token_count, model_width = normed1.shape
    head_dim = model_width // HEADS
    factor = 1.0 / math.sqrt(head_dim)
    joined = jnp.dot(
        normed1, project_weight, preferred_element_type=wide_type
    ) + project_bias.astype(wide_type)
    pieces = joined.reshape(sequences, -1, 3, HEADS, head_dim)
    queries = (rotate(pieces[:, :, 0], cosine, sine_table) * factor).astype(low_type)
    keys_low = rotate(pieces[:, :, 1], cosine, sine_table).astype(low_type)
    values_low = pieces[:, :, 2].astype(low_type)
    scores = jnp.einsum("slhe,smhe->shlm", queries, keys_low, preferred_element_type=wide_type)
    peak_score = jnp.max(scores, axis=-1, keepdims=True)
    unnormed = jnp.exp(scores - peak_score)
    totals = jnp.sum(unnormed, axis=-1, keepdims=True)
    probs_low = (unnormed / totals).astype(low_type)
    log_total = peak_score + jnp.log(totals)
    context = jnp.einsum("shlm,smhe->slhe", probs_low, values_low, preferred_element_type=wide_type)
    context = context.reshape(token_count, model_width).astype(low_type)
    branch = jnp.dot(context, output_weight, preferred_element_type=wide_type) + output_bias.astype(
        wide_type
    )
    return (branch, (queries, keys_low, values_low, log_total, context))


def attend_backward(
    grad_middle, kept_attn, project_weight, output_weight, normed1, cosine, sine_table
):
    queries, keys_low, values_low, log_total, context = kept_attn
    head_dim = queries.shape[3]
    token_count, model_width = context.shape
    factor = 1.0 / math.sqrt(head_dim)
    grad_branch = grad_middle.astype(low_type)
    grad_out_bias = jnp.sum(grad_branch.astype(wide_type), axis=0)
    grad_out_weight = jnp.einsum(
        "nd,ne->de", context, grad_branch, preferred_element_type=wide_type
    )
    grad_context = jnp.einsum(
        "ne,de->nd", grad_branch, output_weight, preferred_element_type=wide_type
    )
    grad_context = grad_context.astype(low_type).reshape(queries.shape)
    scores = jnp.einsum("slhe,smhe->shlm", queries, keys_low, preferred_element_type=wide_type)
    probs = jnp.exp(scores - log_total)
    probs_low = probs.astype(low_type)
    grad_values = jnp.einsum(
        "shlm,slhe->smhe", probs_low, grad_context, preferred_element_type=wide_type
    )
    grad_probs = jnp.einsum(
        "slhe,smhe->shlm", grad_context, values_low, preferred_element_type=wide_type
    )
    grad_scores = probs * (grad_probs - jnp.sum(grad_probs * probs, axis=-1, keepdims=True))
    grad_scores = grad_scores.astype(low_type)
    grad_queries = (
        jnp.einsum("shlm,smhe->slhe", grad_scores, keys_low, preferred_element_type=wide_type)
        * factor
    )
    grad_keys = jnp.einsum(
        "shlm,slhe->smhe", grad_scores, queries, preferred_element_type=wide_type
    )
    grad_joined = jnp.stack(
        [
            unrotate(grad_queries, cosine, sine_table),
            unrotate(grad_keys, cosine, sine_table),
            grad_values,
        ],
        axis=2,
    )
    grad_joined = grad_joined.reshape(token_count, 3 * model_width).astype(low_type)
    grad_proj_bias = jnp.sum(grad_joined.astype(wide_type), axis=0)
    grad_proj_weight = jnp.einsum(
        "nd,nf->df", normed1, grad_joined, preferred_element_type=wide_type
    )
    grad_normed = jnp.einsum(
        "nf,df->nd", grad_joined, project_weight, preferred_element_type=wide_type
    )
    return (grad_normed, grad_proj_weight, grad_proj_bias, grad_out_weight, grad_out_bias)


def shards(
    inputs,
    noise_times,
    cotangent,
    norm1_gain,
    norm1_bias,
    norm1_time,
    project_weight,
    project_bias,
    output_weight,
    output_bias,
    norm2_gain,
    norm2_bias,
    norm2_time,
    up_weight,
    up_bias,
    down_weight,
    down_bias,
):
    sequences = noise_times.shape[0]
    model_width = inputs.shape[1]
    time_feat = features(noise_times, TE).astype(low_type)
    cosine, sine_table = rotary_tables(inputs.shape[0] // sequences, model_width // HEADS)
    tokens_wide = inputs.astype(wide_type)
    attn_set = (
        lax.all_gather(norm1_gain, "fsdp", axis=0, tiled=True),
        lax.all_gather(norm1_bias, "fsdp", axis=0, tiled=True),
        lax.all_gather(norm1_time, "fsdp", axis=0, tiled=True),
        lax.all_gather(project_weight, "fsdp", axis=0, tiled=True),
        lax.all_gather(project_bias, "fsdp", axis=0, tiled=True),
        lax.all_gather(output_weight, "fsdp", axis=0, tiled=True),
        lax.all_gather(output_bias, "fsdp", axis=0, tiled=True),
    )
    normed1, kept_norm1 = norm_forward(
        tokens_wide, attn_set[0], attn_set[1], attn_set[2], time_feat, sequences
    )
    branch, kept_attn = attend_forward(
        normed1, attn_set[3], attn_set[4], attn_set[5], attn_set[6], cosine, sine_table, sequences
    )
    middle = tokens_wide + branch
    mlp_set = (
        lax.all_gather(norm2_gain, "fsdp", axis=0, tiled=True),
        lax.all_gather(norm2_bias, "fsdp", axis=0, tiled=True),
        lax.all_gather(norm2_time, "fsdp", axis=0, tiled=True),
        lax.all_gather(up_weight, "fsdp", axis=0, tiled=True),
        lax.all_gather(up_bias, "fsdp", axis=0, tiled=True),
        lax.all_gather(down_weight, "fsdp", axis=0, tiled=True),
        lax.all_gather(down_bias, "fsdp", axis=0, tiled=True),
    )
    normed2, kept_norm2 = norm_forward(
        middle, mlp_set[0], mlp_set[1], mlp_set[2], time_feat, sequences
    )
    up_proj = jnp.dot(normed2, mlp_set[3], preferred_element_type=wide_type) + mlp_set[4].astype(
        wide_type
    )
    activ = gelu_exact(up_proj).astype(low_type)
    result = (
        middle
        + jnp.dot(activ, mlp_set[5], preferred_element_type=wide_type)
        + mlp_set[6].astype(wide_type)
    )
    layer_out = result.astype(low_type)
    mlp_back = (
        lax.all_gather(norm2_gain, "fsdp", axis=0, tiled=True),
        lax.all_gather(norm2_bias, "fsdp", axis=0, tiled=True),
        lax.all_gather(norm2_time, "fsdp", axis=0, tiled=True),
        lax.all_gather(up_weight, "fsdp", axis=0, tiled=True),
        lax.all_gather(up_bias, "fsdp", axis=0, tiled=True),
        lax.all_gather(down_weight, "fsdp", axis=0, tiled=True),
        lax.all_gather(down_bias, "fsdp", axis=0, tiled=True),
    )
    grad_down_bias = jnp.sum(cotangent.astype(wide_type), axis=0)
    grad_down_weight = jnp.einsum("nf,nd->fd", activ, cotangent, preferred_element_type=wide_type)
    grad_activ = jnp.einsum("nd,fd->nf", cotangent, mlp_back[5], preferred_element_type=wide_type)
    unused, gelu_pull = jax.vjp(gelu_exact, up_proj)
    grad_up = gelu_pull(grad_activ)[0].astype(low_type)
    grad_up_bias = jnp.sum(grad_up.astype(wide_type), axis=0)
    grad_up_weight = jnp.einsum("nd,nf->df", normed2, grad_up, preferred_element_type=wide_type)
    grad_normed2 = jnp.einsum("nf,df->nd", grad_up, mlp_back[3], preferred_element_type=wide_type)
    grad_from2, grad_gain2, grad_bias2, grad_time2 = norm_backward(
        grad_normed2, kept_norm2, time_feat
    )
    grad_middle = cotangent.astype(wide_type) + grad_from2
    mlp_part = (
        lax.psum_scatter(grad_gain2, "fsdp", scatter_dimension=0, tiled=True),
        lax.psum_scatter(grad_bias2, "fsdp", scatter_dimension=0, tiled=True),
        lax.psum_scatter(grad_time2, "fsdp", scatter_dimension=0, tiled=True),
        lax.psum_scatter(grad_up_weight, "fsdp", scatter_dimension=0, tiled=True),
        lax.psum_scatter(grad_up_bias, "fsdp", scatter_dimension=0, tiled=True),
        lax.psum_scatter(grad_down_weight, "fsdp", scatter_dimension=0, tiled=True),
        lax.psum_scatter(grad_down_bias, "fsdp", scatter_dimension=0, tiled=True),
    )
    attn_back = (
        lax.all_gather(norm1_gain, "fsdp", axis=0, tiled=True),
        lax.all_gather(norm1_bias, "fsdp", axis=0, tiled=True),
        lax.all_gather(norm1_time, "fsdp", axis=0, tiled=True),
        lax.all_gather(project_weight, "fsdp", axis=0, tiled=True),
        lax.all_gather(project_bias, "fsdp", axis=0, tiled=True),
        lax.all_gather(output_weight, "fsdp", axis=0, tiled=True),
        lax.all_gather(output_bias, "fsdp", axis=0, tiled=True),
    )
    grad_normed1, grad_proj_weight, grad_proj_bias, grad_out_weight, grad_out_bias = (
        attend_backward(
            grad_middle, kept_attn, attn_back[3], attn_back[5], normed1, cosine, sine_table
        )
    )
    grad_from1, grad_gain1, grad_bias1, grad_time1 = norm_backward(
        grad_normed1, kept_norm1, time_feat
    )
    input_grad = grad_middle + grad_from1
    attn_part = (
        lax.psum_scatter(grad_gain1, "fsdp", scatter_dimension=0, tiled=True),
        lax.psum_scatter(grad_bias1, "fsdp", scatter_dimension=0, tiled=True),
        lax.psum_scatter(grad_time1, "fsdp", scatter_dimension=0, tiled=True),
        lax.psum_scatter(grad_proj_weight, "fsdp", scatter_dimension=0, tiled=True),
        lax.psum_scatter(grad_proj_bias, "fsdp", scatter_dimension=0, tiled=True),
        lax.psum_scatter(grad_out_weight, "fsdp", scatter_dimension=0, tiled=True),
        lax.psum_scatter(grad_out_bias, "fsdp", scatter_dimension=0, tiled=True),
    )
    gradients = (
        lax.psum(attn_part[0].astype(jnp.bfloat16), "rep").astype(jnp.float32),
        lax.psum(attn_part[1].astype(jnp.bfloat16), "rep").astype(jnp.float32),
        lax.psum(attn_part[2].astype(jnp.bfloat16), "rep").astype(jnp.float32),
        lax.psum(attn_part[3].astype(jnp.bfloat16), "rep").astype(jnp.float32),
        lax.psum(attn_part[4].astype(jnp.bfloat16), "rep").astype(jnp.float32),
        lax.psum(attn_part[5].astype(jnp.bfloat16), "rep").astype(jnp.float32),
        lax.psum(attn_part[6].astype(jnp.bfloat16), "rep").astype(jnp.float32),
        lax.psum(mlp_part[0].astype(jnp.bfloat16), "rep").astype(jnp.float32),
        lax.psum(mlp_part[1].astype(jnp.bfloat16), "rep").astype(jnp.float32),
        lax.psum(mlp_part[2].astype(jnp.bfloat16), "rep").astype(jnp.float32),
        lax.psum(mlp_part[3].astype(jnp.bfloat16), "rep").astype(jnp.float32),
        lax.psum(mlp_part[4].astype(jnp.bfloat16), "rep").astype(jnp.float32),
        lax.psum(mlp_part[5].astype(jnp.bfloat16), "rep").astype(jnp.float32),
        lax.psum(mlp_part[6].astype(jnp.bfloat16), "rep").astype(jnp.float32),
    )
    return (
        layer_out,
        input_grad,
        gradients[0],
        gradients[1],
        gradients[2],
        gradients[3],
        gradients[4],
        gradients[5],
        gradients[6],
        gradients[7],
        gradients[8],
        gradients[9],
        gradients[10],
        gradients[11],
        gradients[12],
        gradients[13],
    )


def solution(mesh):
    placed = (
        P(("rep", "fsdp"), None),
        P(("rep", "fsdp")),
        P(("rep", "fsdp"), None),
        P("fsdp"),
        P("fsdp"),
        P("fsdp", None),
        P("fsdp", None),
        P("fsdp"),
        P("fsdp", None),
        P("fsdp"),
        P("fsdp"),
        P("fsdp"),
        P("fsdp", None),
        P("fsdp", None),
        P("fsdp"),
        P("fsdp", None),
        P("fsdp"),
    )
    return jax.shard_map(
        shards,
        mesh=mesh,
        in_specs=placed,
        out_specs=(
            P(("rep", "fsdp"), None),
            P(("rep", "fsdp"), None),
            P("fsdp"),
            P("fsdp"),
            P("fsdp", None),
            P("fsdp", None),
            P("fsdp"),
            P("fsdp", None),
            P("fsdp"),
            P("fsdp"),
            P("fsdp"),
            P("fsdp", None),
            P("fsdp", None),
            P("fsdp"),
            P("fsdp", None),
            P("fsdp"),
        ),
        check_vma=False,
    )
```

profile of v0, /device:TPU:0, one launch (start us, length us, event | category | flops | bytes accessed | tf_op | source)
XLA Modules:
  0.0 1660.7 jit_solution(12494626400939016348)
XLA Ops:
  11.3 22.2 %all-gather = bf16[8,1,128]{2,1,0:T(2,128)(2,1)S(1)} all-gather(bf16[1,1,128]{2,1,0:T(2,128)(2,1)S(1)} %bitcast.146), channel_id=1, replica_groups=mesh['rep'=4,'fsdp'=8] {'fsdp'}, dimensions={0}, use_global_device_ids=true | all-gather | bytes 2304 | tf_op jit(solution)/shard_map/all_gather | solution.py:202
  33.5 16.3 all-gather.1
  49.8 18.1 %all-gather.3 = bf16[8,1,128]{2,1,0:T(2,128)(2,1)S(1)} all-gather(bf16[1,1,128]{2,1,0:T(2,128)(2,1)S(1)} %bitcast.148), channel_id=1, replica_groups=mesh['rep'=4,'fsdp'=8] {'fsdp'}, dimensions={0}, use_global_device_ids=true | all-gather | bytes 2304 | tf_op jit(solution)/shard_map/all_gather | solution.py:208
  67.9 16.3 all-gather.4
  84.2 18.1 %all-gather.5 = bf16[8,1,128]{2,1,0:T(2,128)(2,1)S(1)} all-gather(bf16[1,1,128]{2,1,0:T(2,128)(2,1)S(1)} %bitcast.150), channel_id=1, replica_groups=mesh['rep'=4,'fsdp'=8] {'fsdp'}, dimensions={0}, use_global_device_ids=true | all-gather | bytes 2304 | tf_op jit(solution)/shard_map/all_gather | solution.py:219
  102.2 26.6 %all-gather.2 = bf16[8,1,384]{2,1,0:T(2,128)(2,1)S(1)} all-gather(bf16[1,1,384]{2,1,0:T(2,128)(2,1)S(1)} %reshape.260), channel_id=1, replica_groups=mesh['rep'=4,'fsdp'=8] {'fsdp'}, dimensions={0}, use_global_device_ids=true | all-gather | bytes 6912 | tf_op jit(solution)/shard_map/all_gather | solution.py:206
  128.9 26.5 %all-gather.6 = bf16[8,1,512]{2,1,0:T(2,128)(2,1)S(1)} all-gather(bf16[1,1,512]{2,1,0:T(2,128)(2,1)S(1)} %reshape.268), channel_id=1, replica_groups=mesh['rep'=4,'fsdp'=8] {'fsdp'}, dimensions={0}, use_global_device_ids=true | all-gather | bytes 9216 | tf_op jit(solution)/shard_map/all_gather | solution.py:222
  162.9 31.8 %all-gather.17.cloned.1.call-done = bf16[1024,3072]{1,0:T(8,128)(2,1)} async-done(((bf16[128,3072]{1,0:T(8,128)(2,1)}), bf16[1024,3072]{1,0:T(8,128)(2,1)}) %all-gather.17.cloned.1.call-update) | async-done | bytes 6291472 | tf_op jit(solution)/shard_map/all_gather | solution.py:205
  194.7 10.2 convolution_add_fusion
  204.9 14.3 reshape.289
  226.0 10.1 fusion.74
  240.7 6.6 copy.83
  266.3 103.4 %all-gather.23.cloned.1.call-done = bf16[1024,4096]{1,0:T(8,128)(2,1)} async-done(((bf16[128,4096]{1,0:T(8,128)(2,1)}), bf16[1024,4096]{1,0:T(8,128)(2,1)}) %all-gather.23.cloned.1.call-update) | async-done | bytes 8388624 | tf_op jit(solution)/shard_map/all_gather | solution.py:221
  369.6 12.2 fusion.77
  381.8 112.9 %all-gather.25.cloned.1.call-done = bf16[4096,1024]{1,0:T(8,128)(2,1)} async-done(((bf16[512,1024]{1,0:T(8,128)(2,1)}), bf16[4096,1024]{1,0:T(8,128)(2,1)}) %all-gather.25.cloned.1.call-update) | async-done | bytes 8388624 | tf_op jit(solution)/shard_map/all_gather | solution.py:223
  494.7 49.9 %convert_reduce_fusion = (f32[4096]{0:T(1024)S(1)}, bf16[768,4096]{1,0:T(8,128)(2,1)S(1)}, f32[768,4096]{1,0:T(8,128)}) fusion(f32[768,4096]{1,0:T(8,128)} %fusion.77, f32[4096]{0:T(1024)S(1)} %bitcast.137, bf16[768,1024]{1,0:T(8,128)(2,1)} %param.19, bf16[4096,1024]{1,0:T(8,128)(2,1)} %all-gather.25.cloned.1.call-done), kind=kOutput, calls=%fused_computation.2 | convolution fusion | flops 6678376448 | bytes 41451520 | tf_op jit(solution)/shard_map/nd,fd->nf/dot_general | solution.py:250
  544.6 7.4 multiply_reduce_fusion.2
  594.7 8.6 fusion.39
  611.2 11.8 copy.71
  623.0 8.3 fusion.10
  631.4 9.6 multiply_convert_fusion
  643.6 10.3 fusion.79
  655.4 13.1 fusion.78
  671.7 17.5 %all-gather.7 = bf16[8,1,128]{2,1,0:T(2,128)(2,1)S(1)} all-gather(bf16[1,1,128]{2,1,0:T(2,128)(2,1)S(1)} %bitcast.151), channel_id=1, replica_groups=mesh['rep'=4,'fsdp'=8] {'fsdp'}, dimensions={0}, use_global_device_ids=true | all-gather | bytes 2304 | tf_op jit(solution)/shard_map/all_gather | solution.py:224
  696.2 87.4 %reduce-scatter.11.cloned.1.call-done = f32[128,1024]{1,0:T(8,128)} async-done(((f32[1024,1024]{1,0:T(8,128)}), f32[128,1024]{1,0:T(8,128)}) %reduce-scatter.11.cloned.1.call-update) | async-done | bytes 524304 | tf_op jit(solution)/shard_map/reduce_scatter | solution.py:293
  785.4 209.2 %reduce-scatter.9.cloned.1.call-done = f32[128,3072]{1,0:T(8,128)} async-done(((f32[1024,3072]{1,0:T(8,128)}), f32[128,3072]{1,0:T(8,128)}) %reduce-scatter.9.cloned.1.call-update) | async-done | bytes 1572880 | tf_op jit(solution)/shard_map/reduce_scatter | solution.py:291
  997.0 283.6 %reduce-scatter.17.cloned.1.call-done = f32[512,1024]{1,0:T(8,128)} async-done(((f32[4096,1024]{1,0:T(8,128)}), f32[512,1024]{1,0:T(8,128)}) %reduce-scatter.17.cloned.1.call-update) | async-done | bytes 2097168 | tf_op jit(solution)/shard_map/reduce_scatter | solution.py:266
  1283.3 282.5 %reduce-scatter.15.cloned.1.call-done = f32[128,4096]{1,0:T(8,128)} async-done(((f32[1024,4096]{1,0:T(8,128)}), f32[128,4096]{1,0:T(8,128)}) %reduce-scatter.15.cloned.1.call-update) | async-done | bytes 2097168 | tf_op jit(solution)/shard_map/reduce_scatter | solution.py:264
  1574.3 35.7 %all-reduce.8 = (bf16[1024]{0:T(1024)(128)(2,1)S(1)}, bf16[1024]{0:T(1024)(128)(2,1)S(1)}, bf16[3072]{0:T(1024)(128)(2,1)S(1)}, bf16[1024]{0:T(1024)(128)(2,1)S(...) all-reduce(f32[1024]{0:T(1024)S(1)} %get-tuple-element.20, ...), channel_id=2, replica_groups=mesh['rep'=4,'fsdp'=8] {'fsdp'}, use_global_device_ids=true, to_apply=%region_12.0.clone | all-reduce | flops 13312 | bytes 79872
  1610.6 6.3 all-reduce.9
  1621.1 12.1 add_convert_fusion.1
  1633.3 9.7 all-reduce.13.cloned.1.call-done
  (232 shorter events, 135.0 us)
Async XLA Ops:
  7.2 26.3 %copy-start.41 = (bf16[128]{0:T(256)(128)(2,1)S(1)}, bf16[128]{0:T(256)(128)(2,1)}, u32[]{:S(2)}) copy-start(bf16[128]{0:T(256)(128)(2,1)} %param.21) | copy-start | bytes 772
  7.2 42.6 %copy-start.42 = (bf16[128]{0:T(256)(128)(2,1)S(1)}, bf16[128]{0:T(256)(128)(2,1)}, u32[]{:S(2)}) copy-start(bf16[128]{0:T(256)(128)(2,1)} %param.26) | copy-start | bytes 772
  7.2 60.6 %copy-start.43 = (bf16[128]{0:T(256)(128)(2,1)S(1)}, bf16[128]{0:T(256)(128)(2,1)}, u32[]{:S(2)}) copy-start(bf16[128]{0:T(256)(128)(2,1)} %param.27) | copy-start | bytes 772
  7.2 76.9 %copy-start.44 = (bf16[128]{0:T(256)(128)(2,1)S(1)}, bf16[128]{0:T(256)(128)(2,1)}, u32[]{:S(2)}) copy-start(bf16[128]{0:T(256)(128)(2,1)} %param.28) | copy-start | bytes 772
  7.3 148.2 %copy-start.4 = (bf16[768,1024]{1,0:T(8,128)(2,1)S(1)}, bf16[768,1024]{1,0:T(8,128)(2,1)}, u32[]{:S(2)}) copy-start(bf16[768,1024]{1,0:T(8,128)(2,1)} %param.17) | copy-start | bytes 4718596
  7.3 148.5 %copy-start.48 = (f32[6]{0:T(128)S(1)}, f32[6]{0:T(128)}, u32[]{:S(2)}) copy-start(f32[6]{0:T(128)} %param.18) | copy-start | bytes 76
  7.3 150.5 %all-gather.15.cloned.1.call-start = ((), (), s32[]{:S(2)}) async-start(), calls=%async_computation.6 | async-start | bytes 1179648 | tf_op jit(solution)/shard_map/all_gather | solution.py:204
  8.0 152.8 %all-gather.21.cloned.1.call-start = ((), (), s32[]{:S(2)}) async-start(), calls=%async_computation.9 | async-start | bytes 1179648 | tf_op jit(solution)/shard_map/all_gather | solution.py:220
  8.8 185.9 %all-gather.17.cloned.1.call-start = ((), (), s32[]{:S(2)}) async-start(), calls=%async_computation.7 | async-start | bytes 7077888 | tf_op jit(solution)/shard_map/all_gather | solution.py:205
  9.5 249.6 %all-gather.19.cloned.1.call-start = ((), (), s32[]{:S(2)}) async-start(), calls=%async_computation.8 | async-start | bytes 2359296 | tf_op jit(solution)/shard_map/all_gather | solution.py:207
  10.1 359.5 %all-gather.23.cloned.1.call-start = ((), (), s32[]{:S(2)}) async-start(), calls=%async_computation.10 | async-start | bytes 9437184 | tf_op jit(solution)/shard_map/all_gather | solution.py:221
  10.7 484.1 %all-gather.25.cloned.1.call-start = ((), (), s32[]{:S(2)}) async-start(), calls=%async_computation.11 | async-start | bytes 9437184 | tf_op jit(solution)/shard_map/all_gather | solution.py:223
  11.2 681.8 %reduce-scatter.13.cloned.1.call-start = ((), (), s32[]{:S(2)}) async-start(), calls=%async_computation.15 | async-start | bytes 2359296 | tf_op jit(solution)/shard_map/reduce_scatter | solution.py:263
  155.9 7.0 copy-start.32
  157.8 89.5 %copy-start.28 = (f32[128,32]{0,1:T(8,128)}, f32[128,32]{0,1:T(8,128)S(1)}, u32[]{:S(2)}) copy-start(f32[128,32]{0,1:T(8,128)S(1)} %get-tuple-element.87) | copy-start | bytes 49156
  157.8 89.5 %copy-start.30 = (f32[128,32]{0,1:T(8,128)}, f32[128,32]{0,1:T(8,128)S(1)}, u32[]{:S(2)}) copy-start(f32[128,32]{0,1:T(8,128)S(1)} %get-tuple-element.88) | copy-start | bytes 49156
  160.8 44.1 %copy-start.22 = (bf16[768,1024]{1,0:T(8,128)(2,1)}, bf16[768,1024]{1,0:T(8,128)(2,1)S(1)}, u32[]{:S(2)}) copy-start(bf16[768,1024]{1,0:T(8,128)(2,1)S(1)} %fusion.18) | copy-start | bytes 4718596
  263.9 292.2 %copy-start.1 = (f32[768,1024]{1,0:T(8,128)}, f32[768,1024]{1,0:T(8,128)S(1)}, u32[]{:S(2)}) copy-start(f32[768,1024]{1,0:T(8,128)S(1)} %get-tuple-element.92) | copy-start | bytes 9437188
  494.7 49.9 %copy-start.46 = (bf16[1024,4096]{1,0:T(8,128)(2,1)S(1)}, bf16[1024,4096]{1,0:T(8,128)(2,1)}, u32[]{:S(2)}) copy-start(bf16[1024,4096]{1,0:T(8,128)(2,1)} %all-gather.23.cloned.1.call-done) | copy-start | bytes 25165828
  544.6 7.4 copy-start.18
  556.0 138.6 %reduce-scatter.7.cloned.1.call-start = ((), (), s32[]{:S(2)}) async-start(), calls=%async_computation.12 | async-start | bytes 2359296 | tf_op jit(solution)/shard_map/reduce_scatter | solution.py:290
  567.2 10.9 slice-start
  605.7 177.9 %reduce-scatter.11.cloned.1.call-start = ((), (), s32[]{:S(2)}) async-start(), calls=%async_computation.14 | async-start | bytes 4718592 | tf_op jit(solution)/shard_map/reduce_scatter | solution.py:293
  611.2 11.8 copy-start.23
  611.2 383.4 %reduce-scatter.9.cloned.1.call-start = ((), (), s32[]{:S(2)}) async-start(), calls=%async_computation.13 | async-start | bytes 14155776 | tf_op jit(solution)/shard_map/reduce_scatter | solution.py:291
  631.3 649.2 %reduce-scatter.17.cloned.1.call-start = ((), (), s32[]{:S(2)}) async-start(), calls=%async_computation.17 | async-start | bytes 18874368 | tf_op jit(solution)/shard_map/reduce_scatter | solution.py:266
  631.4 12.3 copy-start.21
  654.0 911.9 %reduce-scatter.15.cloned.1.call-start = ((), (), s32[]{:S(2)}) async-start(), calls=%async_computation.16 | async-start | bytes 18874368 | tf_op jit(solution)/shard_map/reduce_scatter | solution.py:264
  668.5 20.7 %copy-start.20 = (f32[6,128,1024]{2,1,0:T(8,128)S(1)}, f32[6,128,1024]{2,1,0:T(8,128)}, u32[]{:S(2)}) copy-start(f32[6,128,1024]{2,1,0:T(8,128)} %get-tuple-element.57) | copy-start | bytes 9437188
  668.5 974.5 %all-reduce.13.cloned.1.call-start = ((), (), s32[]{:S(2)}) async-start(), calls=%async_computation.18 | async-start | bytes 6815744 | tf_op jit(solution)/shard_map/psum | solution.py:299
  1568.6 52.6 %copy-start.2 = (f32[768,1024]{1,0:T(8,128)S(1)}, f32[768,1024]{1,0:T(8,128)}, u32[]{:S(2)}) copy-start(f32[768,1024]{1,0:T(8,128)} %copy-done.1) | copy-start | bytes 9437188
  1643.0 7.7 copy-start.25
  (35 other events, 105.2 us)
Sparse Core Ops, SparseCore 0:
  10.2 42.9 all-gather.14
  55.3 39.0 all-gather.20
  96.5 98.0 all-gather.16
  196.7 47.4 all-gather.18
  246.1 123.4 all-gather.22
  371.6 123.1 all-gather.24
  556.2 65.8 reduce-scatter.12
  626.1 66.8 reduce-scatter.6
  696.7 86.8 reduce-scatter.10
  787.5 207.0 reduce-scatter.8
  998.8 281.7 reduce-scatter.16
  1284.2 281.5 reduce-scatter.14
  1570.0 72.9 all-reduce.12
where the time goes:
time: 1670 us; the launch traced here: 1660 us
  waiting for transfers between devices  1120 us (67%)
  blocking collectives  203 us (12%)
  matrix products  168 us (10%)
  local copies, waits for them, and re-layouts  80.6 us (5%)
  other arithmetic  66.6 us (4%)
  between operations  17.2 us (1%)
    reduce_scatter x1, waiting for transfers between devices, shards(): lax.psum_scatter(grad_down_weight, 'fsdp', scatter_dimension=0, tiled=True)  284 us
    reduce_scatter x1, waiting for transfers between devices, shards(): lax.psum_scatter(grad_up_weight, 'fsdp', scatter_dimension=0, tiled=True)  283 us
    reduce_scatter x1, waiting for transfers between devices, shards(): lax.psum_scatter(grad_proj_weight, 'fsdp', scatter_dimension=0, tiled=True)  209 us
    all_gather x1, waiting for transfers between devices, shards(): lax.all_gather(down_weight, 'fsdp', axis=0, tiled=True)  113 us
    all_gather x1, waiting for transfers between devices, shards(): lax.all_gather(up_weight, 'fsdp', axis=0, tiled=True)  103 us
    reduce_scatter x1, waiting for transfers between devices, shards(): lax.psum_scatter(grad_out_weight, 'fsdp', scatter_dimension=0, tiled=True)  87.4 us
    dot_general x1, matrix products, shards(): jnp.einsum('nd,fd->nf', cotangent, mlp_back[5], preferred_element_type=wi...  49.9 us
    unnamed x1, blocking collectives  35.7 us
  transfers between devices with their start and end apart: 13, of which 8 were waited for; matrix products, arithmetic and copies ran while one was open for 14% of the time, Pallas kernels for 0%

commit v1 on v0

--- a/solution.py
+++ b/solution.py
@@ -3,6 +3,8 @@
 import jax
 import jax.numpy as jnp
 from jax import lax
+from jax.experimental import pallas as pl
+from jax.experimental.pallas import tpu as pltpu
 from jax.sharding import PartitionSpec as P
 
 HEADS = 16
@@ -174,158 +176,518 @@
     return (grad_normed, grad_proj_weight, grad_proj_bias, grad_out_weight, grad_out_bias)
 
 
+MESH = pl.DeviceIdType.MESH
+CHUNK = 1024
+FRONT = 384
+
+
+class Place:
+    def __init__(self):
+        r, f = lax.axis_index("rep"), lax.axis_index("fsdp")
+        self.r, self.f = r, f
+        self.x, self.core = r // 2, r % 2
+        self.z, self.y = f // 2, f % 2
+        z = self.z
+        self.zs = [z, z + 1 - 2 * (z % 2), (z + 2) % 4, 3 - z]
+        self.same = [zk * 2 + self.y for zk in self.zs]
+        self.other = [zk * 2 + 1 - self.y for zk in self.zs]
+        self.across_x = ((1 - self.x) * 2 + self.core, f)
+        self.across_y = (r, self.other[0])
+        self.across_core = (self.x * 2 + 1 - self.core, f)
+        self.diagonal = ((1 - self.x) * 2 + 1 - self.core, f)
+        self.along_z = [(r, fk) for fk in self.same]
+        self.group = [(r, fk) for fk in self.same[1:] + self.other]
+
+
+def greet(peers):
+    barrier = pltpu.get_barrier_semaphore()
+    for peer in peers:
+        pl.semaphore_signal(barrier, inc=1, device_id=peer, device_id_type=MESH)
+    pl.semaphore_wait(barrier, len(peers))
+
+
+def remote(src, dst, send, recv, peer):
+    return pltpu.make_async_remote_copy(
+        src_ref=src, dst_ref=dst, send_sem=send, recv_sem=recv, device_id=peer, device_id_type=MESH
+    )
+
+
+def gather_kernel(own, vec, full, vecs, send, recv, vsend, vrecv, lsem):
+    at = Place()
+    chunks, rows = own.shape[0], own.shape[1]
+    half = rows // 2
+    greet([at.across_core, at.across_x] + at.group)
+    wide = CHUNK - FRONT
+    mine = pl.ds(pl.multiple_of(at.x * FRONT, 128), wide)
+    xcols = pl.ds(pl.multiple_of(at.x * wide, 128), FRONT)
+    xland = pl.ds(pl.multiple_of((1 - at.x) * wide, 128), FRONT)
+    lo = at.core * half
+
+    def rows_of(f, core):
+        return pl.ds(pl.multiple_of(f * rows + core * half, half), half)
+
+    own_rows = pl.ds(pl.multiple_of(lo, half), half)
+    seven = at.same[1:] + at.other
+
+    def z_copy(c, k):
+        dst = full.at[c, rows_of(at.f, at.core), mine]
+        return remote(own.at[c, own_rows, mine], dst, send.at[c, k - 1], recv.at[c, k - 1], at.along_z[k])
+
+    def z_land(c, k):
+        dst = full.at[c, rows_of(at.same[k], at.core), mine]
+        return remote(dst, dst, send.at[c, k - 1], recv.at[c, k - 1], at.along_z[k])
+
+    def y_copy(c, k):
+        dst = full.at[c, rows_of(at.same[k], at.core), mine]
+        src = own.at[c, own_rows, mine] if k == 0 else dst
+        return remote(src, dst, send.at[c, 3 + k], recv.at[c, 3 + k], at.across_y)
+
+    def y_land(c, k):
+        dst = full.at[c, rows_of(at.other[k], at.core), mine]
+        return remote(dst, dst, send.at[c, 3 + k], recv.at[c, 3 + k], at.across_y)
+
+    def x_copy(c, m):
+        dst = full.at[c, rows_of(seven[m], at.core), xcols]
+        return remote(dst, dst, send.at[c, 7 + m], recv.at[c, 7 + m], at.across_x)
+
+    def x_land(c, m):
+        dst = full.at[c, rows_of(seven[m], at.core), xland]
+        return remote(dst, dst, send.at[c, 7 + m], recv.at[c, 7 + m], at.across_x)
+
+    def core_copy(c, m):
+        dst = full.at[c, rows_of(seven[m], at.core)]
+        return remote(dst, dst, send.at[c, 14 + m], recv.at[c, 14 + m], at.across_core)
+
+    def core_land(c, m):
+        dst = full.at[c, rows_of(seven[m], 1 - at.core)]
+        return remote(dst, dst, send.at[c, 14 + m], recv.at[c, 14 + m], at.across_core)
+
+    def local(c):
+        dst = full.at[c, pl.ds(pl.multiple_of(at.f * rows, rows), rows)]
+        return pltpu.make_async_copy(own.at[c], dst, lsem.at[c])
+
+    for i, peer in enumerate(at.group):
+        remote(vec, vecs.at[at.f], vsend.at[i], vrecv.at[i], peer).start()
+    vlocal = pltpu.make_async_copy(vec, vecs.at[at.f], vsend.at[7])
+    vlocal.start()
+
+    def first(c):
+        for k in range(1, 4):
+            z_copy(c, k).start()
+        y_copy(c, 0).start()
+        local(c).start()
+
+    ahead = 2
+    for c in range(ahead):
+        first(c)
+
+    def step(t, carry):
+        @pl.when(t + ahead < chunks)
+        def _():
+            first(t + ahead)
+
+        @pl.when(t < chunks)
+        def _():
+            for k in range(1, 4):
+                z_land(t, k).wait_recv()
+                y_copy(t, k).start()
+
+        @pl.when(jnp.logical_and(t >= 1, t < chunks + 1))
+        def _():
+            c = t - 1
+            for m in range(7):
+                if m >= 3:
+                    y_land(c, m - 3).wait_recv()
+                x_copy(c, m).start()
+
+        @pl.when(jnp.logical_and(t >= 2, t < chunks + 2))
+        def _():
+            c = t - 2
+            for m in range(7):
+                x_land(c, m).wait_recv()
+                core_copy(c, m).start()
+
+        @pl.when(t >= 3)
+        def _():
+            c = t - 3
+            for m in range(7):
+                core_land(c, m).wait_recv()
+            local(c).wait()
+            for k in range(1, 4):
+                z_copy(c, k).wait_send()
+            for k in range(4):
+                y_copy(c, k).wait_send()
+            for m in range(7):
+                x_copy(c, m).wait_send()
+                core_copy(c, m).wait_send()
+
+        return carry
+
+    lax.fori_loop(0, chunks + 3, step, 0)
+    for i, peer in enumerate(at.group):
+        f = seven[i]
+        remote(vec, vecs.at[f], vsend.at[i], vrecv.at[i], peer).wait()
+    vlocal.wait()
+
+
+def gather_fast(own, vec):
+    chunks, rows, _ = own.shape
+    shards_of = 8
+    any_space = pl.BlockSpec(memory_space=pl.ANY)
+    return pl.pallas_call(
+        gather_kernel,
+        out_shape=(
+            jax.ShapeDtypeStruct((chunks, shards_of * rows, CHUNK), own.dtype),
+            jax.ShapeDtypeStruct((shards_of,) + vec.shape, vec.dtype),
+        ),
+        in_specs=[any_space, any_space],
+        out_specs=(any_space, any_space),
+        scratch_shapes=[
+            pltpu.SemaphoreType.DMA((chunks, 21)),
+            pltpu.SemaphoreType.DMA((chunks, 21)),
+            pltpu.SemaphoreType.DMA((8,)),
+            pltpu.SemaphoreType.DMA((7,)),
+            pltpu.SemaphoreType.DMA((chunks,)),
+        ],
+        compiler_params=pltpu.CompilerParams(
+            collective_id=0, has_side_effects=True, vmem_limit_bytes=32 * 2**20
+        ),
+        name="gather_weights",
+    )(own, vec)
+
+
+def add_low(a, b):
+    return (a.astype(jnp.float32) + b.astype(jnp.float32)).astype(jnp.bfloat16)
+
+
+def reduce_kernel(
+    parts, vec, out, vec_out, held, l0, l1a, l1b, l2, l3, la, lv, lr, hsem, send, recv, vsend, vrecv
+):
+    at = Place()
+    chunks = parts.shape[0]
+    half = parts.shape[4]
+    quarter = half // 2
+    greet([at.across_core, at.across_x, at.diagonal] + at.group)
+    front, back = pl.ds(0, FRONT), pl.ds(FRONT, CHUNK - FRONT)
+    mine = pl.ds(pl.multiple_of(at.x * quarter, quarter), quarter)
+    theirs = pl.ds(pl.multiple_of((1 - at.x) * quarter, quarter), quarter)
+    slots = held.shape[0]
+
+    def core_copy(c):
+        return remote(parts.at[c, :, :, 1 - at.core], l0.at[c], send.at[c, 0], recv.at[c, 0], at.across_core)
+
+    def load(c):
+        return pltpu.make_async_copy(parts.at[c, :, :, at.core], held.at[c % slots], hsem.at[c % slots])
+
+    def x_one(c):
+        return remote(l0.at[c, :, :, theirs, front], l1a.at[c], send.at[c, 1], recv.at[c, 1], at.across_x)
+
+    def y_one(c):
+        return remote(l0.at[c, :, 1 - at.y, :, back], l1b.at[c], send.at[c, 2], recv.at[c, 2], at.across_y)
+
+    def y_two(c):
+        return remote(l1a.at[c, :, 1 - at.y], l2.at[c, :, :, front], send.at[c, 3], recv.at[c, 3], at.across_y)
+
+    def x_two(c):
+        return remote(l1b.at[c, :, theirs], l2.at[c, :, :, back], send.at[c, 4], recv.at[c, 4], at.across_x)
+
+    def z_copy(c, k):
+        return remote(l2.at[c, at.zs[k]], l3.at[c, k - 1], send.at[c, 4 + k], recv.at[c, 4 + k], at.along_z[k])
+
+    def x_back(c):
+        piece = la.at[c, at.core, at.x]
+        return remote(piece, piece, send.at[c, 8], recv.at[c, 8], at.across_x)
+
+    def core_back(c):
+        piece = la.at[c, at.core]
+        return remote(piece, piece, send.at[c, 9], recv.at[c, 9], at.across_core)
+
+    def v_copy(i):
+        f = (at.same[1:] + at.other)[i]
+        return remote(vec.at[f], lv.at[i], vsend.at[i], vrecv.at[i], at.group[i])
+
+    reps = [at.across_x, at.across_core, at.diagonal]
+
+    def r_copy(i):
+        return remote(lr.at[3], lr.at[i], vsend.at[7 + i], vrecv.at[7 + i], reps[i])
+
+    for i in range(7):
+        v_copy(i).start()
+    for c in range(slots):
+        load(c).start()
+
+    def begin(c, carry):
+        core_copy(c).start()
+        return carry
+
+    lax.fori_loop(0, chunks, begin, 0)
+
+    def step(t, carry):
+        @pl.when(t < chunks)
+        def _():
+            c = t
+            load(c).wait()
+            core_copy(c).wait_recv()
+
+            def add(i, carry):
+                z, y = i // 2, i % 2
+                l0[c, z, y] = add_low(l0[c, z, y], held[c % slots, z, y])
+                return carry
+
+            lax.fori_loop(0, 8, add, 0)
+            x_one(c).start()
+            y_one(c).start()
+
+            @pl.when(c + slots < chunks)
+            def _():
+                load(c + slots).start()
+
+        @pl.when(jnp.logical_and(t >= 1, t < chunks + 1))
+        def _():
+            c = t - 1
+            x_one(c).wait_recv()
+
+            def add_a(i, carry):
+                z, y = i // 2, i % 2
+                l1a[c, z, y] = add_low(l1a[c, z, y], l0[c, z, y, mine, front])
+                return carry
+
+            lax.fori_loop(0, 8, add_a, 0)
+            y_two(c).start()
+            y_one(c).wait_recv()
+
+            def add_b(z, carry):
+                l1b[c, z] = add_low(l1b[c, z], l0[c, z, at.y, :, back])
+                return carry
+
+            lax.fori_loop(0, 4, add_b, 0)
+            x_two(c).start()
+
+        @pl.when(jnp.logical_and(t >= 2, t < chunks + 2))
+        def _():
+            c = t - 2
+            y_two(c).wait_recv()
+            x_two(c).wait_recv()
+
+            def add_c(z, carry):
+                l2[c, z, :, front] = add_low(l2[c, z, :, front], l1a[c, z, at.y])
+                l2[c, z, :, back] = add_low(l2[c, z, :, back], l1b[c, z, mine])
+                return carry
+
+            lax.fori_loop(0, 4, add_c, 0)
+            for k in range(1, 4):
+                z_copy(c, k).start()
+
+        @pl.when(jnp.logical_and(t >= 3, t < chunks + 3))
+        def _():
+            c = t - 3
+            for k in range(1, 4):
+                z_copy(c, k).wait_recv()
+            total = l2[c, at.z].astype(jnp.float32)
+            for k in range(3):
+                total = total + l3[c, k].astype(jnp.float32)
+            la[c, at.core, at.x] = total.astype(jnp.bfloat16)
+            x_back(c).start()
+
+        @pl.when(jnp.logical_and(t >= 4, t < chunks + 4))
+        def _():
+            c = t - 4
+            there = la.at[c, at.core, 1 - at.x]
+            remote(there, there, send.at[c, 8], recv.at[c, 8], at.across_x).wait_recv()
+            core_back(c).start()
+
+        @pl.when(t >= 5)
+        def _():
+            c = t - 5
+            there = la.at[c, 1 - at.core]
+            remote(there, there, send.at[c, 9], recv.at[c, 9], at.across_core).wait_recv()
+            for j in range(4):
+                out[c, j * quarter : (j + 1) * quarter, :] = la[c, j // 2, j % 2].astype(jnp.float32)
+            core_copy(c).wait_send()
+            x_one(c).wait_send()
+            y_one(c).wait_send()
+            x_two(c).wait_send()
+            y_two(c).wait_send()
+            for k in range(1, 4):
+                z_copy(c, k).wait_send()
+            x_back(c).wait_send()
+            core_back(c).wait_send()
+
+        return carry
+
+    lax.fori_loop(0, chunks + 5, step, 0)
+    total = vec[at.f]
+    for i in range(7):
+        v_copy(i).wait()
+        total = total + lv[i]
+    lr[3] = total
+    for i in range(3):
+        r_copy(i).start()
+    for i in range(3):
+        r_copy(i).wait()
+        total = total + lr[i]
+    vec_out[...] = total
+
+
+def reduce_fast(parts, vec):
+    chunks, depth, _ = parts.shape
+    rows = depth // 8
+    half, quarter = rows // 2, rows // 4
+    low = jnp.bfloat16
+    wide = CHUNK - FRONT
+    shaped = parts.reshape(chunks, 4, 2, 2, half, CHUNK)
+    vmem = pl.BlockSpec(memory_space=pltpu.VMEM)
+    return pl.pallas_call(
+        reduce_kernel,
+        out_shape=(
+            jax.ShapeDtypeStruct((chunks, rows, CHUNK), jnp.float32),
+            jax.ShapeDtypeStruct(vec.shape[1:], jnp.float32),
+        ),
+        in_specs=[pl.BlockSpec(memory_space=pl.ANY), vmem],
+        out_specs=(vmem, vmem),
+        scratch_shapes=[
+            pltpu.VMEM((3, 4, 2, half, CHUNK), low),
+            pltpu.VMEM((chunks, 4, 2, half, CHUNK), low),
+            pltpu.VMEM((chunks, 4, 2, quarter, FRONT), low),
+            pltpu.VMEM((chunks, 4, half, wide), low),
+            pltpu.VMEM((chunks, 4, quarter, CHUNK), low),
+            pltpu.VMEM((chunks, 3, quarter, CHUNK), low),
+            pltpu.VMEM((chunks, 2, 2, quarter, CHUNK), low),
+            pltpu.VMEM((7,) + vec.shape[1:], jnp.float32),
+            pltpu.VMEM((4,) + vec.shape[1:], jnp.float32),
+            pltpu.SemaphoreType.DMA((3,)),
+            pltpu.SemaphoreType.DMA((chunks, 10)),
+            pltpu.SemaphoreType.DMA((chunks, 10)),
+            pltpu.SemaphoreType.DMA((10,)),
+            pltpu.SemaphoreType.DMA((10,)),
+        ],
+        compiler_params=pltpu.CompilerParams(
+            collective_id=1, has_side_effects=True, vmem_limit_bytes=56 * 2**20
+        ),
+        name="reduce_gradients",
+    )(shaped, vec)
+
+def pack_local(weights):
+    (project, output, up, down, time1, time2) = weights
+    rows, width = output.shape
+    shards_of = width // rows
+    up_blocks = up.reshape(rows, shards_of, 4, rows).transpose(2, 0, 1, 3).reshape(4, rows, width)
+    times = jnp.stack([time1, time2]).reshape(2, -1, 2, width).transpose(0, 2, 1, 3)
+    return jnp.concatenate(
+        [
+            times.reshape(1, rows, width),
+            project.reshape(rows, 3, width).transpose(1, 0, 2),
+            output[None],
+            up_blocks,
+            down.reshape(4, rows, width),
+        ]
+    )
+
+
+def pack_vectors(vectors, shards_of):
+    flat = jnp.concatenate(vectors)
+    return jnp.pad(flat.reshape(-1, 128), ((0, 3), (0, 0))) if flat.shape[0] == 13 * 128 else flat[None]
+
+
+def gather_all(own, vec, shards_of):
+    if shards_of == 8:
+        return gather_fast(own, vec)
+    full = lax.all_gather(own, "fsdp", axis=1, tiled=True)
+    return full, lax.all_gather(vec, "fsdp", axis=0)
+
+
+def reduce_all(parts, vec, shards_of):
+    if shards_of == 8:
+        return reduce_fast(parts, vec)
+    mine = lax.psum_scatter(parts, "fsdp", scatter_dimension=1, tiled=True)
+    mine = lax.psum(mine, "rep").astype(jnp.float32)
+    vec = lax.psum_scatter(vec, "fsdp", scatter_dimension=0, tiled=True)[0]
+    return mine, lax.psum(vec, "rep")
+
+
 def shards(
-    inputs,
-    noise_times,
-    cotangent,
-    norm1_gain,
-    norm1_bias,
-    norm1_time,
-    project_weight,
-    project_bias,
-    output_weight,
-    output_bias,
-    norm2_gain,
-    norm2_bias,
-    norm2_time,
-    up_weight,
-    up_bias,
-    down_weight,
-    down_bias,
+    inputs, noise_times, cotangent, norm1_gain, norm1_bias, norm1_time, project_weight, project_bias,
+    output_weight, output_bias, norm2_gain, norm2_bias, norm2_time, up_weight, up_bias, down_weight, down_bias,
 ):
     sequences = noise_times.shape[0]
-    model_width = inputs.shape[1]
+    width = inputs.shape[1]
+    rows = output_weight.shape[0]
+    shards_of = width // rows
     time_feat = features(noise_times, TE).astype(low_type)
-    cosine, sine_table = rotary_tables(inputs.shape[0] // sequences, model_width // HEADS)
+    cosine, sine_table = rotary_tables(inputs.shape[0] // sequences, width // HEADS)
     tokens_wide = inputs.astype(wide_type)
-    attn_set = (
-        lax.all_gather(norm1_gain, "fsdp", axis=0, tiled=True),
-        lax.all_gather(norm1_bias, "fsdp", axis=0, tiled=True),
-        lax.all_gather(norm1_time, "fsdp", axis=0, tiled=True),
-        lax.all_gather(project_weight, "fsdp", axis=0, tiled=True),
-        lax.all_gather(project_bias, "fsdp", axis=0, tiled=True),
-        lax.all_gather(output_weight, "fsdp", axis=0, tiled=True),
-        lax.all_gather(output_bias, "fsdp", axis=0, tiled=True),
-    )
-    normed1, kept_norm1 = norm_forward(
-        tokens_wide, attn_set[0], attn_set[1], attn_set[2], time_feat, sequences
-    )
+    own = pack_local((project_weight, output_weight, up_weight, down_weight, norm1_time, norm2_time))
+    vectors = (norm1_gain, norm1_bias, project_bias, output_bias, norm2_gain, norm2_bias, up_bias, down_bias)
+    sizes = [v.shape[0] for v in vectors]
+    vec = pack_vectors(vectors, shards_of)
+    full, vecs = gather_all(own, vec, shards_of)
+    flat = vecs.reshape(shards_of, -1)
+    at, whole = 0, []
+    for size in sizes:
+        whole.append(flat[:, at : at + size].reshape(-1))
+        at += size
+    gain1, bias1, bias_p, bias_o, gain2, bias2, bias_u, bias_d = whole
+    bias_u = bias_u.reshape(shards_of, 4, rows).transpose(1, 0, 2).reshape(-1)
+    times = full[0].reshape(shards_of, 2, 2, -1, width).transpose(1, 0, 3, 2, 4).reshape(2, TE, 2 * width)
+    project = full[1:4].transpose(1, 0, 2).reshape(width, 3 * width)
+    output = full[4]
+    up = full[5:9].transpose(1, 0, 2).reshape(width, 4 * width)
+    down = full[9:13].reshape(4 * width, width)
+    normed1, kept_norm1 = norm_forward(tokens_wide, gain1, bias1, times[0], time_feat, sequences)
     branch, kept_attn = attend_forward(
-        normed1, attn_set[3], attn_set[4], attn_set[5], attn_set[6], cosine, sine_table, sequences
+        normed1, project, bias_p, output, bias_o, cosine, sine_table, sequences
     )
     middle = tokens_wide + branch
-    mlp_set = (
-        lax.all_gather(norm2_gain, "fsdp", axis=0, tiled=True),
-        lax.all_gather(norm2_bias, "fsdp", axis=0, tiled=True),
-        lax.all_gather(norm2_time, "fsdp", axis=0, tiled=True),
-        lax.all_gather(up_weight, "fsdp", axis=0, tiled=True),
-        lax.all_gather(up_bias, "fsdp", axis=0, tiled=True),
-        lax.all_gather(down_weight, "fsdp", axis=0, tiled=True),
-        lax.all_gather(down_bias, "fsdp", axis=0, tiled=True),
-    )
-    normed2, kept_norm2 = norm_forward(
-        middle, mlp_set[0], mlp_set[1], mlp_set[2], time_feat, sequences
-    )
-    up_proj = jnp.dot(normed2, mlp_set[3], preferred_element_type=wide_type) + mlp_set[4].astype(
-        wide_type
-    )
+    normed2, kept_norm2 = norm_forward(middle, gain2, bias2, times[1], time_feat, sequences)
+    up_proj = jnp.dot(normed2, up, preferred_element_type=wide_type) + bias_u.astype(wide_type)
     activ = gelu_exact(up_proj).astype(low_type)
-    result = (
-        middle
-        + jnp.dot(activ, mlp_set[5], preferred_element_type=wide_type)
-        + mlp_set[6].astype(wide_type)
-    )
+    result = middle + jnp.dot(activ, down, preferred_element_type=wide_type) + bias_d.astype(wide_type)
     layer_out = result.astype(low_type)
-    mlp_back = (
-        lax.all_gather(norm2_gain, "fsdp", axis=0, tiled=True),
-        lax.all_gather(norm2_bias, "fsdp", axis=0, tiled=True),
-        lax.all_gather(norm2_time, "fsdp", axis=0, tiled=True),
-        lax.all_gather(up_weight, "fsdp", axis=0, tiled=True),
-        lax.all_gather(up_bias, "fsdp", axis=0, tiled=True),
-        lax.all_gather(down_weight, "fsdp", axis=0, tiled=True),
-        lax.all_gather(down_bias, "fsdp", axis=0, tiled=True),
-    )
     grad_down_bias = jnp.sum(cotangent.astype(wide_type), axis=0)
-    grad_down_weight = jnp.einsum("nf,nd->fd", activ, cotangent, preferred_element_type=wide_type)
-    grad_activ = jnp.einsum("nd,fd->nf", cotangent, mlp_back[5], preferred_element_type=wide_type)
+    grad_down = jnp.einsum("nf,nd->fd", activ, cotangent, preferred_element_type=wide_type)
+    grad_activ = jnp.einsum("nd,fd->nf", cotangent, down, preferred_element_type=wide_type)
     unused, gelu_pull = jax.vjp(gelu_exact, up_proj)
     grad_up = gelu_pull(grad_activ)[0].astype(low_type)
     grad_up_bias = jnp.sum(grad_up.astype(wide_type), axis=0)
     grad_up_weight = jnp.einsum("nd,nf->df", normed2, grad_up, preferred_element_type=wide_type)
-    grad_normed2 = jnp.einsum("nf,df->nd", grad_up, mlp_back[3], preferred_element_type=wide_type)
-    grad_from2, grad_gain2, grad_bias2, grad_time2 = norm_backward(
-        grad_normed2, kept_norm2, time_feat
-    )
+    grad_normed2 = jnp.einsum("nf,df->nd", grad_up, up, preferred_element_type=wide_type)
+    grad_from2, grad_gain2, grad_bias2, grad_time2 = norm_backward(grad_normed2, kept_norm2, time_feat)
     grad_middle = cotangent.astype(wide_type) + grad_from2
-    mlp_part = (
-        lax.psum_scatter(grad_gain2, "fsdp", scatter_dimension=0, tiled=True),
-        lax.psum_scatter(grad_bias2, "fsdp", scatter_dimension=0, tiled=True),
-        lax.psum_scatter(grad_time2, "fsdp", scatter_dimension=0, tiled=True),
-        lax.psum_scatter(grad_up_weight, "fsdp", scatter_dimension=0, tiled=True),
-        lax.psum_scatter(grad_up_bias, "fsdp", scatter_dimension=0, tiled=True),
-        lax.psum_scatter(grad_down_weight, "fsdp", scatter_dimension=0, tiled=True),
-        lax.psum_scatter(grad_down_bias, "fsdp", scatter_dimension=0, tiled=True),
-    )
-    attn_back = (
-        lax.all_gather(norm1_gain, "fsdp", axis=0, tiled=True),
-        lax.all_gather(norm1_bias, "fsdp", axis=0, tiled=True),
-        lax.all_gather(norm1_time, "fsdp", axis=0, tiled=True),
-        lax.all_gather(project_weight, "fsdp", axis=0, tiled=True),
-        lax.all_gather(project_bias, "fsdp", axis=0, tiled=True),
-        lax.all_gather(output_weight, "fsdp", axis=0, tiled=True),
-        lax.all_gather(output_bias, "fsdp", axis=0, tiled=True),
-    )
-    grad_normed1, grad_proj_weight, grad_proj_bias, grad_out_weight, grad_out_bias = (
-        attend_backward(
-            grad_middle, kept_attn, attn_back[3], attn_back[5], normed1, cosine, sine_table
-        )
-    )
-    grad_from1, grad_gain1, grad_bias1, grad_time1 = norm_backward(
-        grad_normed1, kept_norm1, time_feat
-    )
+    grad_normed1, grad_proj, grad_proj_bias, grad_out, grad_out_bias = attend_backward(
+        grad_middle, kept_attn, project, output, normed1, cosine, sine_table
+    )
+    grad_from1, grad_gain1, grad_bias1, grad_time1 = norm_backward(grad_normed1, kept_norm1, time_feat)
     input_grad = grad_middle + grad_from1
-    attn_part = (
-        lax.psum_scatter(grad_gain1, "fsdp", scatter_dimension=0, tiled=True),
-        lax.psum_scatter(grad_bias1, "fsdp", scatter_dimension=0, tiled=True),
-        lax.psum_scatter(grad_time1, "fsdp", scatter_dimension=0, tiled=True),
-        lax.psum_scatter(grad_proj_weight, "fsdp", scatter_dimension=0, tiled=True),
-        lax.psum_scatter(grad_proj_bias, "fsdp", scatter_dimension=0, tiled=True),
-        lax.psum_scatter(grad_out_weight, "fsdp", scatter_dimension=0, tiled=True),
-        lax.psum_scatter(grad_out_bias, "fsdp", scatter_dimension=0, tiled=True),
-    )
-    gradients = (
-        lax.psum(attn_part[0].astype(jnp.bfloat16), "rep").astype(jnp.float32),
-        lax.psum(attn_part[1].astype(jnp.bfloat16), "rep").astype(jnp.float32),
-        lax.psum(attn_part[2].astype(jnp.bfloat16), "rep").astype(jnp.float32),
-        lax.psum(attn_part[3].astype(jnp.bfloat16), "rep").astype(jnp.float32),
-        lax.psum(attn_part[4].astype(jnp.bfloat16), "rep").astype(jnp.float32),
-        lax.psum(attn_part[5].astype(jnp.bfloat16), "rep").astype(jnp.float32),
-        lax.psum(attn_part[6].astype(jnp.bfloat16), "rep").astype(jnp.float32),
-        lax.psum(mlp_part[0].astype(jnp.bfloat16), "rep").astype(jnp.float32),
-        lax.psum(mlp_part[1].astype(jnp.bfloat16), "rep").astype(jnp.float32),
-        lax.psum(mlp_part[2].astype(jnp.bfloat16), "rep").astype(jnp.float32),
-        lax.psum(mlp_part[3].astype(jnp.bfloat16), "rep").astype(jnp.float32),
-        lax.psum(mlp_part[4].astype(jnp.bfloat16), "rep").astype(jnp.float32),
-        lax.psum(mlp_part[5].astype(jnp.bfloat16), "rep").astype(jnp.float32),
-        lax.psum(mlp_part[6].astype(jnp.bfloat16), "rep").astype(jnp.float32),
-    )
+    grad_times = jnp.stack([grad_time1, grad_time2]).reshape(2, shards_of, -1, 2, width)
+    parts = jnp.concatenate(
+        [
+            grad_times.transpose(1, 0, 3, 2, 4).reshape(1, width, width).astype(low_type),
+            grad_proj.astype(low_type).reshape(width, 3, width).transpose(1, 0, 2),
+            grad_out.astype(low_type)[None],
+            grad_up_weight.astype(low_type).reshape(width, 4, width).transpose(1, 0, 2),
+            grad_down.astype(low_type).reshape(4, width, width),
+        ]
+    )
+    grad_up_bias = grad_up_bias.reshape(4, shards_of, rows).transpose(1, 0, 2).reshape(-1)
+    grad_vectors = (
+        grad_gain1, grad_bias1, grad_proj_bias, grad_out_bias, grad_gain2, grad_bias2, grad_up_bias, grad_down_bias
+    )
+    grad_vec = jnp.concatenate([g.reshape(shards_of, -1) for g in grad_vectors], axis=1)
+    pad = vec.size - grad_vec.shape[1]
+    grad_vec = jnp.pad(grad_vec, ((0, 0), (0, pad))).reshape((shards_of,) + vec.shape)
+    mine, mine_vec = reduce_all(parts, grad_vec, shards_of)
+    mine_vec = mine_vec.reshape(-1)
+    at, got = 0, []
+    for size in sizes:
+        got.append(mine_vec[at : at + size])
+        at += size
+    my_times = mine[0].reshape(2, 2, -1, width).transpose(0, 2, 1, 3).reshape(2, -1, 2 * width)
+    my_project = mine[1:4].transpose(1, 0, 2).reshape(rows, 3 * width)
+    my_up = mine[5:9].reshape(4, rows, shards_of, rows).transpose(1, 2, 0, 3).reshape(rows, 4 * width)
+    my_down = mine[9:13].reshape(4 * rows, width)
     return (
-        layer_out,
-        input_grad,
-        gradients[0],
-        gradients[1],
-        gradients[2],
-        gradients[3],
-        gradients[4],
-        gradients[5],
-        gradients[6],
-        gradients[7],
-        gradients[8],
-        gradients[9],
-        gradients[10],
-        gradients[11],
-        gradients[12],
-        gradients[13],
+        layer_out, input_grad, got[0], got[1], my_times[0], my_project, got[2], mine[4], got[3],
+        got[4], got[5], my_times[1], my_up, got[6], my_down, got[7],
     )
 
 

time: 1670 us -> 689 us (0.41)
  waiting for transfers between devices: 1120 us -> 0 us
  Pallas kernels: 0 us -> 283 us
  blocking collectives: 203 us -> 0 us
  local copies, waits for them, and re-layouts: 80.6 us -> 199 us
  other arithmetic: 66.6 us -> 33.8 us
    reduce_scatter x6 -> x0, waiting for transfers between devices: 863 us -> none  [the longest x1 284 us: shards(): lax.psum_scatter(grad_down_weight, 'fsdp', scatter_dimension=0, tiled=True)]
    pallas_call x0 -> x2, Pallas kernels: none -> 283 us  [the longest x1 151 us: reduce_fast(): pl.pallas_call(reduce_kernel, out_shape=(jax.ShapeDtypeStruct((chunks, ro...]
    all_gather x6 -> x0, waiting for transfers between devices: 248 us -> none  [the longest x1 113 us: shards(): lax.all_gather(down_weight, 'fsdp', axis=0, tiled=True)]
    all_gather x8 -> x0, blocking collectives: 161 us -> none  [the longest x1 26.6 us: shards(): lax.all_gather(project_bias, 'fsdp', axis=0, tiled=True)]
    transpose x0 -> x8, local copies, waits for them, and re-layouts: none -> 41.5 us  [the longest x2 15.3 us: shards(): project = full[1:4].transpose(1, 0, 2).reshape(width, 3 * width)]
    convert_element_type x28 -> x2, other arithmetic: 37.5 us -> 0.6 us  [the longest x1 0.6 us: shards(): bias_d.astype(wide_type)]
    unnamed x1 -> x0, blocking collectives: 35.7 us -> none
    unnamed x122 -> x167, local copies, waits for them, and re-layouts: 28.1 us -> 46.2 us
  transfers between devices with their start and end apart: 13 -> 0, of which waited for: 8 -> 0; matrix products, arithmetic and copies ran while one was open for 14% -> 0% of each run, Pallas kernels for 0% -> 0%
where the time goes in v1:
time: 689 us; the launch traced here: 678 us
  Pallas kernels  283 us (41%)
  local copies, waits for them, and re-layouts  199 us (29%)
  matrix products  161 us (23%)
  other arithmetic  33.8 us (5%)
    pallas_call x1, Pallas kernels, reduce_fast(): pl.pallas_call(reduce_kernel, out_shape=(jax.ShapeDtypeStruct((chunks, ro...  151 us
    pallas_call x1, Pallas kernels, gather_fast(): pl.pallas_call(gather_kernel, out_shape=(jax.ShapeDtypeStruct((chunks, sh...  132 us
    unnamed x167, local copies, waits for them, and re-layouts  46.2 us
    dot_general x1, matrix products, shards(): jnp.dot(normed2, up, preferred_element_type=wide_type)  37.6 us
    dot_general x1, matrix products, shards(): jnp.einsum('nd,fd->nf', cotangent, down, preferred_element_type=wide_type)  18.9 us
    transpose x2, local copies, waits for them, and re-layouts, shards(): project = full[1:4].transpose(1, 0, 2).reshape(width, 3 * width)  15.3 us
    convert_element_type x2, local copies, waits for them, and re-layouts, attend_backward(): grad_joined.reshape(token_count, 3 * model_width).astype(low_type)  15.3 us
    reshape x1, local copies, waits for them, and re-layouts, attend_forward(): pieces = joined.reshape(sequences, -1, 3, HEADS, head_dim)  14.3 us

profile of v1, /device:TPU:0, one launch (start us, length us, event | category | flops | bytes accessed | tf_op | source)
XLA Modules:
  0.0 678.0 jit_solution(17877536196650267111)
XLA Ops:
  17.2 131.6 %gather_weights.1 = (bf16[13,1024,1024]{2,1,0:T(8,128)(2,1)}, bf16[8,16,128]{2,1,0:T(8,128)(2,1)S(1)}) custom-call(bf16[13,128,1024]{2,1,0:T(8,128)(2,1)S(1)} %constant_dynamic-update-slice_fusion.own, bf16[16,128]{1,0:T(8,128)(2,1)S(1)} %pad.8.vec), custom_call_target="tpu_custom_call" | custom-call | tf_op jit(solution)/shard_map/gather_weights/pallas_call | solution.py:337
  157.5 6.7 slice_bitcast_fusion.1
  164.1 8.7 %copy.58 = bf16[1024,3,1024]{0,2,1:T(8,128)(2,1)} copy(bf16[1024,3,1024]{2,0,1:T(8,128)(2,1)} %slice_bitcast_fusion.1) | data formatting | bytes 12582912 | tf_op jit(solution)/shard_map/transpose | solution.py:632
  172.8 10.8 %convolution_add_fusion = f32[768,3072]{1,0:T(8,128)} fusion(bf16[768,1024]{1,0:T(8,128)(2,1)S(1)} %fusion.21, bf16[1024,3072]{0,1:T(8,128)(2,1)} %bitcast.321, f32[3072]{0:T(1024)S(1)} %reshape.453), kind=kOutput, calls=%fused_computation.40 | convolution fusion | flops 4834197504 | bytes 17313792 | tf_op jit(solution)/shard_map/dot_general | solution.py:105
  183.5 14.3 %reshape.462 = f32[6,128,3,16,64]{4,3,2,1,0:T(8,128)} reshape(f32[768,3072]{1,0:T(8,128)} %convolution_add_fusion) | data formatting | bytes 18874368 | tf_op jit(solution)/shard_map/reshape | solution.py:108
  201.1 10.0 %fusion.96 = (f32[6,128,1,16,64]{4,3,2,1,0:T(8,128)}, f32[6,128,1,16,64]{4,3,2,1,0:T(8,128)}) fusion(f32[6,128,3,16,64]{4,3,2,1,0:T(8,128)} %reshape.462), kind=kLoop, calls=%fused_computation.211 | loop fusion | bytes 12582912 | tf_op jit(solution)/shard_map/slice | solution.py:109
  214.4 4.6 copy.101
  219.0 6.5 copy.102
  235.7 5.2 fusion.101
  244.6 6.2 fusion.95
  250.8 11.4 %copy.65 = bf16[1024,4,1024]{0,2,1:T(8,128)(2,1)} copy(bf16[1024,4,1024]{2,0,1:T(8,128)(2,1)} %get-tuple-element.60) | data formatting | bytes 16777216 | tf_op jit(solution)/shard_map/transpose | solution.py:634
  262.2 37.6 %multiply_convert_fusion = (bf16[768,4096]{1,0:T(8,128)(2,1)}, f32[768,4096]{1,0:T(8,128)}, f32[768,4096]{1,0:T(8,128)}) fusion(f32[4096]{0:T(1024)S(1)} %convert_bitcast_fusion, bf16[768,1024]{1,0:T(8,128)(2,1)} %fusion.20, bf16[1024,4096]{0,1:T(8,128)(2,1)} %bitcast.311), kind=kOutput, calls=%fused_computation.12 | convolution fusion | flops 6650068992 | bytes 41435136 | tf_op jit(solution)/shard_map/dot_general | solution.py:642
  299.8 18.9 %convert_reduce_fusion = (f32[4096]{0:T(1024)S(1)}, bf16[768,4096]{1,0:T(8,128)(2,1)}) fusion(f32[768,4096]{1,0:T(8,128)} %get-tuple-element.58, bf16[4096,1024]{1,0:T(8,128)(2,1)} %bitcast.319, bf16[768,1024]{1,0:T(8,128)(2,1)S(1)} %copy-done.16, f32[768,4096]{1,0:T(8,128)} %get-tuple-element.117, f32[4096]{0:T(1024)S(1)} %convert_bitcast_fusion), kind=kOutput, calls=%fused_computation.11 | convolution fusion | flops 6495924224 | bytes 41451520 | tf_op jit(solution)/shard_map/nd,fd->nf/dot_general | solution.py:648
  318.7 12.6 %add_convert_fusion = bf16[768,1024]{1,0:T(8,128)(2,1)} fusion(f32[768,1024]{1,0:T(8,128)S(1)} %get-tuple-element.116, bf16[768,4096]{1,0:T(8,128)(2,1)} %get-tuple-element.57, bf16[4096,1024]{1,0:T(8,128)(2,1)} %bitcast.320, f32[1024]{0:T(1024)S(1)} %copy-done.53), kind=kOutput, calls=%fused_computation.67 | convolution fusion | flops 6444810240 | bytes 19402752 | tf_op jit(solution)/shard_map/dot_general | solution.py:644
  331.4 7.7 %fusion.57 = (f32[1024]{0:T(1024)S(1)}, f32[6,128]{1,0:T(8,128)S(1)}, f32[6,1024]{1,0:T(8,128)S(1)}, f32[6,128]{1,0:T(8,128)S(1)}, f32[1024]{0:T(1024)S(1)}, /*i...) fusion(f32[6,128]{1,0:T(8,128)S(1)} %copy-done.52, f32[6,128,1024]{2,1,0:T(8,128)S(1)} %bitcast.299, ...), kind=kOutput, calls=%fused_computation.116 | convolution fusion | flops 6451085312 | bytes 21065728 | tf_op jit(solution)/shard_map/nf,df->nd/dot_general | solution.py:653
  349.3 4.8 fusion.36
  357.1 5.4 reshape.463
  362.5 4.9 copy.68
  367.5 6.8 %fusion.31 = bf16[6,128,1,16,64]{1,4,3,0,2:T(8,128)(2,1)} fusion(bf16[6,128,16,64]{1,3,2,0:T(8,128)(2,1)} %copy.68, f32[6,16,128,128]{2,3,1,0:T(8,128)} %copy-done, f32[6,16,128]{2,1,0:T(8,128)S(1)} %copy-done.33), kind=kOutput, calls=%fused_computation.88 | convolution fusion | flops 204472320 | bytes 9486336 | tf_op jit(solution)/shard_map/shlm,slhe->smhe/dot_general | solution.py:145
  374.3 12.2 %convolution_convert_fusion = bf16[4096,1024]{1,0:T(8,128)(2,1)} fusion(bf16[768,4096]{1,0:T(8,128)(2,1)} %get-tuple-element.57, bf16[768,1024]{1,0:T(8,128)(2,1)S(1)} %copy-done.18), kind=kOutput, calls=%fused_computation.30 | convolution fusion | flops 6446645248 | bytes 16252928 | tf_op jit(solution)/shard_map/nf,nd->fd/dot_general | solution.py:647
  386.5 4.3 multiply_reduce_fusion
  390.9 4.9 multiply_convert_fusion.1
  407.9 8.3 %fusion.55 = (f32[1024]{0:T(1024)S(1)}, f32[6,128]{1,0:T(8,128)S(1)}, f32[6,1024]{1,0:T(8,128)S(1)}, f32[6,128]{1,0:T(8,128)S(1)}, f32[1024]{0:T(1024)S(1)}, /*i...) fusion(f32[6,128]{1,0:T(8,128)S(1)} %copy-done.50, f32[6,128]{1,0:T(8,128)S(1)} %copy-done.49, ...), kind=kOutput, calls=%fused_computation.114 | convolution fusion | flops 4841259008 | bytes 18968576 | tf_op jit(solution)/shard_map/nf,df->nd/dot_general | solution.py:173
  424.6 11.7 %copy.78 = bf16[6,128,3,16,64]{1,0,4,3,2:T(8,128)(2,1)S(1)} copy(bf16[6,128,3,16,64]{1,4,3,0,2:T(8,128)(2,1)} %get-tuple-element.55) | data formatting | bytes 9437184 | tf_op jit(solution)/shard_map/convert_element_type | solution.py:168
  436.3 7.4 %convolution_convert_fusion.2 = bf16[1024,3072]{1,0:T(8,128)(2,1)} fusion(bf16[768,1024]{1,0:T(8,128)(2,1)S(1)} %copy-done.28, bf16[384,8,6,128]{3,2,1,0:T(8,128)(2,1)S(1)} %bitcast.324), kind=kOutput, calls=%fused_computation.38 | convolution fusion | flops 4834983936 | bytes 12582912 | tf_op jit(solution)/shard_map/nd,nf->df/dot_general | solution.py:170
  443.7 8.6 %copy.79 = bf16[1024,3072]{0,1:T(8,128)(2,1)} copy(bf16[1024,3072]{1,0:T(8,128)(2,1)} %convolution_convert_fusion.2) | data formatting | bytes 12582912 | tf_op jit(solution)/shard_map/convert_element_type | solution.py:665
  452.4 8.8 %copy.80 = bf16[3,1024,1024]{2,1,0:T(8,128)(2,1)} copy(bf16[3,1024,1024]{1,2,0:T(8,128)(2,1)} %bitcast.304) | data formatting | bytes 12582912 | tf_op jit(solution)/shard_map/transpose | solution.py:665
  461.2 11.8 %convolution_convert_fusion.1 = bf16[1024,4096]{1,0:T(8,128)(2,1)} fusion(bf16[768,1024]{1,0:T(8,128)(2,1)S(1)} %copy-done.29, bf16[768,4096]{1,0:T(8,128)(2,1)} %get-tuple-element.123), kind=kOutput, calls=%fused_computation.31 | convolution fusion | flops 6446645248 | bytes 16252928 | tf_op jit(solution)/shard_map/nd,nf->df/dot_general | solution.py:652
  473.0 8.2 %copy.132 = bf16[128,4,8,1024]{3,2,0,1:T(8,128)(2,1)} copy(bf16[128,4,8,1024]{3,2,1,0:T(8,128)(2,1)} %bitcast.313) | data formatting | bytes 16777216 | tf_op jit(solution)/shard_map/reshape | solution.py:667
  489.2 8.5 %constant_dynamic-update-slice_fusion.4 = bf16[13,4,2,2,64,1024]{5,4,3,2,1,0:T(8,128)(2,1)} fusion(bf16[13,4,2,2,64,1024]{5,4,3,2,1,0:T(8,128)(2,1)} %constant_dynamic-update-slice_fusion.5, bf16[4,4,2,2,64,1024]{5,4,3,2,1,0:T(8,128)(2,1)} %bitcast.298), kind=kLoop, calls=%fused_computation.137 | loop fusion | bytes 16777216
  497.7 8.6 %constant_dynamic-update-slice_fusion.3.parts = bf16[13,4,2,2,64,1024]{5,4,3,2,1,0:T(8,128)(2,1)} fusion(bf16[13,4,2,2,64,1024]{5,4,3,2,1,0:T(8,128)(2,1)} %constant_dynamic-update-slice_fusion.4, bf16[4,4,2,2,64,1024]{5,4,3,2,1,0:T(8,128)(2,1)} %bitcast.310), kind=kLoop, calls=%fused_computation.136 | loop fusion | bytes 16777216 | tf_op jit(solution)/shard_map/concatenate | solution.py:662
  506.3 151.4 %reduce_gradients.1 = (f32[13,128,1024]{2,1,0:T(8,128)}, f32[16,128]{1,0:T(8,128)}) custom-call(bf16[13,4,2,2,64,1024]{5,4,3,2,1,0:T(8,128)(2,1)} %constant_dynamic-update-slice_fusion.3.parts, f32[8,16,128]{2,1,0:T(8,128)} %bitcast.341), custom_call_target="tpu_custom_call" | custom-call | tf_op jit(solution)/shard_map/reduce_gradients/pallas_call | solution.py:540
  (249 shorter events, 106.7 us)
Async XLA Ops:
  0.6 12.9 %copy-start.44 = (bf16[32,2048]{1,0:T(8,128)(2,1)S(1)}, bf16[32,2048]{1,0:T(8,128)(2,1)}, u32[]{:S(2)}) copy-start(bf16[32,2048]{1,0:T(8,128)(2,1)} %param.29) | copy-start | bytes 393220
  0.7 13.1 %copy-start.32 = (bf16[128,3072]{1,0:T(8,128)(2,1)S(1)}, bf16[128,3072]{1,0:T(8,128)(2,1)}, u32[]{:S(2)}) copy-start(bf16[128,3072]{1,0:T(8,128)(2,1)} %param.23) | copy-start | bytes 2359300
  0.7 12.8 %copy-start.43 = (bf16[32,2048]{1,0:T(8,128)(2,1)S(1)}, bf16[32,2048]{1,0:T(8,128)(2,1)}, u32[]{:S(2)}) copy-start(bf16[32,2048]{1,0:T(8,128)(2,1)} %param.22) | copy-start | bytes 393220
  1.6 154.1 %copy-start.45 = (bf16[6,128]{1,0:T(8,128)(2,1)}, bf16[6,128]{1,0:T(8,128)(2,1)S(1)}, u32[]{:S(2)}) copy-start(bf16[6,128]{1,0:T(8,128)(2,1)S(1)} %get-tuple-element.109) | copy-start | bytes 4612
  1.6 154.1 %copy-start.47 = (bf16[6,128]{1,0:T(8,128)(2,1)}, bf16[6,128]{1,0:T(8,128)(2,1)S(1)}, u32[]{:S(2)}) copy-start(bf16[6,128]{1,0:T(8,128)(2,1)S(1)} %get-tuple-element.110) | copy-start | bytes 4612
  13.4 212.1 %copy-start.39 = (f32[128,32]{0,1:T(8,128)}, f32[128,32]{0,1:T(8,128)S(1)}, u32[]{:S(2)}) copy-start(f32[128,32]{0,1:T(8,128)S(1)} %get-tuple-element.111) | copy-start | bytes 49156
  13.4 212.1 %copy-start.41 = (f32[128,32]{0,1:T(8,128)}, f32[128,32]{0,1:T(8,128)S(1)}, u32[]{:S(2)}) copy-start(f32[128,32]{0,1:T(8,128)S(1)} %get-tuple-element.112) | copy-start | bytes 49156
  156.0 86.5 %copy-start.36 = (f32[6,1024]{1,0:T(8,128)}, f32[6,1024]{1,0:T(8,128)S(1)}, u32[]{:S(2)}) copy-start(f32[6,1024]{1,0:T(8,128)S(1)} %get-tuple-element.81) | copy-start | bytes 73732
  157.5 15.3 %copy-start.27 = (bf16[768,1024]{1,0:T(8,128)(2,1)}, bf16[768,1024]{1,0:T(8,128)(2,1)S(1)}, u32[]{:S(2)}) copy-start(bf16[768,1024]{1,0:T(8,128)(2,1)S(1)} %fusion.21) | copy-start | bytes 4718596
  233.2 11.4 %slice-start.4 = ((s8[27262976]{0:T(1024)(128)(4,1)}), s8[2097152]{0:T(1024)(128)(4,1)S(1)}, s32[]{:S(2)}) async-start(s8[27262976]{0:T(1024)(128)(4,1)} %bitcast.305), calls=%async_computation.4 | async-start | bytes 4194304
  233.2 11.4 %slice-start.5 = ((s8[27262976]{0:T(1024)(128)(4,1)}), s8[4194304]{0:T(1024)(128)(4,1)S(1)}, s32[]{:S(2)}) async-start(s8[27262976]{0:T(1024)(128)(4,1)} %bitcast.305), calls=%async_computation.5 | async-start | bytes 8388608
  233.2 11.4 %slice-start.6 = ((s8[27262976]{0:T(1024)(128)(4,1)}), s8[4194304]{0:T(1024)(128)(4,1)S(1)}, s32[]{:S(2)}) async-start(s8[27262976]{0:T(1024)(128)(4,1)} %bitcast.305), calls=%async_computation.6 | async-start | bytes 8388608
  233.2 11.4 %slice-start.7 = ((s8[27262976]{0:T(1024)(128)(4,1)}), s8[4194304]{0:T(1024)(128)(4,1)S(1)}, s32[]{:S(2)}) async-start(s8[27262976]{0:T(1024)(128)(4,1)} %bitcast.305), calls=%async_computation.7 | async-start | bytes 8388608
  234.3 10.2 %slice-start.8 = ((s8[27262976]{0:T(1024)(128)(4,1)}), s8[4194304]{0:T(1024)(128)(4,1)S(1)}, s32[]{:S(2)}) async-start(s8[27262976]{0:T(1024)(128)(4,1)} %bitcast.305), calls=%async_computation.8 | async-start | bytes 8388608
  235.7 8.9 %slice-start.9 = ((s8[27262976]{0:T(1024)(128)(4,1)}), s8[4194304]{0:T(1024)(128)(4,1)S(1)}, s32[]{:S(2)}) async-start(s8[27262976]{0:T(1024)(128)(4,1)} %bitcast.305), calls=%async_computation.9 | async-start | bytes 8388608
  262.2 37.6 %copy-start.16 = (bf16[768,1024]{1,0:T(8,128)(2,1)S(1)}, bf16[768,1024]{1,0:T(8,128)(2,1)}, u32[]{:S(2)}) copy-start(bf16[768,1024]{1,0:T(8,128)(2,1)} %param.19) | copy-start | bytes 4718596
  299.8 18.9 %copy-start.53 = (f32[1024]{0:T(1024)S(1)}, f32[1024]{0:T(1024)}, u32[]{:S(2)}) copy-start(f32[1024]{0:T(1024)} %get-tuple-element.87) | copy-start | bytes 12292
  318.7 12.7 %copy-start.10 = (bf16[1024,4,1024]{0,2,1:T(8,128)(2,1)S(1)}, bf16[1024,4,1024]{0,2,1:T(8,128)(2,1)}, u32[]{:S(2)}) copy-start(bf16[1024,4,1024]{0,2,1:T(8,128)(2,1)} %copy.65) | copy-start | bytes 25165828
  318.7 12.7 %copy-start.37 = (f32[6,1024]{1,0:T(8,128)S(1)}, f32[6,1024]{1,0:T(8,128)}, u32[]{:S(2)}) copy-start(f32[6,1024]{1,0:T(8,128)} %copy-done.36) | copy-start | bytes 73732
  318.7 12.7 %copy-start.51 = (f32[6,128]{1,0:T(8,128)S(1)}, f32[6,128]{1,0:T(8,128)}, u32[]{:S(2)}) copy-start(f32[6,128]{1,0:T(8,128)} %get-tuple-element.105) | copy-start | bytes 9220
  318.7 12.7 %copy-start.52 = (f32[6,128]{1,0:T(8,128)S(1)}, f32[6,128]{1,0:T(8,128)}, u32[]{:S(2)}) copy-start(f32[6,128]{1,0:T(8,128)} %get-tuple-element.107) | copy-start | bytes 9220
  318.7 12.7 %copy-start.54 = (bf16[768,4096]{1,0:T(8,128)(2,1)S(1)}, bf16[768,4096]{1,0:T(8,128)(2,1)}, u32[]{:S(2)}) copy-start(bf16[768,4096]{1,0:T(8,128)(2,1)} %get-tuple-element.123) | copy-start | bytes 18874372
  341.4 7.2 %copy-start.1 = (f32[6,128,1024]{2,1,0:T(8,128)S(1)}, f32[6,128,1024]{2,1,0:T(8,128)}, u32[]{:S(2)}) copy-start(f32[6,128,1024]{2,1,0:T(8,128)} %subtract_multiply_fusion.2) | copy-start | bytes 9437188
  367.5 19.0 %slice-start = ((s8[6291456]{0:T(1024)(128)(4,1)}), s8[4194304]{0:T(1024)(128)(4,1)S(1)}, s32[]{:S(2)}) async-start(s8[6291456]{0:T(1024)(128)(4,1)} %bitcast.296), calls=%async_computation | async-start | bytes 8388608
  374.3 12.2 %slice-start.1 = ((s8[6291456]{0:T(1024)(128)(4,1)}), s8[2097152]{0:T(1024)(128)(4,1)S(1)}, s32[]{:S(2)}) async-start(s8[6291456]{0:T(1024)(128)(4,1)} %bitcast.296), calls=%async_computation.1 | async-start | bytes 4194304
  374.3 12.2 %copy-start.9 = (bf16[6,128,16,64]{1,3,2,0:T(8,128)(2,1)S(1)}, bf16[6,128,16,64]{1,3,2,0:T(8,128)(2,1)}, u32[]{:S(2)}) copy-start(bf16[6,128,16,64]{1,3,2,0:T(8,128)(2,1)} %copy.68) | copy-start | bytes 4718596
  374.3 12.2 %copy-start.22 = (bf16[6,128,1,16,64]{1,4,3,0,2:T(8,128)(2,1)S(1)}, bf16[6,128,1,16,64]{1,4,3,0,2:T(8,128)(2,1)}, u32[]{:S(2)}) copy-start(bf16[6,128,1,16,64]{1,4,3,0,2:T(8,128)(2,1)} %copy.100) | copy-start | bytes 4718596
  424.6 11.7 %copy-start.28 = (bf16[768,1024]{1,0:T(8,128)(2,1)S(1)}, bf16[768,1024]{1,0:T(8,128)(2,1)}, u32[]{:S(2)}) copy-start(bf16[768,1024]{1,0:T(8,128)(2,1)} %copy-done.27) | copy-start | bytes 4718596
  452.4 8.8 %copy-start.29 = (bf16[768,1024]{1,0:T(8,128)(2,1)S(1)}, bf16[768,1024]{1,0:T(8,128)(2,1)}, u32[]{:S(2)}) copy-start(bf16[768,1024]{1,0:T(8,128)(2,1)} %fusion.20) | copy-start | bytes 4718596
  473.0 11.3 %slice-start.2 = ((s8[6291456]{0:T(1024)(128)(4,1)}), s8[4194304]{0:T(1024)(128)(4,1)S(1)}, s32[]{:S(2)}) async-start(s8[6291456]{0:T(1024)(128)(4,1)} %bitcast.301), calls=%async_computation.2 | async-start | bytes 8388608
  473.0 11.3 %slice-start.3 = ((s8[6291456]{0:T(1024)(128)(4,1)}), s8[2097152]{0:T(1024)(128)(4,1)S(1)}, s32[]{:S(2)}) async-start(s8[6291456]{0:T(1024)(128)(4,1)} %bitcast.301), calls=%async_computation.3 | async-start | bytes 4194304
  661.6 7.0 %copy-start.15 = (f32[13,128,1024]{2,1,0:T(8,128)S(1)}, f32[13,128,1024]{2,1,0:T(8,128)}, u32[]{:S(2)}) copy-start(f32[13,128,1024]{2,1,0:T(8,128)} %get-tuple-element.23) | copy-start | bytes 20447236
  (34 other events, 94.7 us)

commit v2 on v0

v2 whole, which is shorter than its diff:
```python
import functools
import math

import jax
import jax.numpy as jnp
import numpy as np
from jax import lax
from jax.experimental import pallas as pl
from jax.experimental.pallas import tpu as pltpu
from jax.sharding import PartitionSpec as P

HEADS = 16
TE = 256
epsilon = 1e-05


MESH = pl.DeviceIdType.MESH
LOW, WIDE = jnp.bfloat16, jnp.float32
FRONT = 384
BLOCKS = 13
PIECES = 2 * BLOCKS
NT = (((1,), (1,)), ((), ()))
TN = (((0,), (0,)), ((), ()))


class Place:
    def __init__(self):
        r, f = lax.axis_index("rep"), lax.axis_index("fsdp")
        self.r, self.f = r, f
        self.x, self.core = r // 2, r % 2
        self.z, self.y = f // 2, f % 2
        z = self.z
        self.zs = [z, z + 1 - 2 * (z % 2), (z + 2) % 4, 3 - z]
        self.same = [zk * 2 + self.y for zk in self.zs]
        self.other = [zk * 2 + 1 - self.y for zk in self.zs]
        self.across_x = ((1 - self.x) * 2 + self.core, f)
        self.across_y = (r, self.other[0])
        self.across_core = (self.x * 2 + 1 - self.core, f)
        self.diagonal = ((1 - self.x) * 2 + 1 - self.core, f)
        self.along_z = [(r, fk) for fk in self.same]
        self.shards = self.same[1:] + self.other
        self.group = [(r, fk) for fk in self.shards]


def greet(peers):
    barrier = pltpu.get_barrier_semaphore()
    for peer in peers:
        pl.semaphore_signal(barrier, inc=1, device_id=peer, device_id_type=MESH)
    pl.semaphore_wait(barrier, len(peers))


def remote(src, dst, send, recv, peer):
    return pltpu.make_async_remote_copy(
        src_ref=src, dst_ref=dst, send_sem=send, recv_sem=recv, device_id=peer, device_id_type=MESH
    )


class Gather:
    steps = PIECES + 3

    def __init__(self, own, vec, full, vecs, send, recv, vsend, vrecv, lsem):
        self.at = Place()
        self.own, self.full, self.send, self.recv, self.lsem = own, full, send, recv, lsem
        self.vec, self.vecs, self.vsend, self.vrecv = vec, vecs, vsend, vrecv
        x = self.at.x
        rest = 1024 - FRONT
        self.mine = pl.ds(pl.multiple_of(x * FRONT, 128), rest)
        self.xcols = pl.ds(pl.multiple_of(x * rest, 128), FRONT)
        self.xland = pl.ds(pl.multiple_of((1 - x) * rest, 128), FRONT)

    def spot(self, c, z, y, cols, core=None):
        core = self.at.core if core is None else core
        return self.full.at[c // 2, z, y, core, c % 2, :, cols]

    def pair(self, c, i, src, dst, peer):
        return remote(src, dst, self.send.at[c, i], self.recv.at[c, i], peer)

    def z_copy(self, c, k):
        at = self.at
        src = self.own.at[c // 2, at.core, c % 2, :, self.mine]
        return self.pair(c, k - 1, src, self.spot(c, at.z, at.y, self.mine), at.along_z[k])

    def z_land(self, c, k):
        dst = self.spot(c, self.at.zs[k], self.at.y, self.mine)
        return self.pair(c, k - 1, dst, dst, self.at.along_z[k])

    def y_copy(self, c, k):
        at = self.at
        dst = self.spot(c, at.zs[k], at.y, self.mine)
        src = self.own.at[c // 2, at.core, c % 2, :, self.mine] if k == 0 else dst
        return self.pair(c, 3 + k, src, dst, at.across_y)

    def y_land(self, c, k):
        dst = self.spot(c, self.at.zs[k], 1 - self.at.y, self.mine)
        return self.pair(c, 3 + k, dst, dst, self.at.across_y)

    def x_place(self, c, k, cols):
        at = self.at
        if k < 3:
            return self.spot(c, at.zs[k + 1], at.y, cols)
        return self.spot(c, slice(None), 1 - at.y, cols)

    def x_copy(self, c, k):
        src = self.x_place(c, k, self.xcols)
        return self.pair(c, 7 + k, src, src, self.at.across_x)

    def x_land(self, c, k):
        dst = self.x_place(c, k, self.xland)
        return self.pair(c, 7 + k, dst, dst, self.at.across_x)

    def core_copy(self, c, core=None):
        part = self.spot(c, slice(None), slice(None), slice(None), core)
        return self.pair(c, 11, part, part, self.at.across_core)

    def local(self, c):
        at = self.at
        dst = self.spot(c, at.z, at.y, slice(None))
        return pltpu.make_async_copy(self.own.at[c // 2, at.core, c % 2], dst, self.lsem.at[c])

    def first(self, c):
        for k in range(1, 4):
            self.z_copy(c, k).start()
        self.y_copy(c, 0).start()
        self.local(c).start()

    ahead = 4

    def begin(self):
        at = self.at
        greet([at.across_core, at.across_x] + at.group)
        for i, peer in enumerate(at.group):
            remote(self.vec, self.vecs.at[at.f], self.vsend.at[i], self.vrecv.at[i], peer).start()
        for c in range(self.ahead):
            self.first(c)

    def vectors(self):
        at = self.at
        self.vecs[at.f] = self.vec[...]
        for i, peer in enumerate(at.group):
            remote(self.vec, self.vecs.at[at.shards[i]], self.vsend.at[i], self.vrecv.at[i], peer).wait()

    def step(self, t):
        @pl.when(t + self.ahead < PIECES)
        def _():
            self.first(t + self.ahead)

        @pl.when(t < PIECES)
        def _():
            for k in range(1, 4):
                self.z_land(t, k).wait_recv()
                self.y_copy(t, k).start()

        @pl.when(jnp.logical_and(t >= 1, t < PIECES + 1))
        def _():
            c = t - 1
            for k in range(4):
                if k == 3:
                    for j in range(4):
                        self.y_land(c, j).wait_recv()
                self.x_copy(c, k).start()

        @pl.when(jnp.logical_and(t >= 2, t < PIECES + 2))
        def _():
            c = t - 2
            self.local(c).wait()
            for k in range(4):
                self.x_land(c, k).wait_recv()
            self.core_copy(c).start()

        @pl.when(jnp.logical_and(t >= 3, t < PIECES + 3))
        def _():
            c = t - 3
            self.core_copy(c, 1 - self.at.core).wait_recv()
            for k in range(1, 4):
                self.z_copy(c, k).wait_send()
            for k in range(4):
                self.y_copy(c, k).wait_send()
                self.x_copy(c, k).wait_send()
            self.core_copy(c).wait_send()

    def run(self, lo, hi):
        def one(t, carry):
            self.step(t)
            return carry

        lax.fori_loop(lo, hi, one, 0)


GATHER_SCRATCH = [
    pltpu.VMEM((8, 16, 128), LOW),
    pltpu.SemaphoreType.DMA((PIECES, 12)),
    pltpu.SemaphoreType.DMA((PIECES, 12)),
    pltpu.SemaphoreType.DMA((7,)),
    pltpu.SemaphoreType.DMA((7,)),
    pltpu.SemaphoreType.DMA((PIECES,)),
]


GAIN1, BIAS1, BIAS_P, BIAS_O, GAIN2, BIAS2, BIAS_U, BIAS_D = 0, 1, 2, 5, 6, 7, 8, 12
HALF = 512
TILE = 32


def vector_spot(row, f):
    if BIAS_P <= row < BIAS_O:
        block = f * 3 + row - BIAS_P
        return BIAS_P + block // 8, block % 8
    return row, f


def for_each(count, body):
    def one(i, carry):
        body(i)
        return carry

    lax.fori_loop(0, count, one, 0)


def rows_at(i, size=TILE):
    return pl.ds(pl.multiple_of(i * size, size), size)


def lane_mean(v):
    return jnp.mean(v, axis=-1, keepdims=True)


def normalise(v):
    centred = v - lane_mean(v)
    inverse = lax.rsqrt(lane_mean(centred * centred) + epsilon)
    return centred * inverse, inverse


def row_of(ref, i):
    return ref[pl.ds(i, 1), :]


def modulated(ref, out, table, mods, gain, which, seqs):
    per = ref.shape[0] // seqs // TILE

    def body(i):
        s = i // per
        scale = table[gain : gain + 1, :] + row_of(mods, 2 * which * seqs + s)
        shift = table[gain + 1 : gain + 2, :] + row_of(mods, (2 * which + 1) * seqs + s)
        rows = rows_at(i)
        normed, _ = normalise(ref[rows, :].astype(WIDE))
        out[rows, :] = (normed * scale + shift).astype(LOW)

    for_each(ref.shape[0] // TILE, body)


def swapped(v):
    lane = lax.broadcasted_iota(jnp.int32, v.shape, 1)
    return jnp.where(lane % 64 < 32, pltpu.roll(v, 96, 1), pltpu.roll(v, 32, 1))


def forward_kernel(comm, seqs, *refs):
    refs = list(refs)
    take = lambda n: [refs.pop(0) for _ in range(n)]
    if comm:
        own, vec = take(2)
    else:
        full_in, table_in = take(2)
    tokens_hbm, feat, cosine, sine = take(4)
    if comm:
        (full,) = take(1)
    else:
        full = full_in
    table, mods = take(2)
    out_o, q_o, k_o, v_o, ctx_o, mid_o, normed2_o, activ_o, slope_o = take(9)
    tokens, weights, normed, q, k, v, ctx, mid, acc, activ, slope, wide, out_low = take(13)
    sem_in, sem_w, sem_out = take(3)
    tokens_n = tokens.shape[0]
    per = tokens_n // seqs

    tokens_in = pltpu.make_async_copy(tokens_hbm, tokens, sem_in)
    tokens_in.start()
    if comm:
        gather = Gather(own, vec, full, *refs)
        gather.begin()
        gather.vectors()
        for f in range(8):
            block = gather.vecs[f].astype(WIDE)
            for row in range(13):
                r, b = vector_spot(row, f)
                table[r : r + 1, b * 128 : (b + 1) * 128] = block[row : row + 1, :]
        run = gather.run
    else:
        table[...] = table_in[...]
        run = lambda lo, hi: None

    def weight(c, slot):
        copy = pltpu.make_async_copy(full.at[c], weights.at[slot], sem_w.at[slot])
        copy.start()
        copy.wait()
        return weights.at[slot]

    flat = (lambda w: w[...].reshape(1024, 1024)) if comm else (lambda w: w[...])

    saves = []

    def save(src, dst):
        copy = pltpu.make_async_copy(src, dst, sem_out.at[len(saves)])
        copy.start()
        saves.append(copy)

    run(0, 5)
    w = weight(0, 0)
    mods[...] = jnp.dot(feat[...], flat(w), preferred_element_type=WIDE)
    tokens_in.wait()
    modulated(tokens, normed, table, mods, GAIN1, 0, seqs)

    for j, (dst, dst_o) in enumerate([(q, q_o), (k, k_o), (v, v_o)]):
        run(5 + 2 * j, 7 + 2 * j)
        w = weight(1 + j, (1 + j) % 2)
        for h in range(2):
            cols = slice(h * HALF, (h + 1) * HALF)
            wide[...] = jnp.dot(normed[...], half_of(w, cols, comm), preferred_element_type=WIDE)
            bias = table[BIAS_P + j : BIAS_P + j + 1, cols]

            def body(i, h=h, bias=bias, dst=dst, j=j):
                rows = rows_at(i)
                where = pl.ds(pl.multiple_of((i % (per // TILE)) * TILE, TILE), TILE)
                piece = wide[rows, :] + bias
                if j == 2:
                    dst[rows, h * HALF : (h + 1) * HALF] = piece.astype(LOW)
                    return
                for n in range(HALF // 128):
                    part = piece[:, n * 128 : (n + 1) * 128]
                    turned = part * cosine[where, :] + swapped(part) * sine[where, :]
                    if j == 0:
                        turned = turned * 0.125
                    at = h * HALF + n * 128
                    dst[rows, at : at + 128] = turned.astype(LOW)

            for_each(tokens_n // TILE, body)
        save(dst, dst_o)

    lane = lax.broadcasted_iota(jnp.int32, (1, 128), 1)
    first_head = (lane < 64).astype(WIDE)
    second_head = 1.0 - first_head

    def heads(n):
        cols = pl.ds(pl.multiple_of(n * 128, 128), 128)
        for s in range(seqs):
            rows = slice(s * per, (s + 1) * per)
            qs = q[rows, cols]
            both = jnp.concatenate([qs * first_head.astype(LOW), qs * second_head.astype(LOW)], axis=0)
            scores = lax.dot_general(both, k[rows, cols], NT, preferred_element_type=WIDE)
            grown = jnp.exp(scores - jnp.max(scores, axis=-1, keepdims=True))
            probs = (grown / jnp.sum(grown, axis=-1, keepdims=True)).astype(LOW)
            mixed = jnp.dot(probs, v[rows, cols], preferred_element_type=WIDE)
            ctx[rows, cols] = (mixed[:per] * first_head + mixed[per:] * second_head).astype(LOW)
        if comm:
            pl.when(n >= 2)(lambda: gather.step(9 + n))

    for_each(8, heads)
    save(ctx, ctx_o)

    w = weight(4, 0)
    for h in range(2):
        cols = slice(h * HALF, (h + 1) * HALF)
        dot = jnp.dot(ctx[...], half_of(w, cols, comm), preferred_element_type=WIDE)
        mid[:, cols] = tokens[:, cols].astype(WIDE) + (dot + table[BIAS_O : BIAS_O + 1, cols])
    save(mid, mid_o)
    modulated(mid, normed, table, mods, GAIN2, 1, seqs)
    save(normed, normed2_o)

    def up(j):
        if comm:
            pl.when(j >= 1)(lambda: run(15 + 2 * j, 17 + 2 * j))
        w = weight(5 + j, 0)
        for h in range(2):
            cols = slice(h * HALF, (h + 1) * HALF)
            wide[...] = jnp.dot(normed[...], half_of(w, cols, comm), preferred_element_type=WIDE)

            def body(i, h=h, cols=cols):
                rows = rows_at(i)
                u = wide[rows, :] + table[pl.ds(BIAS_U + j, 1), cols]
                phi = 0.5 + 0.5 * lax.erf(u * (0.5**0.5))
                activ[j, rows, cols] = (u * phi).astype(LOW)
                bell = jnp.exp(-0.5 * (u * u)) * (1.0 / math.sqrt(2.0 * math.pi))
                slope[j, rows, cols] = (phi + u * bell).astype(LOW)

            for_each(tokens_n // TILE, body)

    for_each(4, up)
    save(activ, activ_o)
    save(slope, slope_o)

    def down(j):
        if comm:
            pl.when(j >= 1)(lambda: run(21 + 2 * j, 23 + 2 * j))
        w = weight(9 + j, 0)
        for h in range(2):
            cols = slice(h * HALF, (h + 1) * HALF)
            dot = jnp.dot(activ[j], half_of(w, cols, comm), preferred_element_type=WIDE)

            @pl.when(j == 0)
            def _():
                acc[:, cols] = mid[:, cols] + table[BIAS_D : BIAS_D + 1, cols] + dot

            @pl.when(j > 0)
            def _():
                acc[:, cols] = acc[:, cols] + dot

    for_each(4, down)
    out_low[...] = acc[...].astype(LOW)
    save(out_low, out_o)
    for copy in saves:
        copy.wait()


def half_of(w, cols, comm):
    if comm:
        return w[..., cols].reshape(1024, HALF)
    return w[:, cols]


def forward_call(comm, first, second, tokens, feat, cosine, sine, seqs):
    n, width = tokens.shape
    vmem, hbm = pl.BlockSpec(memory_space=pltpu.VMEM), pl.BlockSpec(memory_space=pl.ANY)
    low = jax.ShapeDtypeStruct((n, width), LOW)
    wide = jax.ShapeDtypeStruct((n, width), WIDE)
    shape4 = jax.ShapeDtypeStruct((4, n, width), LOW)
    block = (4, 2, 2, 2, 32, width) if comm else (width, width)
    outs = [
        (jax.ShapeDtypeStruct((16, width), WIDE), vmem),
        (jax.ShapeDtypeStruct((feat.shape[0], width), WIDE), vmem),
    ] + [(s, hbm) for s in (low, low, low, low, low, wide, low, shape4, shape4)]
    if comm:
        outs = [(jax.ShapeDtypeStruct((BLOCKS,) + block, LOW), hbm)] + outs
        first = first.reshape(BLOCKS, 2, 2, 32, width)
    buffer = pltpu.VMEM((n, width), LOW)
    got = pl.pallas_call(
        functools.partial(forward_kernel, comm, seqs),
        out_shape=tuple(s for s, _ in outs),
        in_specs=[hbm, vmem, hbm, vmem, vmem, vmem],
        out_specs=tuple(m for _, m in outs),
        scratch_shapes=[
            buffer,
            pltpu.VMEM((2,) + block, LOW),
            buffer,
            buffer,
            buffer,
            buffer,
            buffer,
            pltpu.VMEM((n, width), WIDE),
            pltpu.VMEM((n, width), WIDE),
            pltpu.VMEM((4, n, width), LOW),
            pltpu.VMEM((4, n, width), LOW),
            pltpu.VMEM((n, HALF), WIDE),
            buffer,
            pltpu.SemaphoreType.DMA,
            pltpu.SemaphoreType.DMA((2,)),
            pltpu.SemaphoreType.DMA((9,)),
        ]
        + (GATHER_SCRATCH if comm else []),
        compiler_params=pltpu.CompilerParams(
            collective_id=0 if comm else None, has_side_effects=comm, vmem_limit_bytes=60 * 2**20
        ),
        name="forward",
    )(first, second, tokens, feat, cosine, sine)
    if not comm:
        return (first, second) + tuple(got[1:])
    return (got[0].reshape(BLOCKS, width, width),) + tuple(got[1:])


RING = 10


class Reduce:
    def __init__(self, slots, own, l0, out, *scratch):
        self.at = Place()
        self.slots, self.own, self.l0, self.out = slots, own, l0, out
        (self.held, self.s0, self.l1a, self.l1b, self.l2, self.l3, self.la, self.stage) = scratch[:8]
        (self.bsend, self.brecv, self.lsem, self.send, self.recv, self.osem) = scratch[8:14]
        x = self.at.x
        self.front, self.back = pl.ds(0, FRONT), pl.ds(FRONT, 1024 - FRONT)
        self.mine = pl.ds(pl.multiple_of(x * 16, 16), 16)
        self.theirs = pl.ds(pl.multiple_of((1 - x) * 16, 16), 16)

    def begin(self):
        at = self.at
        greet([at.across_core, at.across_x, at.diagonal] + at.group)

    def core_copy(self, b):
        src = self.slots.at[b % 2, :, :, 1 - self.at.core]
        return remote(src, self.l0.at[b], self.bsend.at[b], self.brecv.at[b], self.at.across_core)

    def own_copy(self, b):
        return pltpu.make_async_copy(self.slots.at[b % 2, :, :, self.at.core], self.own.at[b], self.lsem.at[b % 2])

    def loads(self, b):
        return (
            pltpu.make_async_copy(self.own.at[b], self.held.at[0], self.lsem.at[2]),
            pltpu.make_async_copy(self.l0.at[b], self.held.at[1], self.lsem.at[3]),
        )

    def free(self, b):
        pl.when(b >= 2)(lambda: self.core_copy(b - 2).wait_send())

    def produced(self, b):
        self.core_copy(b).start()
        self.own_copy(b).start()

    def load(self, b):
        self.own_copy(b).wait()
        self.core_copy(b).wait_recv()
        for copy in self.loads(b):
            copy.start()

    def feed(self, b):
        for copy in self.loads(b):
            copy.wait()

        def add(i):
            z, y, h = i // 4, (i // 2) % 2, i % 2
            piece = self.held[0, z, y, h].astype(WIDE) + self.held[1, z, y, h].astype(WIDE)
            self.s0[(2 * b + h) % RING, z, y] = piece.astype(LOW)

        for_each(16, add)
        for h in range(2):
            self.x_one(2 * b + h).start()
            self.y_one(2 * b + h).start()

    def pair(self, p, i, src, dst, peer):
        return remote(src, dst, self.send.at[p, i], self.recv.at[p, i], peer)

    def x_one(self, p):
        src = self.s0.at[p % RING, :, :, self.theirs, self.front]
        return self.pair(p, 0, src, self.l1a.at[p], self.at.across_x)

    def y_one(self, p):
        src = self.s0.at[p % RING, :, 1 - self.at.y, :, self.back]
        return self.pair(p, 1, src, self.l1b.at[p], self.at.across_y)

    def y_two(self, p):
        return self.pair(p, 2, self.l1a.at[p, :, 1 - self.at.y], self.l2.at[p, :, :, self.front], self.at.across_y)

    def x_two(self, p):
        return self.pair(p, 3, self.l1b.at[p, :, self.theirs], self.l2.at[p, :, :, self.back], self.at.across_x)

    def z_copy(self, p, k):
        return self.pair(p, 3 + k, self.l2.at[p, self.at.zs[k]], self.l3.at[p, k - 1], self.at.along_z[k])

    def x_back(self, p, x=None):
        piece = self.la.at[p, self.at.core, self.at.x if x is None else x]
        return self.pair(p, 7, piece, piece, self.at.across_x)

    def core_back(self, p, core=None):
        piece = self.la.at[p, self.at.core if core is None else core]
        return self.pair(p, 8, piece, piece, self.at.across_core)

    def store(self, p):
        return pltpu.make_async_copy(self.stage.at[p % 2], self.out.at[p // 2, :, p % 2], self.osem.at[p % 2])

    def drain(self, d):
        at = self.at

        @pl.when(d < PIECES)
        def _():
            p = d
            self.x_one(p).wait()

            def add(i):
                z, y = i // 2, i % 2
                more = self.s0[p % RING, z, y, self.mine, self.front].astype(WIDE)
                self.l1a[p, z, y] = (self.l1a[p, z, y].astype(WIDE) + more).astype(LOW)

            for_each(8, add)
            self.y_two(p).start()
            self.y_one(p).wait()

            def add_too(z):
                more = self.s0[p % RING, z, at.y, :, self.back].astype(WIDE)
                self.l1b[p, z] = (self.l1b[p, z].astype(WIDE) + more).astype(LOW)

            for_each(4, add_too)
            self.x_two(p).start()

        @pl.when(jnp.logical_and(d >= 1, d < PIECES + 1))
        def _():
            p = d - 1
            self.y_two(p).wait()
            self.x_two(p).wait()

            def add(z):
                one = self.l2[p, z, :, self.front].astype(WIDE) + self.l1a[p, z, at.y].astype(WIDE)
                two = self.l2[p, z, :, self.back].astype(WIDE) + self.l1b[p, z, self.mine].astype(WIDE)
                self.l2[p, z, :, self.front] = one.astype(LOW)
                self.l2[p, z, :, self.back] = two.astype(LOW)

            for_each(4, add)
            for k in range(1, 4):
                self.z_copy(p, k).start()

        @pl.when(jnp.logical_and(d >= 2, d < PIECES + 2))
        def _():
            p = d - 2
            total = self.l2[p, at.z].astype(WIDE)
            for k in range(1, 4):
                self.z_copy(p, k).wait()
            for k in range(3):
                total = total + self.l3[p, k].astype(WIDE)
            self.la[p, at.core, at.x] = total.astype(LOW)
            self.x_back(p).start()

        @pl.when(jnp.logical_and(d >= 3, d < PIECES + 3))
        def _():
            p = d - 3
            self.x_back(p, 1 - at.x).wait_recv()
            self.core_back(p).start()

        @pl.when(jnp.logical_and(d >= 4, d < PIECES + 4))
        def _():
            p = d - 4
            self.x_back(p).wait_send()
            self.core_back(p).wait_send()
            self.core_back(p, 1 - at.core).wait_recv()
            pl.when(p >= 2)(lambda: self.store(p - 2).wait())
            self.stage[p % 2] = self.la[p].astype(WIDE)
            self.store(p).start()

    drains = PIECES + 4

    def run(self, lo, hi):
        def one(d, carry):
            self.drain(d)
            return carry

        lax.fori_loop(lo, hi, one, 0)

    def end(self):
        self.core_copy(BLOCKS - 2).wait_send()
        self.core_copy(BLOCKS - 1).wait_send()
        self.store(PIECES - 2).wait()
        self.store(PIECES - 1).wait()


REDUCE_SCRATCH = [
    pltpu.VMEM((2, 4, 2, 2, 32, 1024), LOW),
    pltpu.VMEM((RING, 4, 2, 32, 1024), LOW),
    pltpu.VMEM((PIECES, 4, 2, 16, FRONT), LOW),
    pltpu.VMEM((PIECES, 4, 32, 1024 - FRONT), LOW),
    pltpu.VMEM((PIECES, 4, 16, 1024), LOW),
    pltpu.VMEM((PIECES, 3, 16, 1024), LOW),
    pltpu.VMEM((PIECES, 2, 2, 16, 1024), LOW),
    pltpu.VMEM((2, 2, 2, 16, 1024), WIDE),
    pltpu.SemaphoreType.DMA((BLOCKS,)),
    pltpu.SemaphoreType.DMA((BLOCKS,)),
    pltpu.SemaphoreType.DMA((4,)),
    pltpu.SemaphoreType.DMA((PIECES, 9)),
    pltpu.SemaphoreType.DMA((PIECES, 9)),
    pltpu.SemaphoreType.DMA((2,)),
]


def sum_vectors(at, parts, got, sums, out, send, recv):
    def part(i):
        return remote(parts.at[at.shards[i]], got.at[i], send.at[i], recv.at[i], at.group[i])

    reps = [at.across_x, at.across_core, at.diagonal]

    def rest(i):
        return remote(sums.at[3], sums.at[i], send.at[7 + i], recv.at[7 + i], reps[i])

    def start():
        for i in range(7):
            part(i).start()

    def middle():
        total = parts[at.f]
        for i in range(7):
            part(i).wait()
            total = total + got[i]
        sums[3] = total
        for i in range(3):
            rest(i).start()

    def end():
        total = sums[3]
        for i in range(3):
            rest(i).wait()
            total = total + sums[i]
        out[...] = total

    return start, middle, end


COT, NORMED2, PAIR, GRAD_UP, QUERY, KEY, VALUE, NORMED1, TOKENS = 0, 1, 2, 4, 5, 6, 7, 8, 9
GRAD_BRANCH, CONTEXT, GRAD_CONTEXT = 2, 3, 4


def backward_kernel(comm, seqs, *refs):
    refs = list(refs)
    take = lambda n: [refs.pop(0) for _ in range(n)]
    full, cot_h, activ_h, slope_h, normed2_h, mid_h, q_h, k_h, v_h, ctx_h, tokens_h = take(11)
    table, mods, feat, cosine, sine = take(5)
    if comm:
        out, vec_out, input_o, own, l0 = take(5)
    else:
        out, vec_out, input_o = take(3)
    pool, gn, mid, weights, slots, sums, gtab, sem_in, sem_pair, sem_w, sem_mid, sem_slot = take(12)
    if comm:
        parts, vgot, vsums, vsend, vrecv = take(5)
        red = Reduce(slots, own, l0, out, *refs)
    tokens_n = pool.shape[1]
    per = tokens_n // seqs

    def fetch(src, i):
        return pltpu.make_async_copy(src, pool.at[i], sem_in.at[i])

    def fetch_pair(src, j):
        return pltpu.make_async_copy(src.at[j], pool.at[PAIR + j % 2], sem_pair.at[j % 2])

    def fetch_w(c, slot):
        return pltpu.make_async_copy(full.at[c], weights.at[slot], sem_w.at[slot])

    mid_in = pltpu.make_async_copy(mid_h, mid, sem_mid)
    fetch(cot_h, COT).start()
    fetch_pair(activ_h, 0).start()
    fetch_pair(activ_h, 1).start()
    fetch(normed2_h, NORMED2).start()
    fetch_w(9, 0).start()
    fetch_w(5, 1).start()
    mid_in.start()
    for src, i in ((q_h, QUERY), (k_h, KEY), (v_h, VALUE), (tokens_h, TOKENS)):
        fetch(src, i).start()
    if comm:
        red.begin()
        run, load, feed = red.run, red.load, red.feed
    else:
        run = load = feed = lambda *a: None
    when = pl.when if comm else (lambda cond: lambda body: None)

    half_cols = lambda h: slice(h * HALF, (h + 1) * HALF)

    def half_rows(slot, h):
        if comm:
            return weights[slot, 2 * h : 2 * h + 2].reshape(HALF, 1024)
        return weights[slot, half_cols(h), :]

    def produce(b, lhs, rhs_of):
        if comm:
            red.free(b)
        else:
            pl.when(b >= 2)(lambda: pltpu.make_async_copy(slots.at[b % 2], out.at[b - 2], sem_slot.at[b % 2]).wait())
        for h in range(2):
            block = rhs_of(lhs, h).astype(LOW)
            if comm:
                slots[b % 2, :, :, :, :, :, half_cols(h)] = block.reshape(4, 2, 2, 2, 32, HALF)
            else:
                slots[b % 2, :, half_cols(h)] = block
        if comm:
            red.produced(b)
        else:
            pltpu.make_async_copy(slots.at[b % 2], out.at[b], sem_slot.at[b % 2]).start()

    def times(i):
        return lambda lhs, h: lax.dot_general(lhs[...], pool[i, :, half_cols(h)], TN, preferred_element_type=WIDE)

    ones = jnp.ones((8, tokens_n), LOW)

    def column_sums(i, row):
        gtab[pl.ds(row, 1), :] = jnp.dot(ones, pool[i], preferred_element_type=WIDE)[:1]

    fetch(cot_h, COT).wait()

    def down(j):
        fetch_pair(activ_h, j).wait()
        produce(j, pool.at[PAIR + j % 2], times(COT))

        @pl.when(j < 2)
        def _():
            fetch_pair(activ_h, j + 2).start()

        @pl.when(j >= 2)
        def _():
            fetch_pair(slope_h, j - 2).start()

        @when(j == 0)
        def _():
            load(0)
            feed(0)

        when(j == 2)(lambda: load(1))

        @when(j == 3)
        def _():
            feed(1)
            load(2)
            run(0, 1)

    for_each(4, down)
    column_sums(COT, BIAS_D)
    fetch(normed2_h, NORMED2).wait()

    def up(j):
        fetch_pair(slope_h, j).wait()
        fetch_w(9 + j, 0).wait()
        for h in range(2):
            grad = lax.dot_general(pool[COT], half_rows(0, h), NT, preferred_element_type=WIDE)
            grad = grad * pool[PAIR + j % 2, :, half_cols(h)].astype(WIDE)
            pool[GRAD_UP, :, half_cols(h)] = grad.astype(LOW)

        @pl.when(j < 3)
        def _():
            fetch_w(10 + j, 0).start()

        pl.when(j < 2)(lambda: fetch_pair(slope_h, j + 2).start())
        feed(2 + j)
        run(1 + 2 * j, 2 + 2 * j)
        column_sums(GRAD_UP, BIAS_U + j)
        produce(4 + j, pool.at[NORMED2], times(GRAD_UP))
        fetch_w(5 + j, 1).wait()
        for h in range(2):
            more = lax.dot_general(pool[GRAD_UP], half_rows(1, h), NT, preferred_element_type=WIDE)

            @pl.when(j == 0)
            def _():
                gn[:, half_cols(h)] = more

            @pl.when(j > 0)
            def _():
                gn[:, half_cols(h)] = gn[:, half_cols(h)] + more

        @pl.when(j < 3)
        def _():
            fetch_w(6 + j, 1).start()

        load(3 + j)
        run(2 + 2 * j, 3 + 2 * j)

    for_each(4, up)
    fetch_w(4, 0).start()
    fetch_w(1, 1).start()
    fetch(ctx_h, CONTEXT).start()

    sums[...] = jnp.zeros_like(sums)

    def norm_back(which, gain, value_of, done):
        def body(i):
            rows = rows_at(i)
            s = i // (per // TILE)
            at_scale, at_shift = 2 * which * seqs + s, (2 * which + 1) * seqs + s
            scale = table[gain : gain + 1, :] + row_of(mods, at_scale)
            normed, inverse = normalise(value_of(rows).astype(WIDE))
            grad = gn[rows, :]
            sums[pl.ds(at_scale, 1), :] += jnp.sum(grad * normed, axis=0, keepdims=True)
            sums[pl.ds(at_shift, 1), :] += jnp.sum(grad, axis=0, keepdims=True)
            hat = grad * scale
            done(rows, inverse * (hat - lane_mean(hat) - normed * lane_mean(hat * normed)))

        for_each(tokens_n // TILE, body)
        for n in range(2):
            at = (2 * which + n) * seqs
            gtab[gain + n : gain + n + 1, :] = jnp.sum(sums[at : at + seqs, :], axis=0, keepdims=True)

    mid_in.wait()

    def done2(rows, grad):
        total = pool[COT, rows, :].astype(WIDE) + grad
        mid[rows, :] = total
        pool[GRAD_BRANCH, rows, :] = total.astype(LOW)

    norm_back(1, GAIN2, lambda rows: mid[rows, :], done2)
    feed(6)
    load(7)
    run(9, 10)

    fetch(ctx_h, CONTEXT).wait()
    column_sums(GRAD_BRANCH, BIAS_O)
    produce(8, pool.at[CONTEXT], times(GRAD_BRANCH))
    fetch_w(4, 0).wait()
    for h in range(2):
        grad = lax.dot_general(pool[GRAD_BRANCH], half_rows(0, h), NT, preferred_element_type=WIDE)
        pool[GRAD_CONTEXT, :, half_cols(h)] = grad.astype(LOW)
    fetch_w(2, 0).start()
    feed(7)
    load(8)
    run(10, 11)

    for src, i in ((q_h, QUERY), (k_h, KEY), (v_h, VALUE), (tokens_h, TOKENS)):
        fetch(src, i).wait()
    modulated(pool.at[TOKENS], pool.at[NORMED1], table, mods, GAIN1, 0, seqs)
    feed(8)

    lane = lax.broadcasted_iota(jnp.int32, (1, 128), 1)
    first_head = (lane < 64).astype(WIDE)
    second_head = 1.0 - first_head

    def split(v):
        return jnp.concatenate([v * first_head.astype(LOW), v * second_head.astype(LOW)], axis=0)

    def unturned(v):
        return v * cosine[...] - swapped(v) * sine[...]

    def heads(n):
        cols = pl.ds(pl.multiple_of(n * 128, 128), 128)
        for s in range(seqs):
            rows = slice(s * per, (s + 1) * per)
            keys = pool[KEY, rows, cols]
            both = split(pool[QUERY, rows, cols])
            grads = split(pool[GRAD_CONTEXT, rows, cols])
            scores = lax.dot_general(both, keys, NT, preferred_element_type=WIDE)
            grown = jnp.exp(scores - jnp.max(scores, axis=-1, keepdims=True))
            probs = grown / jnp.sum(grown, axis=-1, keepdims=True)
            grad_probs = lax.dot_general(grads, pool[VALUE, rows, cols], NT, preferred_element_type=WIDE)
            inner = jnp.sum(grad_probs * probs, axis=-1, keepdims=True)
            grad_scores = (probs * (grad_probs - inner)).astype(LOW)
            grad_v = lax.dot_general(probs.astype(LOW), grads, TN, preferred_element_type=WIDE)
            grad_k = lax.dot_general(grad_scores, both, TN, preferred_element_type=WIDE)
            grad_q = jnp.dot(grad_scores, keys, preferred_element_type=WIDE)
            grad_q = (grad_q[:per] * first_head + grad_q[per:] * second_head) * 0.125
            pool[QUERY, rows, cols] = unturned(grad_q).astype(LOW)
            pool[KEY, rows, cols] = unturned(grad_k).astype(LOW)
            pool[VALUE, rows, cols] = grad_v.astype(LOW)
        when(n < 7)(lambda: run(11 + n, 12 + n))

    for_each(8, heads)

    def project(j):
        column_sums(QUERY + j, BIAS_P + j)
        produce(9 + j, pool.at[NORMED1], times(QUERY + j))
        when(j == 1)(lambda: load(9))

        @when(j == 2)
        def _():
            feed(9)
            load(10)

    for_each(3, project)

    def project_back(j):
        slot = (1 + j) % 2
        fetch_w(1 + j, slot).wait()
        for h in range(2):
            more = lax.dot_general(pool[QUERY + j], half_rows(slot, h), NT, preferred_element_type=WIDE)

            @pl.when(j == 0)
            def _():
                gn[:, half_cols(h)] = more

            @pl.when(j > 0)
            def _():
                gn[:, half_cols(h)] = gn[:, half_cols(h)] + more

        pl.when(j == 0)(lambda: fetch_w(3, 1).start())
        when(j < 2)(lambda: feed(10 + j))
        when(j == 0)(lambda: load(11))
        run(18 + j, 19 + j)

    for_each(3, project_back)

    def done1(rows, grad):
        mid[rows, :] = mid[rows, :] + grad

    norm_back(0, GAIN1, lambda rows: pool[TOKENS, rows, :], done1)
    input_copy = pltpu.make_async_copy(mid, input_o, sem_mid)
    input_copy.start()
    if comm:
        for f in range(8):
            for row in range(13):
                r, b = vector_spot(row, f)
                parts[f, row : row + 1, :] = gtab[r : r + 1, b * 128 : (b + 1) * 128]
            parts[f, 13:16, :] = jnp.zeros((3, 128), WIDE)
        start, middle, end = sum_vectors(red.at, parts, vgot, vsums, vec_out, vsend, vrecv)
        start()
    else:
        vec_out[...] = gtab[...]

    def outer(lhs, h):
        terms = sums[:, half_cols(h)]
        high = terms.astype(LOW)
        rest = (terms - high.astype(WIDE)).astype(LOW)
        return lax.dot_general(lhs[...], high, TN, preferred_element_type=WIDE) + lax.dot_general(
            lhs[...], rest, TN, preferred_element_type=WIDE
        )

    produce(12, feat, outer)
    load(12)
    feed(12)
    if comm:
        run(21, 24)
        middle()
        run(24, 28)
        end()
        run(28, red.drains)
        red.end()
    else:
        for b in (11, 12):
            pltpu.make_async_copy(slots.at[b % 2], out.at[b], sem_slot.at[b % 2]).wait()
    input_copy.wait()


def backward_call(comm, full, cot, saved, tokens, table, mods, feat, cosine, sine, seqs):
    n, width = tokens.shape
    vmem, hbm = pl.BlockSpec(memory_space=pltpu.VMEM), pl.BlockSpec(memory_space=pl.ANY)
    q, k, v, ctx, mid, normed2, activ, slope = saved
    block = (4, 2, 2, 2, 32, width) if comm else (width, width)
    outs = [
        (jax.ShapeDtypeStruct((BLOCKS, 2, 2, 2, 16, width) if comm else (BLOCKS, width, width), WIDE if comm else LOW), hbm),
        (jax.ShapeDtypeStruct((16, 128) if comm else (16, width), WIDE), vmem),
        (jax.ShapeDtypeStruct((n, width), WIDE), hbm),
    ]
    extra = []
    if comm:
        part = jax.ShapeDtypeStruct((BLOCKS, 4, 2, 2, 32, width), LOW)
        outs += [(part, hbm), (part, hbm)]
        extra = [
            pltpu.VMEM((8, 16, 128), WIDE),
            pltpu.VMEM((7, 16, 128), WIDE),
            pltpu.VMEM((4, 16, 128), WIDE),
            pltpu.SemaphoreType.DMA((10,)),
            pltpu.SemaphoreType.DMA((10,)),
        ] + REDUCE_SCRATCH
        full = full.reshape((BLOCKS,) + block)
    got = pl.pallas_call(
        functools.partial(backward_kernel, comm, seqs),
        out_shape=tuple(s for s, _ in outs),
        in_specs=[hbm] * 11 + [vmem] * 5,
        out_specs=tuple(m for _, m in outs),
        scratch_shapes=[
            pltpu.VMEM((10, n, width), LOW),
            pltpu.VMEM((n, width), WIDE),
            pltpu.VMEM((n, width), WIDE),
            pltpu.VMEM((2,) + block, LOW),
            pltpu.VMEM((2,) + block, LOW),
            pltpu.VMEM((feat.shape[0], width), WIDE),
            pltpu.VMEM((16, width), WIDE),
            pltpu.SemaphoreType.DMA((10,)),
            pltpu.SemaphoreType.DMA((2,)),
            pltpu.SemaphoreType.DMA((2,)),
            pltpu.SemaphoreType.DMA,
            pltpu.SemaphoreType.DMA((2,)),
        ]
        + extra,
        compiler_params=pltpu.CompilerParams(
            collective_id=1 if comm else None, has_side_effects=comm, vmem_limit_bytes=62 * 2**20
        ),
        name="backward",
    )(full, cot, activ, slope, normed2, mid, q, k, v, ctx, tokens, table, mods, feat, cosine, sine)
    return got[0], got[1], got[2]


def rotary_constants(length, head_dim):
    half_width = head_dim // 2
    inverse = np.exp(np.arange(half_width, dtype=np.float32) * np.float32(-math.log(10000.0) / half_width))
    angles = np.arange(length, dtype=np.float32)[:, None] * inverse[None, :]
    cosine, sine = np.cos(angles), np.sin(angles)
    pair = np.concatenate([cosine, cosine], axis=1), np.concatenate([-sine, sine], axis=1)
    return tuple(np.concatenate([t, t], axis=1).astype(np.float32) for t in pair)


def wide_features(noise_times, shards_of, width):
    each = TE // shards_of
    half_width = TE // 2
    column = np.arange(width)
    feature = column // (4 * each) * each + column % each
    part = column // each % 4
    rates = np.exp((feature % half_width).astype(np.float32) * np.float32(math.log(100.0) / half_width))
    phases = (jnp.log(noise_times) * 0.25)[:, None] * rates[None, :]
    feat = jnp.where((feature < half_width)[None, :], jnp.sin(phases), jnp.cos(phases))
    chosen = (part[None, :] == np.arange(4)[:, None])[:, None, :]
    feat = jnp.where(chosen, feat[None], 0.0).reshape(-1, width).astype(LOW)
    pad = -feat.shape[0] % 32
    return jnp.pad(feat, ((0, pad), (0, 0)))


def pack_local(weights):
    project, output, up, down, time1, time2 = weights
    rows, width = output.shape
    shards_of = width // rows
    up_blocks = up.reshape(rows, shards_of, 4, rows).transpose(2, 0, 1, 3).reshape(4, rows, width)
    times = jnp.stack([time1, time2]).reshape(2, -1, 2, width).transpose(0, 2, 1, 3)
    return jnp.concatenate(
        [
            times.reshape(1, rows, width),
            project.reshape(rows, 3, width).transpose(1, 0, 2),
            output[None],
            up_blocks,
            down.reshape(4, rows, width),
        ]
    )


def pieces_of(flat, sizes):
    at, got = 0, []
    for size in sizes:
        got.append(flat[..., at : at + size])
        at += size
    return got


def shards(
    inputs,
    noise_times,
    cotangent,
    norm1_gain,
    norm1_bias,
    norm1_time,
    project_weight,
    project_bias,
    output_weight,
    output_bias,
    norm2_gain,
    norm2_bias,
    norm2_time,
    up_weight,
    up_bias,
    down_weight,
    down_bias,
):
    seqs = noise_times.shape[0]
    tokens_n, width = inputs.shape
    rows = output_weight.shape[0]
    shards_of = width // rows
    comm = shards_of == 8
    feat = wide_features(noise_times, shards_of, width)
    cosine, sine = rotary_constants(tokens_n // seqs, width // HEADS)
    own = pack_local((project_weight, output_weight, up_weight, down_weight, norm1_time, norm2_time))
    vectors = (norm1_gain, norm1_bias, project_bias, output_bias, norm2_gain, norm2_bias, up_bias, down_bias)
    sizes = [v.shape[0] for v in vectors]
    vec = jnp.concatenate(vectors)
    if comm:
        first, second = own, jnp.pad(vec.reshape(13, 128), ((0, 3), (0, 0)))
    else:
        first = lax.all_gather(own, "fsdp", axis=1, tiled=True)
        whole = pieces_of(lax.all_gather(vec, "fsdp", axis=0), sizes)
        whole[6] = whole[6].reshape(shards_of, 4, rows).transpose(1, 0, 2)
        second = jnp.concatenate([w.reshape(-1, width) for w in whole]).astype(WIDE)
        second = jnp.pad(second, ((0, 3), (0, 0)))
    full, table, mods, layer_out, *saved = forward_call(comm, first, second, inputs, feat, cosine, sine, seqs)
    mine, mine_vec, input_grad = backward_call(
        comm, full, cotangent, saved, inputs, table, mods, feat, cosine, sine, seqs
    )
    if comm:
        mine = mine.reshape(BLOCKS, rows, width)
        mine_vec = mine_vec.reshape(-1)
    else:
        mine = lax.psum_scatter(mine, "fsdp", scatter_dimension=1, tiled=True)
        mine = lax.psum(mine, "rep").astype(WIDE)
        whole = pieces_of(mine_vec[:13].reshape(-1), [shards_of * size for size in sizes])
        whole[6] = whole[6].reshape(4, shards_of, rows).transpose(1, 0, 2)
        mine_vec = jnp.concatenate([w.reshape(shards_of, -1) for w in whole], axis=1)
        mine_vec = lax.psum(lax.psum_scatter(mine_vec, "fsdp", scatter_dimension=0, tiled=True)[0], "rep")
    got = pieces_of(mine_vec, sizes)
    my_down = mine[0:4].reshape(4 * rows, width)
    my_up = mine[4:8].reshape(4, rows, shards_of, rows).transpose(1, 2, 0, 3).reshape(rows, 4 * width)
    my_project = mine[9:12].transpose(1, 0, 2).reshape(rows, 3 * width)
    my_times = mine[12].reshape(2, 2, -1, width).transpose(0, 2, 1, 3).reshape(2, -1, 2 * width)
    return (
        layer_out,
        input_grad,
        got[0],
        got[1],
        my_times[0],
        my_project,
        got[2],
        mine[8],
        got[3],
        got[4],
        got[5],
        my_times[1],
        my_up,
        got[6],
        my_down,
        got[7],
    )


def solution(mesh):
    placed = (
        P(("rep", "fsdp"), None),
        P(("rep", "fsdp")),
        P(("rep", "fsdp"), None),
        P("fsdp"),
        P("fsdp"),
        P("fsdp", None),
        P("fsdp", None),
        P("fsdp"),
        P("fsdp", None),
        P("fsdp"),
        P("fsdp"),
        P("fsdp"),
        P("fsdp", None),
        P("fsdp", None),
        P("fsdp"),
        P("fsdp", None),
        P("fsdp"),
    )
    return jax.shard_map(
        shards,
        mesh=mesh,
        in_specs=placed,
        out_specs=(
            P(("rep", "fsdp"), None),
            P(("rep", "fsdp"), None),
            P("fsdp"),
            P("fsdp"),
            P("fsdp", None),
            P("fsdp", None),
            P("fsdp"),
            P("fsdp", None),
            P("fsdp"),
            P("fsdp"),
            P("fsdp"),
            P("fsdp", None),
            P("fsdp", None),
            P("fsdp"),
            P("fsdp", None),
            P("fsdp"),
        ),
        check_vma=False,
    )
```

time: 1670 us -> 456 us (0.27)
  waiting for transfers between devices: 1120 us -> 0 us
  Pallas kernels: 0 us -> 402 us
  blocking collectives: 203 us -> 0 us
  matrix products: 168 us -> 0 us
  other arithmetic: 66.6 us -> 3.09 us
  local copies, waits for them, and re-layouts: 80.6 us -> 41.3 us
    reduce_scatter x6 -> x0, waiting for transfers between devices: 863 us -> none  [the longest x1 284 us: shards(): lax.psum_scatter(grad_down_weight, 'fsdp', scatter_dimension=0, tiled=True)]
    pallas_call x0 -> x2, Pallas kernels: none -> 402 us  [the longest x1 213 us: backward_call(): pl.pallas_call(functools.partial(backward_kernel, comm, seqs), out_shape=...]
    all_gather x6 -> x0, waiting for transfers between devices: 248 us -> none  [the longest x1 113 us: shards(): lax.all_gather(down_weight, 'fsdp', axis=0, tiled=True)]
    dot_general x22 -> x0, matrix products: 168 us -> none  [the longest x1 49.9 us: shards(): jnp.einsum('nd,fd->nf', cotangent, mlp_back[5], preferred_element_type=wi...]
    all_gather x8 -> x0, blocking collectives: 161 us -> none  [the longest x1 26.6 us: shards(): lax.all_gather(project_bias, 'fsdp', axis=0, tiled=True)]
    convert_element_type x32 -> x1, other arithmetic: 42.1 us -> 0.71 us  [wide_features(): feat = jnp.where(chosen, feat[None], 0.0).reshape(-1, width).astype(LOW)]
    unnamed x1 -> x0, blocking collectives: 35.7 us -> none
    reshape x3, local copies, waits for them, and re-layouts: 23.2 us -> 2.76 us  [the longest x1 1.85 us: shards(): mine[4:8].reshape(4, rows, shards_of, rows).transpose(1, 2, 0, 3)]
  transfers between devices with their start and end apart: 13 -> 0, of which waited for: 8 -> 0; matrix products, arithmetic and copies ran while one was open for 14% -> 0% of each run, Pallas kernels for 0% -> 0%
where the time goes in v2:
time: 456 us; the launch traced here: 447 us
  Pallas kernels  402 us (88%)
  local copies, waits for them, and re-layouts  41.3 us (9%)
    pallas_call x1, Pallas kernels, backward_call(): pl.pallas_call(functools.partial(backward_kernel, comm, seqs), out_shape=...  213 us
    pallas_call x1, Pallas kernels, forward_call(): pl.pallas_call(functools.partial(forward_kernel, comm, seqs), out_shape=t...  189 us
    unnamed x29, local copies, waits for them, and re-layouts  18 us

profile of v2, /device:TPU:0, one launch (start us, length us, event | category | flops | bytes accessed | tf_op | source)
XLA Modules:
  0.0 447.3 jit_solution(16180201728551805146)
XLA Ops:
  1.4 0.8 dynamic-update-slice
  2.2 0.8 dynamic-update-slice.1
  3.1 0.9 dynamic-update-slice.2
  3.9 0.8 dynamic-update-slice.3
  4.8 0.8 dynamic-update-slice.4
  5.6 0.8 dynamic-update-slice.5
  6.4 0.9 dynamic-update-slice.6
  7.3 0.8 dynamic-update-slice.7
  8.7 0.9 fusion.1
  11.0 1.0 stack.9
  12.0 1.0 stack.10
  13.0 1.5 copy.46
  17.0 1.0 constant_dynamic-update-slice_fusion.3
  18.7 1.1 constant_dynamic-update-slice_fusion.1
  19.8 1.1 constant_dynamic-update-slice_fusion.refs_0_
  20.9 188.8 %forward.1 = (bf16[13,4,2,2,2,32,1024]{6,5,4,3,2,1,0:T(8,128)(2,1)}, f32[16,1024]{1,0:T(8,128)}, f32[32,1024]{1,0:T(8,128)}, bf16[768,1024]{1,0:T(8,128)(2,1)}, ...) custom-call(bf16[13,2,2,32,1024]{4,3,2,1,0:T(8,128)(2,1)} %constant_, ...), custom_call_target="tpu_custom_call" | custom-call | tf_op jit(solution)/shard_map/forward/pallas_call | solution.py:434
  209.8 212.8 %backward.1 = (f32[13,2,2,2,16,1024]{5,4,3,2,1,0:T(8,128)}, f32[16,128]{1,0:T(8,128)}, f32[768,1024]{1,0:T(8,128)}, bf16[13,4,2,2,32,1024]{5,4,3,2,1,0:T(8,128)(2,1)}, bf16[13,4,2,2,32,1024]{5,4,3,2,1,0:T(8,128)(2,1)}) custom-call(bf16[13,4,2,2,2,32,1024]{6,5,4,3,2,1,0:T(8,128)(2,1)} %get-tuple-element.32.refs_0_, bf16[768,1024]{1,0:T(8,128)(2,1)} %refs_1_.1, ...), custom_call_target="tpu_custom_call" | custom-call | tf_op jit(solution)/shard_map/backward/pallas_call | solution.py:1018
  422.6 1.3 slice_bitcast_fusion.1
  423.8 1.3 slice_bitcast_fusion
  425.1 1.4 slice_bitcast_fusion.2
  426.5 2.3 fusion.3
  429.0 0.8 copy.55
  430.0 0.8 copy.54
  430.7 2.7 slice.84
  433.5 1.8 fusion.2
  435.9 1.4 copy.52
  437.2 1.9 reshape.153
  439.1 2.0 copy.50
  441.1 1.6 copy.53
  442.7 1.1 copy.73
  443.8 1.3 copy-done.1
  445.1 1.7 copy.74
  (30 shorter events, 7.0 us)
Async XLA Ops:
  0.6 14.2 %copy-start.3 = (bf16[128,4096]{1,0:T(8,128)(2,1)S(1)}, bf16[128,4096]{1,0:T(8,128)(2,1)}, u32[]{:S(2)}) copy-start(bf16[128,4096]{1,0:T(8,128)(2,1)} %param.35) | copy-start | bytes 3145732
  15.6 2.4 copy-start.5
  16.3 3.5 copy-start.4
  426.5 7.0 %copy-start = (f32[13,2,2,2,16,1024]{5,4,3,2,1,0:T(8,128)S(1)}, f32[13,2,2,2,16,1024]{5,4,3,2,1,0:T(8,128)}, u32[]{:S(2)}) copy-start(f32[13,2,2,2,16,1024]{5,4,3,2,1,0:T(8,128)} %get-tuple-element.45) | copy-start | bytes 20447236
  439.1 3.6 copy-start.2
  442.7 2.5 copy-start.1

commit v3 on v2

--- a/solution.py
+++ b/solution.py
@@ -56,13 +56,12 @@
 
 
 class Gather:
-    steps = PIECES + 3
-
     def __init__(self, own, vec, full, vecs, send, recv, vsend, vrecv, lsem):
         self.at = Place()
         self.own, self.full, self.send, self.recv, self.lsem = own, full, send, recv, lsem
         self.vec, self.vecs, self.vsend, self.vrecv = vec, vecs, vsend, vrecv
         x = self.at.x
+        self.middle = jnp.logical_and(self.at.z >= 1, self.at.z <= 2)
         rest = 1024 - FRONT
         self.mine = pl.ds(pl.multiple_of(x * FRONT, 128), rest)
         self.xcols = pl.ds(pl.multiple_of(x * rest, 128), FRONT)
@@ -75,10 +74,17 @@
     def pair(self, c, i, src, dst, peer):
         return remote(src, dst, self.send.at[c, i], self.recv.at[c, i], peer)
 
+    def owned(self, c, cols):
+        return self.own.at[c // 2, pl.ds(pl.multiple_of(self.at.core * 64 + c % 2 * 32, 32), 32), cols]
+
     def z_copy(self, c, k):
         at = self.at
-        src = self.own.at[c // 2, at.core, c % 2, :, self.mine]
+        src = self.owned(c, self.mine)
         return self.pair(c, k - 1, src, self.spot(c, at.z, at.y, self.mine), at.along_z[k])
+
+    def z_relay(self, c):
+        dst = self.spot(c, self.at.zs[2], self.at.y, self.mine)
+        return remote(dst, dst, self.send.at[c, 12], self.recv.at[c, 2], self.at.along_z[1])
 
     def z_land(self, c, k):
         dst = self.spot(c, self.at.zs[k], self.at.y, self.mine)
@@ -87,7 +93,7 @@
     def y_copy(self, c, k):
         at = self.at
         dst = self.spot(c, at.zs[k], at.y, self.mine)
-        src = self.own.at[c // 2, at.core, c % 2, :, self.mine] if k == 0 else dst
+        src = self.owned(c, self.mine) if k == 0 else dst
         return self.pair(c, 3 + k, src, dst, at.across_y)
 
     def y_land(self, c, k):
@@ -115,11 +121,12 @@
     def local(self, c):
         at = self.at
         dst = self.spot(c, at.z, at.y, slice(None))
-        return pltpu.make_async_copy(self.own.at[c // 2, at.core, c % 2], dst, self.lsem.at[c])
+        return pltpu.make_async_copy(self.owned(c, slice(None)), dst, self.lsem.at[c])
 
     def first(self, c):
-        for k in range(1, 4):
+        for k in range(1, 3):
             self.z_copy(c, k).start()
+        pl.when(self.middle)(lambda: self.z_copy(c, 3).start())
         self.y_copy(c, 0).start()
         self.local(c).start()
 
@@ -130,6 +137,8 @@
         greet([at.across_core, at.across_x] + at.group)
         for i, peer in enumerate(at.group):
             remote(self.vec, self.vecs.at[at.f], self.vsend.at[i], self.vrecv.at[i], peer).start()
+
+    def start(self):
         for c in range(self.ahead):
             self.first(c)
 
@@ -139,45 +148,62 @@
         for i, peer in enumerate(at.group):
             remote(self.vec, self.vecs.at[at.shards[i]], self.vsend.at[i], self.vrecv.at[i], peer).wait()
 
+    lag_x, lag_core, lag_done = 2, 4, 5
+
     def step(self, t):
+        lag_x, lag_core, lag_done = self.lag_x, self.lag_core, self.lag_done
+
         @pl.when(t + self.ahead < PIECES)
         def _():
             self.first(t + self.ahead)
 
         @pl.when(t < PIECES)
         def _():
-            for k in range(1, 4):
+            for k in (2, 1, 3):
                 self.z_land(t, k).wait_recv()
+                if k == 2:
+                    pl.when(self.middle)(lambda: self.z_relay(t).start())
                 self.y_copy(t, k).start()
 
-        @pl.when(jnp.logical_and(t >= 1, t < PIECES + 1))
-        def _():
-            c = t - 1
+        @pl.when(jnp.logical_and(t >= lag_x, t < PIECES + lag_x))
+        def _():
+            c = t - lag_x
             for k in range(4):
                 if k == 3:
                     for j in range(4):
                         self.y_land(c, j).wait_recv()
                 self.x_copy(c, k).start()
 
-        @pl.when(jnp.logical_and(t >= 2, t < PIECES + 2))
-        def _():
-            c = t - 2
+        @pl.when(jnp.logical_and(t >= lag_core, t < PIECES + lag_core))
+        def _():
+            c = t - lag_core
             self.local(c).wait()
             for k in range(4):
                 self.x_land(c, k).wait_recv()
             self.core_copy(c).start()
 
-        @pl.when(jnp.logical_and(t >= 3, t < PIECES + 3))
-        def _():
-            c = t - 3
+        @pl.when(jnp.logical_and(t >= lag_done, t < PIECES + lag_done))
+        def _():
+            c = t - lag_done
             self.core_copy(c, 1 - self.at.core).wait_recv()
-            for k in range(1, 4):
+            for k in range(1, 3):
                 self.z_copy(c, k).wait_send()
+
+            @pl.when(self.middle)
+            def _():
+                self.z_copy(c, 3).wait_send()
+                self.z_relay(c).wait_send()
+
             for k in range(4):
                 self.y_copy(c, k).wait_send()
                 self.x_copy(c, k).wait_send()
             self.core_copy(c).wait_send()
 
+    steps = PIECES + lag_done
+
+    def ready(self, block):
+        return 2 * block + 2 + self.lag_done
+
     def run(self, lo, hi):
         def one(t, carry):
             self.step(t)
@@ -187,8 +213,8 @@
 
 
 GATHER_SCRATCH = [
-    pltpu.VMEM((8, 16, 128), LOW),
-    pltpu.SemaphoreType.DMA((PIECES, 12)),
+    pltpu.VMEM((8, 16, 128), WIDE),
+    pltpu.SemaphoreType.DMA((PIECES, 13)),
     pltpu.SemaphoreType.DMA((PIECES, 12)),
     pltpu.SemaphoreType.DMA((7,)),
     pltpu.SemaphoreType.DMA((7,)),
@@ -202,9 +228,10 @@
 
 
 def vector_spot(row, f):
-    if BIAS_P <= row < BIAS_O:
-        block = f * 3 + row - BIAS_P
-        return BIAS_P + block // 8, block % 8
+    for first, count in ((BIAS_P, 3), (BIAS_U, 4)):
+        if first <= row < first + count:
+            block = f * count + row - first
+            return first + block // 8, block % 8
     return row, f
 
 
@@ -253,11 +280,20 @@
     return jnp.where(lane % 64 < 32, pltpu.roll(v, 96, 1), pltpu.roll(v, 32, 1))
 
 
+def pack(local, own, sems):
+    project, output, up, down, time1, time2 = local
+    pairs = [(t.at[:, pl.ds(1024 * h, 1024)], own.at[0, pl.ds(64 * n + 32 * h, 32)]) for n, t in enumerate((time1, time2)) for h in range(2)]
+    pairs += [(project.at[:, pl.ds(1024 * j, 1024)], own.at[1 + j]) for j in range(3)] + [(output, own.at[4])]
+    pairs += [(up.at[:, pl.ds(1024 * j, 1024)], own.at[5 + j]) for j in range(4)]
+    pairs += [(down.at[pl.ds(128 * j, 128)], own.at[9 + j]) for j in range(4)]
+    return [pltpu.make_async_copy(src, dst, sems.at[i]) for i, (src, dst) in enumerate(pairs)]
+
+
 def forward_kernel(comm, seqs, *refs):
     refs = list(refs)
     take = lambda n: [refs.pop(0) for _ in range(n)]
     if comm:
-        own, vec = take(2)
+        local, vec = take(6), take(1)[0]
     else:
         full_in, table_in = take(2)
     tokens_hbm, feat, cosine, sine = take(4)
@@ -275,11 +311,18 @@
     tokens_in = pltpu.make_async_copy(tokens_hbm, tokens, sem_in)
     tokens_in.start()
     if comm:
+        own, sem_own = take(2)
         gather = Gather(own, vec, full, *refs)
+        packing = pack(local, own, sem_own)
+        for copy in packing:
+            copy.start()
         gather.begin()
+        for copy in packing:
+            copy.wait()
+        gather.start()
         gather.vectors()
         for f in range(8):
-            block = gather.vecs[f].astype(WIDE)
+            block = gather.vecs[f]
             for row in range(13):
                 r, b = vector_spot(row, f)
                 table[r : r + 1, b * 128 : (b + 1) * 128] = block[row : row + 1, :]
@@ -288,12 +331,18 @@
         table[...] = table_in[...]
         run = lambda lo, hi: None
 
-    def weight(c, slot):
-        copy = pltpu.make_async_copy(full.at[c], weights.at[slot], sem_w.at[slot])
-        copy.start()
-        copy.wait()
-        return weights.at[slot]
-
+    def fetch(c):
+        return pltpu.make_async_copy(full.at[c], weights.at[c % 2], sem_w.at[c % 2])
+
+    def arrive(c, lo, hi):
+        run(lo, hi)
+        fetch(c).start()
+
+    def weight(c):
+        fetch(c).wait()
+        return weights.at[c % 2]
+
+    ready = Gather.lag_done + 2
     flat = (lambda w: w[...].reshape(1024, 1024)) if comm else (lambda w: w[...])
 
     saves = []
@@ -303,18 +352,21 @@
         copy.start()
         saves.append(copy)
 
-    run(0, 5)
-    w = weight(0, 0)
+    arrive(0, 0, ready)
+    w = weight(0)
     mods[...] = jnp.dot(feat[...], flat(w), preferred_element_type=WIDE)
     tokens_in.wait()
+    arrive(1, ready, ready + 2)
     modulated(tokens, normed, table, mods, GAIN1, 0, seqs)
 
     for j, (dst, dst_o) in enumerate([(q, q_o), (k, k_o), (v, v_o)]):
-        run(5 + 2 * j, 7 + 2 * j)
-        w = weight(1 + j, (1 + j) % 2)
+        w = weight(1 + j)
         for h in range(2):
             cols = slice(h * HALF, (h + 1) * HALF)
             wide[...] = jnp.dot(normed[...], half_of(w, cols, comm), preferred_element_type=WIDE)
+            run(ready + 2 + 2 * j + h, ready + 3 + 2 * j + h)
+            if h == 1:
+                fetch(2 + j).start()
             bias = table[BIAS_P + j : BIAS_P + j + 1, cols]
 
             def body(i, h=h, bias=bias, dst=dst, j=j):
@@ -351,35 +403,43 @@
             mixed = jnp.dot(probs, v[rows, cols], preferred_element_type=WIDE)
             ctx[rows, cols] = (mixed[:per] * first_head + mixed[per:] * second_head).astype(LOW)
         if comm:
-            pl.when(n >= 2)(lambda: gather.step(9 + n))
+            pl.when(n >= 2)(lambda: gather.step(ready + 6 + n))
 
     for_each(8, heads)
     save(ctx, ctx_o)
 
-    w = weight(4, 0)
+    w = weight(4)
     for h in range(2):
         cols = slice(h * HALF, (h + 1) * HALF)
         dot = jnp.dot(ctx[...], half_of(w, cols, comm), preferred_element_type=WIDE)
         mid[:, cols] = tokens[:, cols].astype(WIDE) + (dot + table[BIAS_O : BIAS_O + 1, cols])
+    arrive(5, ready + 14, ready + 15)
     save(mid, mid_o)
     modulated(mid, normed, table, mods, GAIN2, 1, seqs)
     save(normed, normed2_o)
 
     def up(j):
-        if comm:
-            pl.when(j >= 1)(lambda: run(15 + 2 * j, 17 + 2 * j))
-        w = weight(5 + j, 0)
+        w = weight(5 + j)
         for h in range(2):
             cols = slice(h * HALF, (h + 1) * HALF)
             wide[...] = jnp.dot(normed[...], half_of(w, cols, comm), preferred_element_type=WIDE)
+            if h == 0:
+                once = ready + 15 + 2 * j - jnp.maximum(j - 2, 0)
+                run(once, once + 1)
+            else:
+                run(ready + 16 + 2 * j, ready + 16 + 2 * j + (j < 2).astype(jnp.int32))
+                fetch(6 + j).start()
 
             def body(i, h=h, cols=cols):
                 rows = rows_at(i)
                 u = wide[rows, :] + table[pl.ds(BIAS_U + j, 1), cols]
                 phi = 0.5 + 0.5 * lax.erf(u * (0.5**0.5))
-                activ[j, rows, cols] = (u * phi).astype(LOW)
                 bell = jnp.exp(-0.5 * (u * u)) * (1.0 / math.sqrt(2.0 * math.pi))
-                slope[j, rows, cols] = (phi + u * bell).astype(LOW)
+                result, grow = (u * phi).astype(LOW), (phi + u * bell).astype(LOW)
+                place = pl.ds(pl.multiple_of((2 * j + h) * 128, 128), 128)
+                for n in range(4):
+                    activ[n, rows, place] = result[:, n * 128 : (n + 1) * 128]
+                    slope[n, rows, place] = grow[:, n * 128 : (n + 1) * 128]
 
             for_each(tokens_n // TILE, body)
 
@@ -388,9 +448,7 @@
     save(slope, slope_o)
 
     def down(j):
-        if comm:
-            pl.when(j >= 1)(lambda: run(21 + 2 * j, 23 + 2 * j))
-        w = weight(9 + j, 0)
+        w = weight(9 + j)
         for h in range(2):
             cols = slice(h * HALF, (h + 1) * HALF)
             dot = jnp.dot(activ[j], half_of(w, cols, comm), preferred_element_type=WIDE)
@@ -402,6 +460,9 @@
             @pl.when(j > 0)
             def _():
                 acc[:, cols] = acc[:, cols] + dot
+
+            if h == 0:
+                pl.when(j < 3)(lambda: arrive(10 + j, ready + 21 + j, ready + 22 + j))
 
     for_each(4, down)
     out_low[...] = acc[...].astype(LOW)
@@ -416,7 +477,7 @@
     return w[:, cols]
 
 
-def forward_call(comm, first, second, tokens, feat, cosine, sine, seqs):
+def forward_call(comm, weights, vectors, tokens, feat, cosine, sine, seqs):
     n, width = tokens.shape
     vmem, hbm = pl.BlockSpec(memory_space=pltpu.VMEM), pl.BlockSpec(memory_space=pl.ANY)
     low = jax.ShapeDtypeStruct((n, width), LOW)
@@ -427,14 +488,15 @@
         (jax.ShapeDtypeStruct((16, width), WIDE), vmem),
         (jax.ShapeDtypeStruct((feat.shape[0], width), WIDE), vmem),
     ] + [(s, hbm) for s in (low, low, low, low, low, wide, low, shape4, shape4)]
+    extra = []
     if comm:
         outs = [(jax.ShapeDtypeStruct((BLOCKS,) + block, LOW), hbm)] + outs
-        first = first.reshape(BLOCKS, 2, 2, 32, width)
+        extra = [pltpu.VMEM((BLOCKS, 128, width), LOW), pltpu.SemaphoreType.DMA((16,))] + GATHER_SCRATCH
     buffer = pltpu.VMEM((n, width), LOW)
     got = pl.pallas_call(
         functools.partial(forward_kernel, comm, seqs),
         out_shape=tuple(s for s, _ in outs),
-        in_specs=[hbm, vmem, hbm, vmem, vmem, vmem],
+        in_specs=[hbm] * len(weights) + [vmem, hbm, vmem, vmem, vmem],
         out_specs=tuple(m for _, m in outs),
         scratch_shapes=[
             buffer,
@@ -454,14 +516,14 @@
             pltpu.SemaphoreType.DMA((2,)),
             pltpu.SemaphoreType.DMA((9,)),
         ]
-        + (GATHER_SCRATCH if comm else []),
+        + extra,
         compiler_params=pltpu.CompilerParams(
             collective_id=0 if comm else None, has_side_effects=comm, vmem_limit_bytes=60 * 2**20
         ),
         name="forward",
-    )(first, second, tokens, feat, cosine, sine)
+    )(*weights, vectors, tokens, feat, cosine, sine)
     if not comm:
-        return (first, second) + tuple(got[1:])
+        return (weights[0], vectors) + tuple(got[1:])
     return (got[0].reshape(BLOCKS, width, width),) + tuple(got[1:])
 
 
@@ -469,11 +531,11 @@
 
 
 class Reduce:
-    def __init__(self, slots, own, l0, out, *scratch):
+    def __init__(self, slots, own, l0, outs, *scratch):
         self.at = Place()
-        self.slots, self.own, self.l0, self.out = slots, own, l0, out
-        (self.held, self.s0, self.l1a, self.l1b, self.l2, self.l3, self.la, self.stage) = scratch[:8]
-        (self.bsend, self.brecv, self.lsem, self.send, self.recv, self.osem) = scratch[8:14]
+        self.slots, self.own, self.l0, self.outs = slots, own, l0, outs
+        (self.held, self.s0, self.l1a, self.l1b, self.l2, self.l3, self.la) = scratch[:7]
+        (self.bsend, self.brecv, self.lsem, self.send, self.recv, self.osem) = scratch[7:13]
         x = self.at.x
         self.front, self.back = pl.ds(0, FRONT), pl.ds(FRONT, 1024 - FRONT)
         self.mine = pl.ds(pl.multiple_of(x * 16, 16), 16)
@@ -544,18 +606,37 @@
         return self.pair(p, 3 + k, self.l2.at[p, self.at.zs[k]], self.l3.at[p, k - 1], self.at.along_z[k])
 
     def x_back(self, p, x=None):
-        piece = self.la.at[p, self.at.core, self.at.x if x is None else x]
+        piece = self.la.at[p, self.at.core, pl.ds(pl.multiple_of((self.at.x if x is None else x) * 16, 16), 16)]
         return self.pair(p, 7, piece, piece, self.at.across_x)
 
     def core_back(self, p, core=None):
         piece = self.la.at[p, self.at.core if core is None else core]
         return self.pair(p, 8, piece, piece, self.at.across_core)
 
-    def store(self, p):
-        return pltpu.make_async_copy(self.stage.at[p % 2], self.out.at[p // 2, :, p % 2], self.osem.at[p % 2])
+    def store(self, p, dsts):
+        for core, dst in enumerate(dsts):
+            pltpu.make_async_copy(self.la.at[p, core], dst, self.osem.at[p, core]).start()
+
+    def store_all(self, p):
+        project, output, up, down, *times = self.outs
+        b, h = p // 2, p % 2
+
+        def rows(core, first=0):
+            return pl.ds(pl.multiple_of(first + core * 64 + h * 32, 32), 32)
+
+        def cols(j):
+            return pl.ds(pl.multiple_of(j * 1024, 1024), 1024)
+
+        pl.when(b < 4)(lambda: self.store(p, [down.at[rows(c, b * 128)] for c in range(2)]))
+        pl.when(jnp.logical_and(b >= 4, b < 8))(lambda: self.store(p, [up.at[rows(c), cols(b - 4)] for c in range(2)]))
+        pl.when(b == 8)(lambda: self.store(p, [output.at[rows(c)] for c in range(2)]))
+        pl.when(jnp.logical_and(b >= 9, b < 12))(lambda: self.store(p, [project.at[rows(c), cols(b - 9)] for c in range(2)]))
+        pl.when(b == 12)(lambda: self.store(p, [t.at[:, cols(h)] for t in times]))
+
+    lags = (2, 3, 5, 6)
 
     def drain(self, d):
-        at = self.at
+        at, lags = self.at, self.lags
 
         @pl.when(d < PIECES)
         def _():
@@ -578,9 +659,9 @@
             for_each(4, add_too)
             self.x_two(p).start()
 
-        @pl.when(jnp.logical_and(d >= 1, d < PIECES + 1))
-        def _():
-            p = d - 1
+        @pl.when(jnp.logical_and(d >= lags[0], d < PIECES + lags[0]))
+        def _():
+            p = d - lags[0]
             self.y_two(p).wait()
             self.x_two(p).wait()
 
@@ -594,34 +675,32 @@
             for k in range(1, 4):
                 self.z_copy(p, k).start()
 
-        @pl.when(jnp.logical_and(d >= 2, d < PIECES + 2))
-        def _():
-            p = d - 2
+        @pl.when(jnp.logical_and(d >= lags[1], d < PIECES + lags[1]))
+        def _():
+            p = d - lags[1]
             total = self.l2[p, at.z].astype(WIDE)
             for k in range(1, 4):
                 self.z_copy(p, k).wait()
             for k in range(3):
                 total = total + self.l3[p, k].astype(WIDE)
-            self.la[p, at.core, at.x] = total.astype(LOW)
+            self.la[p, at.core, self.mine] = total.astype(LOW)
             self.x_back(p).start()
 
-        @pl.when(jnp.logical_and(d >= 3, d < PIECES + 3))
-        def _():
-            p = d - 3
+        @pl.when(jnp.logical_and(d >= lags[2], d < PIECES + lags[2]))
+        def _():
+            p = d - lags[2]
             self.x_back(p, 1 - at.x).wait_recv()
             self.core_back(p).start()
 
-        @pl.when(jnp.logical_and(d >= 4, d < PIECES + 4))
-        def _():
-            p = d - 4
+        @pl.when(jnp.logical_and(d >= lags[3], d < PIECES + lags[3]))
+        def _():
+            p = d - lags[3]
             self.x_back(p).wait_send()
             self.core_back(p).wait_send()
             self.core_back(p, 1 - at.core).wait_recv()
-            pl.when(p >= 2)(lambda: self.store(p - 2).wait())
-            self.stage[p % 2] = self.la[p].astype(WIDE)
-            self.store(p).start()
-
-    drains = PIECES + 4
+            self.store_all(p)
+
+    drains = PIECES + lags[3]
 
     def run(self, lo, hi):
         def one(d, carry):
@@ -633,8 +712,12 @@
     def end(self):
         self.core_copy(BLOCKS - 2).wait_send()
         self.core_copy(BLOCKS - 1).wait_send()
-        self.store(PIECES - 2).wait()
-        self.store(PIECES - 1).wait()
+
+        def stored(p):
+            for core in range(2):
+                pltpu.make_async_copy(self.la.at[p, core], self.outs[1].at[pl.ds(0, 32)], self.osem.at[p, core]).wait()
+
+        for_each(PIECES, stored)
 
 
 REDUCE_SCRATCH = [
@@ -644,14 +727,13 @@
     pltpu.VMEM((PIECES, 4, 32, 1024 - FRONT), LOW),
     pltpu.VMEM((PIECES, 4, 16, 1024), LOW),
     pltpu.VMEM((PIECES, 3, 16, 1024), LOW),
-    pltpu.VMEM((PIECES, 2, 2, 16, 1024), LOW),
-    pltpu.VMEM((2, 2, 2, 16, 1024), WIDE),
+    pltpu.VMEM((PIECES, 2, 32, 1024), LOW),
     pltpu.SemaphoreType.DMA((BLOCKS,)),
     pltpu.SemaphoreType.DMA((BLOCKS,)),
     pltpu.SemaphoreType.DMA((4,)),
     pltpu.SemaphoreType.DMA((PIECES, 9)),
     pltpu.SemaphoreType.DMA((PIECES, 9)),
-    pltpu.SemaphoreType.DMA((2,)),
+    pltpu.SemaphoreType.DMA((PIECES, 2)),
 ]
 
 
@@ -687,8 +769,8 @@
     return start, middle, end
 
 
-COT, NORMED2, PAIR, GRAD_UP, QUERY, KEY, VALUE, NORMED1, TOKENS = 0, 1, 2, 4, 5, 6, 7, 8, 9
-GRAD_BRANCH, CONTEXT, GRAD_CONTEXT = 2, 3, 4
+COT, NORMED2, PAIR, GRAD_UP, TOKENS, NORMED1 = 0, 1, 2, 4, 8, 9
+GRAD_BRANCH, CONTEXT, QUERY, KEY, VALUE, GRAD_CONTEXT = 2, 3, 4, 5, 6, 7
 
 
 def backward_kernel(comm, seqs, *refs):
@@ -696,14 +778,16 @@
     take = lambda n: [refs.pop(0) for _ in range(n)]
     full, cot_h, activ_h, slope_h, normed2_h, mid_h, q_h, k_h, v_h, ctx_h, tokens_h = take(11)
     table, mods, feat, cosine, sine = take(5)
+    outs = take(6 if comm else 1)
+    vec_out, input_o = take(2)
     if comm:
-        out, vec_out, input_o, own, l0 = take(5)
+        own, l0 = take(2)
     else:
-        out, vec_out, input_o = take(3)
+        (out,) = outs
     pool, gn, mid, weights, slots, sums, gtab, sem_in, sem_pair, sem_w, sem_mid, sem_slot = take(12)
     if comm:
         parts, vgot, vsums, vsend, vrecv = take(5)
-        red = Reduce(slots, own, l0, out, *refs)
+        red = Reduce(slots, own, l0, outs, *refs)
     tokens_n = pool.shape[1]
     per = tokens_n // seqs
 
@@ -722,10 +806,9 @@
     fetch_pair(activ_h, 1).start()
     fetch(normed2_h, NORMED2).start()
     fetch_w(9, 0).start()
-    fetch_w(5, 1).start()
+    fetch_w(10, 1).start()
     mid_in.start()
-    for src, i in ((q_h, QUERY), (k_h, KEY), (v_h, VALUE), (tokens_h, TOKENS)):
-        fetch(src, i).start()
+    fetch(tokens_h, TOKENS).start()
     if comm:
         red.begin()
         run, load, feed = red.run, red.load, red.feed
@@ -795,26 +878,39 @@
     column_sums(COT, BIAS_D)
     fetch(normed2_h, NORMED2).wait()
 
+    def activ_back(j):
+        fetch_pair(slope_h, j).wait()
+        fetch_w(9 + j, j % 2).wait()
+        for h in range(2):
+            grad = lax.dot_general(pool[COT], half_rows(j % 2, h), NT, preferred_element_type=WIDE)
+            grad = (grad * pool[PAIR + j % 2, :, half_cols(h)].astype(WIDE)).astype(LOW)
+            for n in range(4):
+                f = 4 * h + n
+                place = pl.ds(pl.multiple_of((f % 2 * 4 + j) * 128, 128), 128)
+                pool[GRAD_UP + f // 2, :, place] = grad[:, n * 128 : (n + 1) * 128]
+
+        pl.when(j < 2)(lambda: fetch_w(11 + j, j % 2).start())
+        pl.when(j >= 2)(lambda: fetch_w(3 + j, j % 2).start())
+        pl.when(j < 2)(lambda: fetch_pair(slope_h, j + 2).start())
+
+        @when(j == 0)
+        def _():
+            feed(2)
+            load(3)
+
+        when(j == 1)(lambda: feed(3))
+        run(1 + j, 2 + j)
+
+    for_each(4, activ_back)
+
     def up(j):
-        fetch_pair(slope_h, j).wait()
-        fetch_w(9 + j, 0).wait()
+        column_sums(GRAD_UP + j, BIAS_U + j)
+        produce(4 + j, pool.at[NORMED2], times(GRAD_UP + j))
+        fetch_w(5 + j, j % 2).wait()
+        when(j >= 1)(lambda: feed(3 + j))
+        run(5 + j, 6 + j)
         for h in range(2):
-            grad = lax.dot_general(pool[COT], half_rows(0, h), NT, preferred_element_type=WIDE)
-            grad = grad * pool[PAIR + j % 2, :, half_cols(h)].astype(WIDE)
-            pool[GRAD_UP, :, half_cols(h)] = grad.astype(LOW)
-
-        @pl.when(j < 3)
-        def _():
-            fetch_w(10 + j, 0).start()
-
-        pl.when(j < 2)(lambda: fetch_pair(slope_h, j + 2).start())
-        feed(2 + j)
-        run(1 + 2 * j, 2 + 2 * j)
-        column_sums(GRAD_UP, BIAS_U + j)
-        produce(4 + j, pool.at[NORMED2], times(GRAD_UP))
-        fetch_w(5 + j, 1).wait()
-        for h in range(2):
-            more = lax.dot_general(pool[GRAD_UP], half_rows(1, h), NT, preferred_element_type=WIDE)
+            more = lax.dot_general(pool[GRAD_UP + j], half_rows(j % 2, h), NT, preferred_element_type=WIDE)
 
             @pl.when(j == 0)
             def _():
@@ -824,17 +920,14 @@
             def _():
                 gn[:, half_cols(h)] = gn[:, half_cols(h)] + more
 
-        @pl.when(j < 3)
-        def _():
-            fetch_w(6 + j, 1).start()
-
-        load(3 + j)
-        run(2 + 2 * j, 3 + 2 * j)
+        pl.when(j < 2)(lambda: fetch_w(7 + j, j % 2).start())
+        load(4 + j)
 
     for_each(4, up)
     fetch_w(4, 0).start()
     fetch_w(1, 1).start()
-    fetch(ctx_h, CONTEXT).start()
+    for src, i in ((ctx_h, CONTEXT), (q_h, QUERY), (k_h, KEY), (v_h, VALUE)):
+        fetch(src, i).start()
 
     sums[...] = jnp.zeros_like(sums)
 
@@ -864,8 +957,7 @@
         pool[GRAD_BRANCH, rows, :] = total.astype(LOW)
 
     norm_back(1, GAIN2, lambda rows: mid[rows, :], done2)
-    feed(6)
-    load(7)
+    feed(7)
     run(9, 10)
 
     fetch(ctx_h, CONTEXT).wait()
@@ -876,12 +968,12 @@
         grad = lax.dot_general(pool[GRAD_BRANCH], half_rows(0, h), NT, preferred_element_type=WIDE)
         pool[GRAD_CONTEXT, :, half_cols(h)] = grad.astype(LOW)
     fetch_w(2, 0).start()
-    feed(7)
     load(8)
     run(10, 11)
 
     for src, i in ((q_h, QUERY), (k_h, KEY), (v_h, VALUE), (tokens_h, TOKENS)):
         fetch(src, i).wait()
+
     modulated(pool.at[TOKENS], pool.at[NORMED1], table, mods, GAIN1, 0, seqs)
     feed(8)
 
@@ -998,8 +1090,12 @@
     vmem, hbm = pl.BlockSpec(memory_space=pltpu.VMEM), pl.BlockSpec(memory_space=pl.ANY)
     q, k, v, ctx, mid, normed2, activ, slope = saved
     block = (4, 2, 2, 2, 32, width) if comm else (width, width)
-    outs = [
-        (jax.ShapeDtypeStruct((BLOCKS, 2, 2, 2, 16, width) if comm else (BLOCKS, width, width), WIDE if comm else LOW), hbm),
+    rows = width // 8
+    if comm:
+        shapes = [(rows, 3 * width), (rows, width), (rows, 4 * width), (4 * rows, width), (TE // 8, 2 * width), (TE // 8, 2 * width)]
+    else:
+        shapes = [(BLOCKS, width, width)]
+    outs = [(jax.ShapeDtypeStruct(shape, LOW), hbm) for shape in shapes] + [
         (jax.ShapeDtypeStruct((16, 128) if comm else (16, width), WIDE), vmem),
         (jax.ShapeDtypeStruct((n, width), WIDE), hbm),
     ]
@@ -1040,7 +1136,7 @@
         ),
         name="backward",
     )(full, cot, activ, slope, normed2, mid, q, k, v, ctx, tokens, table, mods, feat, cosine, sine)
-    return got[0], got[1], got[2]
+    return got[: len(shapes) + 2]
 
 
 def rotary_constants(length, head_dim):
@@ -1052,36 +1148,65 @@
     return tuple(np.concatenate([t, t], axis=1).astype(np.float32) for t in pair)
 
 
-def wide_features(noise_times, shards_of, width):
-    each = TE // shards_of
+def wide_features(noise_times, width):
+    seqs = noise_times.shape[0]
     half_width = TE // 2
     column = np.arange(width)
-    feature = column // (4 * each) * each + column % each
-    part = column // each % 4
+    feature = column // 128 * 32 + column % 32
     rates = np.exp((feature % half_width).astype(np.float32) * np.float32(math.log(100.0) / half_width))
-    phases = (jnp.log(noise_times) * 0.25)[:, None] * rates[None, :]
+    row = np.arange(-(-4 * seqs // 32) * 32)
+    times = jnp.ones(row.shape, WIDE)
+    for s in range(seqs):
+        times = jnp.where(row % seqs == s, noise_times[s], times)
+    phases = (jnp.log(times) * 0.25)[:, None] * rates[None, :]
     feat = jnp.where((feature < half_width)[None, :], jnp.sin(phases), jnp.cos(phases))
-    chosen = (part[None, :] == np.arange(4)[:, None])[:, None, :]
-    feat = jnp.where(chosen, feat[None], 0.0).reshape(-1, width).astype(LOW)
-    pad = -feat.shape[0] % 32
-    return jnp.pad(feat, ((0, pad), (0, 0)))
-
-
-def pack_local(weights):
+    return jnp.where((column // 32 % 4)[None, :] == (row // seqs)[:, None], feat, 0.0).astype(LOW)
+
+
+def gather_plain(weights, vectors):
     project, output, up, down, time1, time2 = weights
     rows, width = output.shape
-    shards_of = width // rows
-    up_blocks = up.reshape(rows, shards_of, 4, rows).transpose(2, 0, 1, 3).reshape(4, rows, width)
-    times = jnp.stack([time1, time2]).reshape(2, -1, 2, width).transpose(0, 2, 1, 3)
-    return jnp.concatenate(
+    each = time1.shape[0]
+    columns = lambda w: w.reshape(rows, -1, width).transpose(1, 0, 2)
+    times = jnp.stack([time1, time2]).reshape(2, each, 2, width).transpose(0, 2, 1, 3)
+    own = jnp.concatenate(
+        [times.reshape(1, rows, width), columns(project), output[None], columns(up), down.reshape(4, rows, width)]
+    )
+    full = lax.all_gather(own, "fsdp", axis=1, tiled=True)
+    times = full[0].reshape(-1, 2, 2, each, width).transpose(1, 2, 0, 3, 4).reshape(2, 2, 8, 32, width)
+    down = full[9:].reshape(4, -1, rows, width).transpose(1, 0, 2, 3).reshape(8, 4, 128, width)
+    full = jnp.concatenate(
         [
-            times.reshape(1, rows, width),
-            project.reshape(rows, 3, width).transpose(1, 0, 2),
-            output[None],
-            up_blocks,
-            down.reshape(4, rows, width),
+            times.transpose(2, 0, 1, 3, 4).reshape(1, width, width),
+            full[1:9],
+            down.transpose(1, 0, 2, 3).reshape(4, width, width),
         ]
     )
+    sizes = [v.shape[0] for v in vectors]
+    whole = pieces_of(lax.all_gather(jnp.concatenate(vectors), "fsdp", axis=0), sizes)
+    table = jnp.concatenate([w.reshape(-1, width) for w in whole]).astype(WIDE)
+    return full, jnp.pad(table, ((0, 3), (0, 0)))
+
+
+def reduce_plain(parts, table, sizes, shards_of):
+    width = parts.shape[-1]
+    rows, each = width // shards_of, TE // shards_of
+    down = parts[:4].reshape(4, 8, 128, width).transpose(1, 0, 2, 3).reshape(shards_of, 4, rows, width)
+    times = parts[12].reshape(8, 2, 2, 32, width).transpose(1, 2, 0, 3, 4).reshape(2, 2, shards_of, each, width)
+    own = jnp.concatenate(
+        [
+            down.transpose(1, 0, 2, 3).reshape(4, width, width),
+            parts[4:12],
+            times.transpose(2, 0, 1, 3, 4).reshape(1, width, width),
+        ]
+    )
+    mine = lax.psum(lax.psum_scatter(own, "fsdp", scatter_dimension=1, tiled=True), "rep")
+    whole = pieces_of(table[:13].reshape(-1), [shards_of * size for size in sizes])
+    vec = jnp.concatenate([w.reshape(shards_of, -1) for w in whole], axis=1)
+    vec = lax.psum(lax.psum_scatter(vec, "fsdp", scatter_dimension=0, tiled=True)[0], "rep")
+    columns = lambda w: w.transpose(1, 0, 2).reshape(rows, -1)
+    times = mine[12].reshape(2, 2, each, width).transpose(0, 2, 1, 3).reshape(2, each, 2 * width)
+    return columns(mine[9:12]), mine[8], columns(mine[4:8]), mine[:4].reshape(-1, width), times[0], times[1], vec
 
 
 def pieces_of(flat, sizes):
@@ -1116,55 +1241,42 @@
     rows = output_weight.shape[0]
     shards_of = width // rows
     comm = shards_of == 8
-    feat = wide_features(noise_times, shards_of, width)
+    feat = wide_features(noise_times, width)
     cosine, sine = rotary_constants(tokens_n // seqs, width // HEADS)
-    own = pack_local((project_weight, output_weight, up_weight, down_weight, norm1_time, norm2_time))
+    weights = (project_weight, output_weight, up_weight, down_weight, norm1_time, norm2_time)
     vectors = (norm1_gain, norm1_bias, project_bias, output_bias, norm2_gain, norm2_bias, up_bias, down_bias)
     sizes = [v.shape[0] for v in vectors]
-    vec = jnp.concatenate(vectors)
     if comm:
-        first, second = own, jnp.pad(vec.reshape(13, 128), ((0, 3), (0, 0)))
+        at, table = 0, jnp.zeros((16, 128), WIDE)
+        for v in vectors:
+            lines = v.astype(WIDE).reshape(-1, 128)
+            table = table + jnp.pad(lines, ((at, 16 - at - lines.shape[0]), (0, 0)))
+            at += lines.shape[0]
     else:
-        first = lax.all_gather(own, "fsdp", axis=1, tiled=True)
-        whole = pieces_of(lax.all_gather(vec, "fsdp", axis=0), sizes)
-        whole[6] = whole[6].reshape(shards_of, 4, rows).transpose(1, 0, 2)
-        second = jnp.concatenate([w.reshape(-1, width) for w in whole]).astype(WIDE)
-        second = jnp.pad(second, ((0, 3), (0, 0)))
-    full, table, mods, layer_out, *saved = forward_call(comm, first, second, inputs, feat, cosine, sine, seqs)
-    mine, mine_vec, input_grad = backward_call(
-        comm, full, cotangent, saved, inputs, table, mods, feat, cosine, sine, seqs
-    )
-    if comm:
-        mine = mine.reshape(BLOCKS, rows, width)
-        mine_vec = mine_vec.reshape(-1)
-    else:
-        mine = lax.psum_scatter(mine, "fsdp", scatter_dimension=1, tiled=True)
-        mine = lax.psum(mine, "rep").astype(WIDE)
-        whole = pieces_of(mine_vec[:13].reshape(-1), [shards_of * size for size in sizes])
-        whole[6] = whole[6].reshape(4, shards_of, rows).transpose(1, 0, 2)
-        mine_vec = jnp.concatenate([w.reshape(shards_of, -1) for w in whole], axis=1)
-        mine_vec = lax.psum(lax.psum_scatter(mine_vec, "fsdp", scatter_dimension=0, tiled=True)[0], "rep")
-    got = pieces_of(mine_vec, sizes)
-    my_down = mine[0:4].reshape(4 * rows, width)
-    my_up = mine[4:8].reshape(4, rows, shards_of, rows).transpose(1, 2, 0, 3).reshape(rows, 4 * width)
-    my_project = mine[9:12].transpose(1, 0, 2).reshape(rows, 3 * width)
-    my_times = mine[12].reshape(2, 2, -1, width).transpose(0, 2, 1, 3).reshape(2, -1, 2 * width)
+        full, table = gather_plain(weights, vectors)
+        weights = (full,)
+    full, table, mods, layer_out, *saved = forward_call(comm, weights, table, inputs, feat, cosine, sine, seqs)
+    *sums, input_grad = backward_call(comm, full, cotangent, saved, inputs, table, mods, feat, cosine, sine, seqs)
+    if not comm:
+        sums = reduce_plain(*sums, sizes, shards_of)
+    project, output, up, down, time1, time2 = [s.astype(WIDE) for s in sums[:6]]
+    got = pieces_of(sums[6].reshape(-1), sizes)
     return (
         layer_out,
         input_grad,
         got[0],
         got[1],
-        my_times[0],
-        my_project,
+        time1,
+        project,
         got[2],
-        mine[8],
+        output,
         got[3],
         got[4],
         got[5],
-        my_times[1],
-        my_up,
+        time2,
+        up,
         got[6],
-        my_down,
+        down,
         got[7],
     )
 

time: 456 us -> 363 us (0.80); the launches traced: 447 us -> 362 us
  Pallas kernels: 402 us -> 333 us
  local copies, waits for them, and re-layouts: 41.3 us -> 9.96 us
  other arithmetic: 3.09 us -> 18.5 us
    pallas_call x1, Pallas kernels: 189 us -> 142 us  [forward_call(): pl.pallas_call(functools.partial(forward_kernel, comm, seqs), out_shape=t...]
    pallas_call x1, Pallas kernels: 213 us -> 191 us  [backward_call(): pl.pallas_call(functools.partial(backward_kernel, comm, seqs), out_shape=...]
    unnamed x29 -> x10, local copies, waits for them, and re-layouts: 18 us -> 4.49 us
    convert_element_type x1 -> x7, other arithmetic: 0.71 us -> 12.5 us  [the longest x6 10.6 us: shards(): project, output, up, down, time1, time2 = [s.astype(WIDE) for s in sums[:6]]]
    slice x7 -> x1, local copies, waits for them, and re-layouts: 9.18 us -> 1.48 us  [wide_features(): times = jnp.where(row % seqs == s, noise_times[s], times)]
where the time goes in v3:
time: 363 us; the launch traced here: 362 us
  Pallas kernels  333 us (92%)
  other arithmetic  18.5 us (5%)
  local copies, waits for them, and re-layouts  9.96 us (3%)
    pallas_call x1, Pallas kernels, backward_call(): pl.pallas_call(functools.partial(backward_kernel, comm, seqs), out_shape=...  191 us
    pallas_call x1, Pallas kernels, forward_call(): pl.pallas_call(functools.partial(forward_kernel, comm, seqs), out_shape=t...  142 us
    convert_element_type x6, other arithmetic, shards(): project, output, up, down, time1, time2 = [s.astype(WIDE) for s in sums[:6]]  10.6 us

profile of v3, /device:TPU:0, one launch (start us, length us, event | category | flops | bytes accessed | tf_op | source)
XLA Modules:
  0.0 362.3 jit_solution(7902670071880150064)
XLA Ops:
  0.6 1.5 fusion.3
  2.1 4.6 %log_multiply_fusion = f32[32]{0:T(128)S(1)} fusion(pred[32]{0:T(512)(128)(4,1)} %constant.37.clone, pred[32]{0:T(512)(128)(4,1)} %constant.36.clone, pred[32]{0:T(512)(128)(4,1)} %constant.35.clone, pred[32]{0:T(512)(128)(4,1)} %constant.34.clone, pred[32]{0:T(512)(128)(4,1)} %constant.33.clone, pred[32]{0:T(512)(128)(4,1)} %constant.32.clone, f32[]{:T(128)} %bitcast.13, ...), kind=kLoop, calls=%fused_computation.14 | loop fusion | flops 224 | bytes 344 | tf_op jit(solution)/shard_map/mul | solution.py:1161
  6.8 1.4 convert_add_fusion.refs_6_
  8.1 2.0 fusion.2.refs_8_.refs_13_
  10.1 142.3 %forward.1 = (bf16[13,4,2,2,2,32,1024]{6,5,4,3,2,1,0:T(8,128)(2,1)}, f32[16,1024]{1,0:T(8,128)}, f32[32,1024]{1,0:T(8,128)}, bf16[768,1024]{1,0:T(8,128)(2,1)}, ...) custom-call(bf16[128,3072]{1,0:T(8,128)(2,1)} %refs_0_.1, ...), custom_call_target="tpu_custom_call" | custom-call | tf_op jit(solution)/shard_map/forward/pallas_call | solution.py:496
  152.4 190.9 %backward.1 = (bf16[128,3072]{1,0:T(8,128)(2,1)}, bf16[128,1024]{1,0:T(8,128)(2,1)}, bf16[128,4096]{1,0:T(8,128)(2,1)}, bf16[512,1024]{1,0:T(8,128)(2,1)}, bf16[...) custom-call(bf16[13,4,2,2,2,32,1024]{6,5,4,3,2,1,0:T(8,128)(2,1)} %g, ...), custom_call_target="tpu_custom_call" | custom-call | tf_op jit(solution)/shard_map/backward/pallas_call | solution.py:1114
  343.3 0.0 copy-start.3
  343.3 1.3 slice_bitcast_fusion.1
  344.6 1.3 slice_bitcast_fusion
  345.9 1.4 slice_bitcast_fusion.2
  347.3 1.6 convert_element_type.46
  348.9 1.6 convert_element_type.49
  350.5 1.8 convert_element_type.48
  352.3 2.4 convert_element_type.47
  354.7 0.0 copy-done.3
  354.8 0.0 copy-start.2
  354.8 1.5 convert_element_type.50
  356.3 0.0 copy-done.2
  356.3 0.0 copy-start.1
  356.3 1.6 convert_element_type.51
  357.9 0.4 copy-done.1
  358.2 0.0 copy-start
  358.2 1.1 copy.47
  359.4 1.3 copy-done
  360.7 1.7 copy.48
Async XLA Ops:
  343.3 11.5 %copy-start.3 = (bf16[128,4096]{1,0:T(8,128)(2,1)S(1)}, bf16[128,4096]{1,0:T(8,128)(2,1)}, u32[]{:S(2)}) copy-start(bf16[128,4096]{1,0:T(8,128)(2,1)} %get-tuple-element.54) | copy-start | bytes 3145732
  354.8 1.5 copy-start.2
  356.3 1.9 copy-start.1
  358.2 2.5 copy-start

commit v4 on v3

--- a/solution.py
+++ b/solution.py
@@ -148,7 +148,7 @@
         for i, peer in enumerate(at.group):
             remote(self.vec, self.vecs.at[at.shards[i]], self.vsend.at[i], self.vrecv.at[i], peer).wait()
 
-    lag_x, lag_core, lag_done = 2, 4, 5
+    lag_x, lag_core, lag_done = 3, 6, 7
 
     def step(self, t):
         lag_x, lag_core, lag_done = self.lag_x, self.lag_core, self.lag_done
@@ -296,20 +296,22 @@
         local, vec = take(6), take(1)[0]
     else:
         full_in, table_in = take(2)
-    tokens_hbm, feat, cosine, sine = take(4)
+    tokens_hbm, cot_hbm, feat, cosine, sine = take(5)
     if comm:
         (full,) = take(1)
     else:
         full = full_in
     table, mods = take(2)
-    out_o, q_o, k_o, v_o, ctx_o, mid_o, normed2_o, activ_o, slope_o = take(9)
-    tokens, weights, normed, q, k, v, ctx, mid, acc, activ, slope, wide, out_low = take(13)
-    sem_in, sem_w, sem_out = take(3)
+    out_o, grad_o, q_o, k_o, v_o, ctx_o, mid_o, normed1_o, normed2_o, slope_o, probs_o = take(11)
+    tokens, cot, weights, normed, normed2, q, k, v, ctx, mid, acc, activ, slope, wide, out_low, probs, grads = take(17)
+    sem_in, sem_w, sem_out, sem_grad = take(4)
     tokens_n = tokens.shape[0]
     per = tokens_n // seqs
 
-    tokens_in = pltpu.make_async_copy(tokens_hbm, tokens, sem_in)
+    tokens_in = pltpu.make_async_copy(tokens_hbm, tokens, sem_in.at[0])
     tokens_in.start()
+    cot_in = pltpu.make_async_copy(cot_hbm, cot, sem_in.at[1])
+    cot_in.start()
     if comm:
         own, sem_own = take(2)
         gather = Gather(own, vec, full, *refs)
@@ -358,6 +360,7 @@
     tokens_in.wait()
     arrive(1, ready, ready + 2)
     modulated(tokens, normed, table, mods, GAIN1, 0, seqs)
+    save(normed, normed1_o)
 
     for j, (dst, dst_o) in enumerate([(q, q_o), (k, k_o), (v, v_o)]):
         w = weight(1 + j)
@@ -399,14 +402,16 @@
             both = jnp.concatenate([qs * first_head.astype(LOW), qs * second_head.astype(LOW)], axis=0)
             scores = lax.dot_general(both, k[rows, cols], NT, preferred_element_type=WIDE)
             grown = jnp.exp(scores - jnp.max(scores, axis=-1, keepdims=True))
-            probs = (grown / jnp.sum(grown, axis=-1, keepdims=True)).astype(LOW)
-            mixed = jnp.dot(probs, v[rows, cols], preferred_element_type=WIDE)
+            share = (grown / jnp.sum(grown, axis=-1, keepdims=True)).astype(LOW)
+            probs[n, 2 * s * per : 2 * (s + 1) * per, :] = share
+            mixed = jnp.dot(share, v[rows, cols], preferred_element_type=WIDE)
             ctx[rows, cols] = (mixed[:per] * first_head + mixed[per:] * second_head).astype(LOW)
         if comm:
             pl.when(n >= 2)(lambda: gather.step(ready + 6 + n))
 
     for_each(8, heads)
     save(ctx, ctx_o)
+    save(probs, probs_o)
 
     w = weight(4)
     for h in range(2):
@@ -415,14 +420,14 @@
         mid[:, cols] = tokens[:, cols].astype(WIDE) + (dot + table[BIAS_O : BIAS_O + 1, cols])
     arrive(5, ready + 14, ready + 15)
     save(mid, mid_o)
-    modulated(mid, normed, table, mods, GAIN2, 1, seqs)
-    save(normed, normed2_o)
+    modulated(mid, normed2, table, mods, GAIN2, 1, seqs)
+    save(normed2, normed2_o)
 
     def up(j):
         w = weight(5 + j)
         for h in range(2):
             cols = slice(h * HALF, (h + 1) * HALF)
-            wide[...] = jnp.dot(normed[...], half_of(w, cols, comm), preferred_element_type=WIDE)
+            wide[...] = jnp.dot(normed2[...], half_of(w, cols, comm), preferred_element_type=WIDE)
             if h == 0:
                 once = ready + 15 + 2 * j - jnp.maximum(j - 2, 0)
                 run(once, once + 1)
@@ -444,10 +449,23 @@
             for_each(tokens_n // TILE, body)
 
     for_each(4, up)
-    save(activ, activ_o)
     save(slope, slope_o)
 
+    cot_in.wait()
+
+    def grad_copy(j):
+        return pltpu.make_async_copy(grads.at[j % 2], grad_o.at[j], sem_grad.at[j % 2])
+
     def down(j):
+        pl.when(j >= 2)(lambda: grad_copy(j - 2).wait())
+        for h in range(2):
+            cols = slice(h * HALF, (h + 1) * HALF)
+            block = lax.dot_general(activ[j], cot[:, cols], TN, preferred_element_type=WIDE).astype(LOW)
+            if comm:
+                grads[j % 2, :, :, :, :, :, cols] = block.reshape(4, 2, 2, 2, 32, HALF)
+            else:
+                grads[j % 2, :, cols] = block
+        grad_copy(j).start()
         w = weight(9 + j)
         for h in range(2):
             cols = slice(h * HALF, (h + 1) * HALF)
@@ -467,6 +485,8 @@
     for_each(4, down)
     out_low[...] = acc[...].astype(LOW)
     save(out_low, out_o)
+    grad_copy(2).wait()
+    grad_copy(3).wait()
     for copy in saves:
         copy.wait()
 
@@ -477,7 +497,7 @@
     return w[:, cols]
 
 
-def forward_call(comm, weights, vectors, tokens, feat, cosine, sine, seqs):
+def forward_call(comm, weights, vectors, tokens, cot, feat, cosine, sine, seqs):
     n, width = tokens.shape
     vmem, hbm = pl.BlockSpec(memory_space=pltpu.VMEM), pl.BlockSpec(memory_space=pl.ANY)
     low = jax.ShapeDtypeStruct((n, width), LOW)
@@ -487,7 +507,10 @@
     outs = [
         (jax.ShapeDtypeStruct((16, width), WIDE), vmem),
         (jax.ShapeDtypeStruct((feat.shape[0], width), WIDE), vmem),
-    ] + [(s, hbm) for s in (low, low, low, low, low, wide, low, shape4, shape4)]
+    ]
+    share = (8, 2 * n, 128)
+    saved = (jax.ShapeDtypeStruct((4,) + block, LOW), low, low, low, low, wide, low, low, shape4)
+    outs += [(s, hbm) for s in (low,) + saved + (jax.ShapeDtypeStruct(share, LOW),)]
     extra = []
     if comm:
         outs = [(jax.ShapeDtypeStruct((BLOCKS,) + block, LOW), hbm)] + outs
@@ -496,11 +519,13 @@
     got = pl.pallas_call(
         functools.partial(forward_kernel, comm, seqs),
         out_shape=tuple(s for s, _ in outs),
-        in_specs=[hbm] * len(weights) + [vmem, hbm, vmem, vmem, vmem],
+        in_specs=[hbm] * len(weights) + [vmem, hbm, hbm, vmem, vmem, vmem],
         out_specs=tuple(m for _, m in outs),
         scratch_shapes=[
             buffer,
+            buffer,
             pltpu.VMEM((2,) + block, LOW),
+            buffer,
             buffer,
             buffer,
             buffer,
@@ -512,28 +537,32 @@
             pltpu.VMEM((4, n, width), LOW),
             pltpu.VMEM((n, HALF), WIDE),
             buffer,
-            pltpu.SemaphoreType.DMA,
+            pltpu.VMEM(share, LOW),
+            pltpu.VMEM((2,) + block, LOW),
             pltpu.SemaphoreType.DMA((2,)),
-            pltpu.SemaphoreType.DMA((9,)),
+            pltpu.SemaphoreType.DMA((2,)),
+            pltpu.SemaphoreType.DMA((10,)),
+            pltpu.SemaphoreType.DMA((2,)),
         ]
         + extra,
         compiler_params=pltpu.CompilerParams(
             collective_id=0 if comm else None, has_side_effects=comm, vmem_limit_bytes=60 * 2**20
         ),
         name="forward",
-    )(*weights, vectors, tokens, feat, cosine, sine)
+    )(*weights, vectors, tokens, cot, feat, cosine, sine)
     if not comm:
         return (weights[0], vectors) + tuple(got[1:])
     return (got[0].reshape(BLOCKS, width, width),) + tuple(got[1:])
 
 
 RING = 10
+READY = 4
 
 
 class Reduce:
-    def __init__(self, slots, own, l0, outs, *scratch):
+    def __init__(self, ready, slots, own, l0, outs, *scratch):
         self.at = Place()
-        self.slots, self.own, self.l0, self.outs = slots, own, l0, outs
+        self.ready, self.slots, self.own, self.l0, self.outs = ready, slots, own, l0, outs
         (self.held, self.s0, self.l1a, self.l1b, self.l2, self.l3, self.la) = scratch[:7]
         (self.bsend, self.brecv, self.lsem, self.send, self.recv, self.osem) = scratch[7:13]
         x = self.at.x
@@ -544,43 +573,50 @@
     def begin(self):
         at = self.at
         greet([at.across_core, at.across_x, at.diagonal] + at.group)
+        for b in range(READY):
+            src = self.ready.at[b, :, :, 1 - at.core]
+            remote(src, self.l0.at[b], self.bsend.at[b], self.brecv.at[b], at.across_core).start()
 
     def core_copy(self, b):
         src = self.slots.at[b % 2, :, :, 1 - self.at.core]
         return remote(src, self.l0.at[b], self.bsend.at[b], self.brecv.at[b], self.at.across_core)
 
     def own_copy(self, b):
-        return pltpu.make_async_copy(self.slots.at[b % 2, :, :, self.at.core], self.own.at[b], self.lsem.at[b % 2])
-
-    def loads(self, b):
+        return pltpu.make_async_copy(self.slots.at[b % 2, :, :, self.at.core], self.own.at[b - READY], self.lsem.at[b % 2])
+
+    def loads(self, b, ready=False):
+        src = self.ready.at[b, :, :, self.at.core] if ready else self.own.at[b - READY]
         return (
-            pltpu.make_async_copy(self.own.at[b], self.held.at[0], self.lsem.at[2]),
+            pltpu.make_async_copy(src, self.held.at[0], self.lsem.at[2]),
             pltpu.make_async_copy(self.l0.at[b], self.held.at[1], self.lsem.at[3]),
         )
 
     def free(self, b):
-        pl.when(b >= 2)(lambda: self.core_copy(b - 2).wait_send())
+        self.core_copy(b - 2).wait_send()
 
     def produced(self, b):
         self.core_copy(b).start()
         self.own_copy(b).start()
 
     def load(self, b):
+        self.core_copy(b).wait_recv()
+        if isinstance(b, int) and b < READY:
+            for copy in self.loads(b, True):
+                copy.start()
+            return
         self.own_copy(b).wait()
-        self.core_copy(b).wait_recv()
         for copy in self.loads(b):
             copy.start()
 
     def feed(self, b):
-        for copy in self.loads(b):
+        for copy in self.loads(READY):
             copy.wait()
 
-        def add(i):
-            z, y, h = i // 4, (i // 2) % 2, i % 2
-            piece = self.held[0, z, y, h].astype(WIDE) + self.held[1, z, y, h].astype(WIDE)
-            self.s0[(2 * b + h) % RING, z, y] = piece.astype(LOW)
-
-        for_each(16, add)
+        def add(z):
+            for h in range(2):
+                self.s0[(2 * b + h) % RING, z] = self.held[0, z, :, h] + self.held[1, z, :, h]
+
+        for_each(4, add)
         for h in range(2):
             self.x_one(2 * b + h).start()
             self.y_one(2 * b + h).start()
@@ -633,7 +669,7 @@
         pl.when(jnp.logical_and(b >= 9, b < 12))(lambda: self.store(p, [project.at[rows(c), cols(b - 9)] for c in range(2)]))
         pl.when(b == 12)(lambda: self.store(p, [t.at[:, cols(h)] for t in times]))
 
-    lags = (2, 3, 5, 6)
+    lags = (4, 6, 10, 11)
 
     def drain(self, d):
         at, lags = self.at, self.lags
@@ -643,20 +679,10 @@
             p = d
             self.x_one(p).wait()
 
-            def add(i):
-                z, y = i // 2, i % 2
-                more = self.s0[p % RING, z, y, self.mine, self.front].astype(WIDE)
-                self.l1a[p, z, y] = (self.l1a[p, z, y].astype(WIDE) + more).astype(LOW)
-
-            for_each(8, add)
+            self.l1a[p] = self.l1a[p] + self.s0[p % RING, :, :, self.mine, self.front]
             self.y_two(p).start()
             self.y_one(p).wait()
-
-            def add_too(z):
-                more = self.s0[p % RING, z, at.y, :, self.back].astype(WIDE)
-                self.l1b[p, z] = (self.l1b[p, z].astype(WIDE) + more).astype(LOW)
-
-            for_each(4, add_too)
+            self.l1b[p] = self.l1b[p] + self.s0[p % RING, :, at.y, :, self.back]
             self.x_two(p).start()
 
         @pl.when(jnp.logical_and(d >= lags[0], d < PIECES + lags[0]))
@@ -665,13 +691,8 @@
             self.y_two(p).wait()
             self.x_two(p).wait()
 
-            def add(z):
-                one = self.l2[p, z, :, self.front].astype(WIDE) + self.l1a[p, z, at.y].astype(WIDE)
-                two = self.l2[p, z, :, self.back].astype(WIDE) + self.l1b[p, z, self.mine].astype(WIDE)
-                self.l2[p, z, :, self.front] = one.astype(LOW)
-                self.l2[p, z, :, self.back] = two.astype(LOW)
-
-            for_each(4, add)
+            self.l2[p, :, :, self.front] = self.l2[p, :, :, self.front] + self.l1a[p, :, at.y]
+            self.l2[p, :, :, self.back] = self.l2[p, :, :, self.back] + self.l1b[p, :, self.mine]
             for k in range(1, 4):
                 self.z_copy(p, k).start()
 
@@ -710,6 +731,8 @@
         lax.fori_loop(lo, hi, one, 0)
 
     def end(self):
+        for b in range(READY - 2):
+            self.core_copy(b).wait_send()
         self.core_copy(BLOCKS - 2).wait_send()
         self.core_copy(BLOCKS - 1).wait_send()
 
@@ -770,13 +793,13 @@
 
 
 COT, NORMED2, PAIR, GRAD_UP, TOKENS, NORMED1 = 0, 1, 2, 4, 8, 9
-GRAD_BRANCH, CONTEXT, QUERY, KEY, VALUE, GRAD_CONTEXT = 2, 3, 4, 5, 6, 7
+QUERY, KEY, VALUE, GRAD_CONTEXT, GRAD_BRANCH, CONTEXT = 2, 3, 4, 5, 10, 11
 
 
 def backward_kernel(comm, seqs, *refs):
     refs = list(refs)
     take = lambda n: [refs.pop(0) for _ in range(n)]
-    full, cot_h, activ_h, slope_h, normed2_h, mid_h, q_h, k_h, v_h, ctx_h, tokens_h = take(11)
+    full, cot_h, slope_h, normed1_h, normed2_h, mid_h, q_h, k_h, v_h, ctx_h, probs_h, tokens_h, ready = take(13)
     table, mods, feat, cosine, sine = take(5)
     outs = take(6 if comm else 1)
     vec_out, input_o = take(2)
@@ -784,31 +807,35 @@
         own, l0 = take(2)
     else:
         (out,) = outs
-    pool, gn, mid, weights, slots, sums, gtab, sem_in, sem_pair, sem_w, sem_mid, sem_slot = take(12)
+    pool, gn, mid, weights, slots, shares, sums, gtab, sem_in, sem_pair, sem_w, sem_mid, sem_slot, sem_share = take(14)
     if comm:
         parts, vgot, vsums, vsend, vrecv = take(5)
-        red = Reduce(slots, own, l0, outs, *refs)
+        red = Reduce(ready, slots, own, l0, outs, *refs)
     tokens_n = pool.shape[1]
     per = tokens_n // seqs
 
     def fetch(src, i):
         return pltpu.make_async_copy(src, pool.at[i], sem_in.at[i])
 
-    def fetch_pair(src, j):
-        return pltpu.make_async_copy(src.at[j], pool.at[PAIR + j % 2], sem_pair.at[j % 2])
+    def fetch_slope(j):
+        return pltpu.make_async_copy(slope_h.at[j], pool.at[PAIR + j % 2], sem_pair.at[j % 2])
+
+    def fetch_share(n):
+        return pltpu.make_async_copy(probs_h.at[n], shares.at[n % 2], sem_share.at[n % 2])
 
     def fetch_w(c, slot):
         return pltpu.make_async_copy(full.at[c], weights.at[slot], sem_w.at[slot])
 
     mid_in = pltpu.make_async_copy(mid_h, mid, sem_mid)
     fetch(cot_h, COT).start()
-    fetch_pair(activ_h, 0).start()
-    fetch_pair(activ_h, 1).start()
+    fetch_slope(0).start()
+    fetch_slope(1).start()
     fetch(normed2_h, NORMED2).start()
     fetch_w(9, 0).start()
     fetch_w(10, 1).start()
     mid_in.start()
-    fetch(tokens_h, TOKENS).start()
+    for src, i in ((tokens_h, TOKENS), (normed1_h, NORMED1), (ctx_h, CONTEXT)):
+        fetch(src, i).start()
     if comm:
         red.begin()
         run, load, feed = red.run, red.load, red.feed
@@ -827,7 +854,9 @@
         if comm:
             red.free(b)
         else:
-            pl.when(b >= 2)(lambda: pltpu.make_async_copy(slots.at[b % 2], out.at[b - 2], sem_slot.at[b % 2]).wait())
+            pl.when(b >= READY + 2)(
+                lambda: pltpu.make_async_copy(slots.at[b % 2], out.at[b - READY - 2], sem_slot.at[b % 2]).wait()
+            )
         for h in range(2):
             block = rhs_of(lhs, h).astype(LOW)
             if comm:
@@ -837,7 +866,7 @@
         if comm:
             red.produced(b)
         else:
-            pltpu.make_async_copy(slots.at[b % 2], out.at[b], sem_slot.at[b % 2]).start()
+            pltpu.make_async_copy(slots.at[b % 2], out.at[b - READY], sem_slot.at[b % 2]).start()
 
     def times(i):
         return lambda lhs, h: lax.dot_general(lhs[...], pool[i, :, half_cols(h)], TN, preferred_element_type=WIDE)
@@ -847,39 +876,16 @@
     def column_sums(i, row):
         gtab[pl.ds(row, 1), :] = jnp.dot(ones, pool[i], preferred_element_type=WIDE)[:1]
 
+    def up(j):
+        produce(4 + j, pool.at[NORMED2], times(GRAD_UP + j))
+
     fetch(cot_h, COT).wait()
-
-    def down(j):
-        fetch_pair(activ_h, j).wait()
-        produce(j, pool.at[PAIR + j % 2], times(COT))
-
-        @pl.when(j < 2)
-        def _():
-            fetch_pair(activ_h, j + 2).start()
-
-        @pl.when(j >= 2)
-        def _():
-            fetch_pair(slope_h, j - 2).start()
-
-        @when(j == 0)
-        def _():
-            load(0)
-            feed(0)
-
-        when(j == 2)(lambda: load(1))
-
-        @when(j == 3)
-        def _():
-            feed(1)
-            load(2)
-            run(0, 1)
-
-    for_each(4, down)
+    load(0)
+    feed(0)
     column_sums(COT, BIAS_D)
-    fetch(normed2_h, NORMED2).wait()
 
     def activ_back(j):
-        fetch_pair(slope_h, j).wait()
+        fetch_slope(j).wait()
         fetch_w(9 + j, j % 2).wait()
         for h in range(2):
             grad = lax.dot_general(pool[COT], half_rows(j % 2, h), NT, preferred_element_type=WIDE)
@@ -891,24 +897,20 @@
 
         pl.when(j < 2)(lambda: fetch_w(11 + j, j % 2).start())
         pl.when(j >= 2)(lambda: fetch_w(3 + j, j % 2).start())
-        pl.when(j < 2)(lambda: fetch_pair(slope_h, j + 2).start())
-
-        @when(j == 0)
-        def _():
-            feed(2)
-            load(3)
-
-        when(j == 1)(lambda: feed(3))
-        run(1 + j, 2 + j)
+        pl.when(j < 2)(lambda: fetch_slope(j + 2).start())
+        when(j >= 1)(lambda: feed(j))
+        when(j == 0)(lambda: load(1))
+        when(j == 1)(lambda: load(2))
+        when(j == 2)(lambda: load(3))
+        when(j >= 1)(lambda: run(j - 1, j))
 
     for_each(4, activ_back)
-
-    def up(j):
-        column_sums(GRAD_UP + j, BIAS_U + j)
-        produce(4 + j, pool.at[NORMED2], times(GRAD_UP + j))
+    fetch(q_h, QUERY).start()
+    fetch(k_h, KEY).start()
+    fetch(normed2_h, NORMED2).wait()
+
+    def up_back(j):
         fetch_w(5 + j, j % 2).wait()
-        when(j >= 1)(lambda: feed(3 + j))
-        run(5 + j, 6 + j)
         for h in range(2):
             more = lax.dot_general(pool[GRAD_UP + j], half_rows(j % 2, h), NT, preferred_element_type=WIDE)
 
@@ -921,13 +923,18 @@
                 gn[:, half_cols(h)] = gn[:, half_cols(h)] + more
 
         pl.when(j < 2)(lambda: fetch_w(7 + j, j % 2).start())
-        load(4 + j)
-
-    for_each(4, up)
-    fetch_w(4, 0).start()
-    fetch_w(1, 1).start()
-    for src, i in ((ctx_h, CONTEXT), (q_h, QUERY), (k_h, KEY), (v_h, VALUE)):
-        fetch(src, i).start()
+        pl.when(j == 2)(lambda: fetch_w(4, 0).start())
+        pl.when(j == 3)(lambda: fetch_w(1, 1).start())
+        column_sums(GRAD_UP + j, BIAS_U + j)
+        when(j == 2)(lambda: load(4))
+        when(j == 3)(lambda: feed(4))
+        pl.when(j % 2 == 1)(lambda: up(j // 2))
+        when(j % 2 == 0)(lambda: run(3 + j // 2, 4 + j // 2))
+
+    for_each(4, up_back)
+    fetch(v_h, VALUE).start()
+    fetch_share(0).start()
+    fetch_share(1).start()
 
     sums[...] = jnp.zeros_like(sums)
 
@@ -957,25 +964,20 @@
         pool[GRAD_BRANCH, rows, :] = total.astype(LOW)
 
     norm_back(1, GAIN2, lambda rows: mid[rows, :], done2)
-    feed(7)
-    run(9, 10)
-
-    fetch(ctx_h, CONTEXT).wait()
+    load(5)
+    run(5, 7)
+
     column_sums(GRAD_BRANCH, BIAS_O)
-    produce(8, pool.at[CONTEXT], times(GRAD_BRANCH))
     fetch_w(4, 0).wait()
     for h in range(2):
         grad = lax.dot_general(pool[GRAD_BRANCH], half_rows(0, h), NT, preferred_element_type=WIDE)
         pool[GRAD_CONTEXT, :, half_cols(h)] = grad.astype(LOW)
     fetch_w(2, 0).start()
-    load(8)
-    run(10, 11)
-
-    for src, i in ((q_h, QUERY), (k_h, KEY), (v_h, VALUE), (tokens_h, TOKENS)):
+    feed(5)
+    up(2)
+    run(7, 8)
+    for src, i in ((q_h, QUERY), (k_h, KEY), (v_h, VALUE), (ctx_h, CONTEXT), (tokens_h, TOKENS), (normed1_h, NORMED1)):
         fetch(src, i).wait()
-
-    modulated(pool.at[TOKENS], pool.at[NORMED1], table, mods, GAIN1, 0, seqs)
-    feed(8)
 
     lane = lax.broadcasted_iota(jnp.int32, (1, 128), 1)
     first_head = (lane < 64).astype(WIDE)
@@ -989,37 +991,47 @@
 
     def heads(n):
         cols = pl.ds(pl.multiple_of(n * 128, 128), 128)
+        fetch_share(n).wait()
         for s in range(seqs):
             rows = slice(s * per, (s + 1) * per)
             keys = pool[KEY, rows, cols]
             both = split(pool[QUERY, rows, cols])
             grads = split(pool[GRAD_CONTEXT, rows, cols])
-            scores = lax.dot_general(both, keys, NT, preferred_element_type=WIDE)
-            grown = jnp.exp(scores - jnp.max(scores, axis=-1, keepdims=True))
-            probs = grown / jnp.sum(grown, axis=-1, keepdims=True)
+            share = shares[n % 2, 2 * s * per : 2 * (s + 1) * per, :]
+            probs = share.astype(WIDE)
             grad_probs = lax.dot_general(grads, pool[VALUE, rows, cols], NT, preferred_element_type=WIDE)
             inner = jnp.sum(grad_probs * probs, axis=-1, keepdims=True)
             grad_scores = (probs * (grad_probs - inner)).astype(LOW)
-            grad_v = lax.dot_general(probs.astype(LOW), grads, TN, preferred_element_type=WIDE)
+            grad_v = lax.dot_general(share, grads, TN, preferred_element_type=WIDE)
             grad_k = lax.dot_general(grad_scores, both, TN, preferred_element_type=WIDE)
             grad_q = jnp.dot(grad_scores, keys, preferred_element_type=WIDE)
             grad_q = (grad_q[:per] * first_head + grad_q[per:] * second_head) * 0.125
             pool[QUERY, rows, cols] = unturned(grad_q).astype(LOW)
             pool[KEY, rows, cols] = unturned(grad_k).astype(LOW)
             pool[VALUE, rows, cols] = grad_v.astype(LOW)
-        when(n < 7)(lambda: run(11 + n, 12 + n))
+
+        pl.when(n < 6)(lambda: fetch_share(n + 2).start())
+        when(n % 3 == 0)(lambda: load(6 + n // 3))
+        when(jnp.logical_and(n % 3 == 1, n < 7))(lambda: feed(6 + n // 3))
+        when(n == 7)(lambda: feed(8))
+
+        @pl.when(jnp.logical_or(n == 2, n == 5))
+        def _():
+            lhs = jnp.where(n == 2, NORMED2, CONTEXT)
+            rhs = jnp.where(n == 2, GRAD_UP + 3, GRAD_BRANCH)
+            produce(6 + (n + 1) // 3, pool.at[lhs], times(rhs))
+
+        done = 8 + n - (n + 2) // 3
+        when(n % 3 != 0)(lambda: run(done, done + 1))
 
     for_each(8, heads)
 
     def project(j):
         column_sums(QUERY + j, BIAS_P + j)
+        when(j == 2)(lambda: feed(9))
         produce(9 + j, pool.at[NORMED1], times(QUERY + j))
-        when(j == 1)(lambda: load(9))
-
-        @when(j == 2)
-        def _():
-            feed(9)
-            load(10)
+        when(j >= 1)(lambda: load(8 + j))
+        run(13 + j, 14 + j)
 
     for_each(3, project)
 
@@ -1040,7 +1052,7 @@
         pl.when(j == 0)(lambda: fetch_w(3, 1).start())
         when(j < 2)(lambda: feed(10 + j))
         when(j == 0)(lambda: load(11))
-        run(18 + j, 19 + j)
+        when(j < 2)(lambda: run(16 + j, 17 + j))
 
     for_each(3, project_back)
 
@@ -1050,6 +1062,7 @@
     norm_back(0, GAIN1, lambda rows: pool[TOKENS, rows, :], done1)
     input_copy = pltpu.make_async_copy(mid, input_o, sem_mid)
     input_copy.start()
+    run(18, 20)
     if comm:
         for f in range(8):
             for row in range(13):
@@ -1073,7 +1086,7 @@
     load(12)
     feed(12)
     if comm:
-        run(21, 24)
+        run(20, 24)
         middle()
         run(24, 28)
         end()
@@ -1081,28 +1094,28 @@
         red.end()
     else:
         for b in (11, 12):
-            pltpu.make_async_copy(slots.at[b % 2], out.at[b], sem_slot.at[b % 2]).wait()
+            pltpu.make_async_copy(slots.at[b % 2], out.at[b - READY], sem_slot.at[b % 2]).wait()
     input_copy.wait()
 
 
 def backward_call(comm, full, cot, saved, tokens, table, mods, feat, cosine, sine, seqs):
     n, width = tokens.shape
     vmem, hbm = pl.BlockSpec(memory_space=pltpu.VMEM), pl.BlockSpec(memory_space=pl.ANY)
-    q, k, v, ctx, mid, normed2, activ, slope = saved
+    ready, q, k, v, ctx, mid, normed1, normed2, slope, probs = saved
     block = (4, 2, 2, 2, 32, width) if comm else (width, width)
     rows = width // 8
     if comm:
         shapes = [(rows, 3 * width), (rows, width), (rows, 4 * width), (4 * rows, width), (TE // 8, 2 * width), (TE // 8, 2 * width)]
     else:
-        shapes = [(BLOCKS, width, width)]
+        shapes = [(BLOCKS - READY, width, width)]
     outs = [(jax.ShapeDtypeStruct(shape, LOW), hbm) for shape in shapes] + [
         (jax.ShapeDtypeStruct((16, 128) if comm else (16, width), WIDE), vmem),
         (jax.ShapeDtypeStruct((n, width), WIDE), hbm),
     ]
     extra = []
     if comm:
-        part = jax.ShapeDtypeStruct((BLOCKS, 4, 2, 2, 32, width), LOW)
-        outs += [(part, hbm), (part, hbm)]
+        part = lambda count: (jax.ShapeDtypeStruct((count, 4, 2, 2, 32, width), LOW), hbm)
+        outs += [part(BLOCKS - READY), part(BLOCKS)]
         extra = [
             pltpu.VMEM((8, 16, 128), WIDE),
             pltpu.VMEM((7, 16, 128), WIDE),
@@ -1114,20 +1127,22 @@
     got = pl.pallas_call(
         functools.partial(backward_kernel, comm, seqs),
         out_shape=tuple(s for s, _ in outs),
-        in_specs=[hbm] * 11 + [vmem] * 5,
+        in_specs=[hbm] * 13 + [vmem] * 5,
         out_specs=tuple(m for _, m in outs),
         scratch_shapes=[
-            pltpu.VMEM((10, n, width), LOW),
+            pltpu.VMEM((12, n, width), LOW),
             pltpu.VMEM((n, width), WIDE),
             pltpu.VMEM((n, width), WIDE),
             pltpu.VMEM((2,) + block, LOW),
             pltpu.VMEM((2,) + block, LOW),
+            pltpu.VMEM((2,) + probs.shape[1:], LOW),
             pltpu.VMEM((feat.shape[0], width), WIDE),
             pltpu.VMEM((16, width), WIDE),
-            pltpu.SemaphoreType.DMA((10,)),
+            pltpu.SemaphoreType.DMA((12,)),
             pltpu.SemaphoreType.DMA((2,)),
             pltpu.SemaphoreType.DMA((2,)),
             pltpu.SemaphoreType.DMA,
+            pltpu.SemaphoreType.DMA((2,)),
             pltpu.SemaphoreType.DMA((2,)),
         ]
         + extra,
@@ -1135,8 +1150,52 @@
             collective_id=1 if comm else None, has_side_effects=comm, vmem_limit_bytes=62 * 2**20
         ),
         name="backward",
-    )(full, cot, activ, slope, normed2, mid, q, k, v, ctx, tokens, table, mods, feat, cosine, sine)
+    )(full, cot, slope, normed1, normed2, mid, q, k, v, ctx, probs, tokens, ready, table, mods, feat, cosine, sine)
     return got[: len(shapes) + 2]
+
+
+def widen(arrays, vec, sizes):
+    count = len(arrays)
+
+    def kernel(vec_in, *refs):
+        srcs, dsts, lines = refs[:count], refs[count : 2 * count], refs[2 * count : 2 * count + len(sizes)]
+        rest = refs[2 * count + len(sizes) :]
+        lows, wides, sems = rest[:count], rest[count : 2 * count], rest[-1]
+        ins = [pltpu.make_async_copy(s, v, sems.at[i]) for i, (s, v) in enumerate(zip(srcs, lows))]
+        outs = [pltpu.make_async_copy(v, d, sems.at[i]) for i, (v, d) in enumerate(zip(wides, dsts))]
+        for copy in ins:
+            copy.start()
+        row = 0
+        for line, size in zip(lines, sizes):
+            for k in range(size // 128):
+                line[pl.ds(128 * k, 128)] = vec_in[row, :]
+                row += 1
+        for i in range(count):
+            ins[i].wait()
+
+            def body(n, i=i):
+                at = pl.ds(pl.multiple_of(n * 16, 16), 16)
+                wides[i][at, :] = lows[i][at, :].astype(WIDE)
+
+            for_each(lows[i].shape[0] // 16, body)
+            outs[i].start()
+        for copy in outs:
+            copy.wait()
+
+    hbm, vmem = pl.BlockSpec(memory_space=pl.ANY), pl.BlockSpec(memory_space=pltpu.VMEM)
+    got = pl.pallas_call(
+        kernel,
+        out_shape=tuple(jax.ShapeDtypeStruct(a.shape, WIDE) for a in arrays)
+        + tuple(jax.ShapeDtypeStruct((size,), WIDE) for size in sizes),
+        in_specs=[vmem] + [hbm] * count,
+        out_specs=(hbm,) * count + (vmem,) * len(sizes),
+        scratch_shapes=[pltpu.VMEM(a.shape, LOW) for a in arrays]
+        + [pltpu.VMEM(a.shape, WIDE) for a in arrays]
+        + [pltpu.SemaphoreType.DMA((count,))],
+        compiler_params=pltpu.CompilerParams(vmem_limit_bytes=60 * 2**20),
+        name="widen",
+    )(vec, *arrays)
+    return got[:count], got[count:]
 
 
 def rotary_constants(length, head_dim):
@@ -1155,9 +1214,7 @@
     feature = column // 128 * 32 + column % 32
     rates = np.exp((feature % half_width).astype(np.float32) * np.float32(math.log(100.0) / half_width))
     row = np.arange(-(-4 * seqs // 32) * 32)
-    times = jnp.ones(row.shape, WIDE)
-    for s in range(seqs):
-        times = jnp.where(row % seqs == s, noise_times[s], times)
+    times = jnp.sum(jnp.where(row[:, None] % seqs == np.arange(seqs)[None, :], noise_times[None, :], 0.0), axis=1)
     phases = (jnp.log(times) * 0.25)[:, None] * rates[None, :]
     feat = jnp.where((feature < half_width)[None, :], jnp.sin(phases), jnp.cos(phases))
     return jnp.where((column // 32 % 4)[None, :] == (row // seqs)[:, None], feat, 0.0).astype(LOW)
@@ -1255,12 +1312,17 @@
     else:
         full, table = gather_plain(weights, vectors)
         weights = (full,)
-    full, table, mods, layer_out, *saved = forward_call(comm, weights, table, inputs, feat, cosine, sine, seqs)
+    full, table, mods, layer_out, *saved = forward_call(
+        comm, weights, table, inputs, cotangent, feat, cosine, sine, seqs
+    )
     *sums, input_grad = backward_call(comm, full, cotangent, saved, inputs, table, mods, feat, cosine, sine, seqs)
     if not comm:
-        sums = reduce_plain(*sums, sizes, shards_of)
-    project, output, up, down, time1, time2 = [s.astype(WIDE) for s in sums[:6]]
-    got = pieces_of(sums[6].reshape(-1), sizes)
+        sums = reduce_plain(jnp.concatenate([saved[0], sums[0]]), sums[1], sizes, shards_of)
+    if comm:
+        wide, got = widen(sums[:6], sums[6], sizes)
+    else:
+        wide, got = [s.astype(WIDE) for s in sums[:6]], pieces_of(sums[6], sizes)
+    project, output, up, down, time1, time2 = wide
     return (
         layer_out,
         input_grad,

time: 363 us -> 312 us (0.86)
  Pallas kernels: 333 us -> 302 us
  other arithmetic: 18.5 us -> 4.12 us
  local copies, waits for them, and re-layouts: 9.96 us -> 4.11 us
    pallas_call x1, Pallas kernels: 191 us -> 152 us  [backward_call(): pl.pallas_call(functools.partial(backward_kernel, comm, seqs), out_shape=...]
    convert_element_type x6 -> x0, other arithmetic: 10.6 us -> none  [shards(): project, output, up, down, time1, time2 = [s.astype(WIDE) for s in sums[:6]]]
    pallas_call x0 -> x1, Pallas kernels: none -> 5.54 us  [widen(): pl.pallas_call(kernel, out_shape=tuple((jax.ShapeDtypeStruct(a.shape, WID...]
    slice x4 -> x0, local copies, waits for them, and re-layouts: 5.47 us -> none  [the longest x3 3.99 us: pieces_of(): got.append(flat[..., at:at + size])]
    mul x1, other arithmetic: 4.63 us -> 0.01 us  [wide_features(): phases = (jnp.log(times) * 0.25)[:, None] * rates[None, :]]
where the time goes in v4:
time: 312 us; the launch traced here: 311 us
  Pallas kernels  302 us (97%)
  other arithmetic  4.12 us (1%)
  local copies, waits for them, and re-layouts  4.11 us (1%)
    pallas_call x1, Pallas kernels, backward_call(): pl.pallas_call(functools.partial(backward_kernel, comm, seqs), out_shape=...  152 us
    pallas_call x1, Pallas kernels, forward_call(): pl.pallas_call(functools.partial(forward_kernel, comm, seqs), out_shape=t...  145 us

profile of v4, /device:TPU:0, one launch (start us, length us, event | category | flops | bytes accessed | tf_op | source)
XLA Modules:
  0.0 311.0 jit_solution(1332173550484806696)
XLA Ops:
  0.6 0.8 select_reduce_fusion
  1.4 1.4 convert_add_fusion.refs_6_
  2.8 2.0 fusion.2.refs_9_.refs_15_
  4.8 144.7 %forward.1 = (bf16[13,4,2,2,2,32,1024]{6,5,4,3,2,1,0:T(8,128)(2,1)}, f32[16,1024]{1,0:T(8,128)}, f32[32,1024]{1,0:T(8,128)}, bf16[768,1024]{1,0:T(8,128)(2,1)}, ...) custom-call(bf16[128,3072]{1,0:T(8,128)(2,1)} %refs_0_.1, ...), custom_call_target="tpu_custom_call" | custom-call | tf_op jit(solution)/shard_map/forward/pallas_call | solution.py:519
  149.5 151.8 %backward.1 = (bf16[128,3072]{1,0:T(8,128)(2,1)}, bf16[128,1024]{1,0:T(8,128)(2,1)}, bf16[128,4096]{1,0:T(8,128)(2,1)}, bf16[512,1024]{1,0:T(8,128)(2,1)}, bf16[...) custom-call(bf16[13,4,2,2,2,32,1024]{6,5,4,3,2,1,0:T(8,128)(2,1)} %g, ...), custom_call_target="tpu_custom_call" | custom-call | tf_op jit(solution)/shard_map/backward/pallas_call | solution.py:1127
  301.3 0.0 copy-start.1
  301.3 5.5 %widen.1 = (f32[128,3072]{1,0:T(8,128)}, f32[128,1024]{1,0:T(8,128)}, f32[128,4096]{1,0:T(8,128)}, f32[512,1024]{1,0:T(8,128)}, f32[32,2048]{1,0:T(8,128)}, /*in...) custom-call(f32[16,128]{1,0:T(8,128)} %get-tuple-element.67.vec_in, ...), custom_call_target="tpu_custom_call" | custom-call | tf_op jit(solution)/shard_map/widen/pallas_call | solution.py:1186
  306.9 0.0 copy-start
  306.9 0.0 copy-done.1
  306.9 1.1 copy.42
  308.1 1.3 copy-done
  309.3 1.7 copy.43
  (1 shorter events, 0.0 us)
Async XLA Ops:
  301.3 5.6 %copy-start.1 = (bf16[768,1024]{1,0:T(8,128)(2,1)S(1)}, bf16[768,1024]{1,0:T(8,128)(2,1)}, u32[]{:S(2)}) copy-start(bf16[768,1024]{1,0:T(8,128)(2,1)} %get-tuple-element.104) | copy-start | bytes 4718596
  306.9 2.5 copy-start
